TPU v7x, 32 devices: a whole 2x2x4 slice. The times are simulated.
32 devices in a mesh: gx: 8 (over z, y), gy: 4 (over x, core).
Axes of the slice: x: 2, y: 2, z: 4, core: 2. Of those that a mesh axis runs over, the one named last changes fastest.
Arguments:
- initial_state: float32 [32, 2, 256, 1024], P(None, None, 'gy', 'gx'), may hold values from -34 to 34
- velocity: float32 [3, 2, 256, 1024], P(None, None, 'gy', 'gx'), may hold values from -0.3 to 0.3
- diffusivity: float32 [32], replicated, may hold values from 0.02 to 0.15
- reaction_rate: float32 [32], replicated, may hold values from 0.05 to 0.5
- start_basis: bfloat16 [1024, 128], replicated, may hold values from -0.1875 to 0.1875
Outputs:
- evolved: float32 [32, 2, 256, 1024], P(None, None, 'gy', 'gx')
- factor: bfloat16 [1024, 128], P(('gx', 'gy'))
- subspace_core: float32 [32, 2, 256, 128], P('gx', None, 'gy')
All inputs are finite; a program needn't handle non-finite values.
Results may differ from a plain program's by a relative error of at most 0.012.
Values may be sent and summed in bfloat16 or wider, within the bound.
No kernel may reach another device: no remote copies, remote signals or barrier semaphores. Data moves between devices by JAX's collectives and lax.ppermute only.
A program may use at most 64 MiB of HBM per device.

v0:
```python
import functools
import math

import jax
import jax.numpy as jnp
from jax import lax
from jax.experimental import pallas as pl
from jax.experimental.pallas import tpu as pltpu
from jax.sharding import PartitionSpec as P

SECTIONS = 4
NS_STEPS = 5
HIGHEST = lax.Precision.HIGHEST
VMEM_BYTES = 48 * 1024 * 1024
BOTH = ("gx", "gy")


def with_halo(x, sides, width):
    for axis, dim in sides:
        count, length = (lax.axis_size(axis), x.shape[dim])
        up = [(i, (i + 1) % count) for i in range(count)]
        down = [(j, i) for i, j in up]
        last = lax.slice_in_dim(x, length - width, length, axis=dim)
        initial = lax.slice_in_dim(x, 0, width, axis=dim)
        before = lax.ppermute(last, axis, up)
        after = lax.ppermute(initial, axis, down)
        x = jnp.concatenate([before, x, after], axis=dim)
    return x


def advance(padded, velocity, diffusivity, reaction_rate):
    centre = padded[:, :, 1:-1, 1:-1]
    east_side = padded[:, :, 1:-1, 2:]
    west_side = padded[:, :, 1:-1, :-2]
    north_side = padded[:, :, 2:, 1:-1]
    south_side = padded[:, :, :-2, 1:-1]
    walled = jnp.pad(centre, ((0, 0), (1, 1), (0, 0), (0, 0)))
    upper_side = walled[:, 2:]
    lower_side = walled[:, :-2]
    laplacian = (
        east_side + west_side + north_side + south_side + upper_side + lower_side - 6.0 * centre
    )
    transport = (
        velocity[0] * (east_side - west_side)
        + velocity[1] * (north_side - south_side)
        + velocity[2] * (upper_side - lower_side)
    )
    decay = reaction_rate[:, None, None, None] * centre * centre * centre / (1.0 + centre * centre)
    return centre + diffusivity[:, None, None, None] * laplacian - 0.5 * transport - decay


def image_kernel(columns_ref, basis_ref, image_ref):
    pieces, rows, width = columns_ref.shape
    project = jnp.zeros((rows, basis_ref.shape[1]), jnp.float32)
    for piece in range(pieces):
        project += jnp.dot(
            columns_ref[piece],
            basis_ref[pl.ds(piece * width, width), :],
            preferred_element_type=jnp.float32,
        )
    project = project.astype(jnp.bfloat16)
    for piece in range(pieces):
        image_ref[pl.ds(piece * width, width), :] = lax.dot_general(
            columns_ref[piece],
            project,
            (((0,), (0,)), ((), ())),
            preferred_element_type=jnp.float32,
        ).astype(image_ref.dtype)


def factor_kernel(owner_ref, image_ref, columns_ref, own_ref, core_ref, factor_ref):
    pieces, rows, width = columns_ref.shape
    rows_all, rank = image_ref.shape
    rows_each = own_ref.shape[0]
    image = image_ref[...]
    row = lax.broadcasted_iota(jnp.int32, (rank, rank), 0)
    column = lax.broadcasted_iota(jnp.int32, (rank, rank), 1)
    identity = (row == column).astype(jnp.float32)
    gram = lax.dot_general(
        image,
        image,
        (((0,), (0,)), ((), ())),
        precision=HIGHEST,
        preferred_element_type=jnp.float32,
    )
    trace = jnp.sum(gram * identity)
    gram = gram / (trace + 1e-06)
    product = None
    for step in range(NS_STEPS):
        update = 1.5 * identity - 0.5 * gram
        if step < NS_STEPS - 1:
            gram = jnp.dot(gram, update, precision=HIGHEST, preferred_element_type=jnp.float32)
            gram = jnp.dot(update, gram, precision=HIGHEST, preferred_element_type=jnp.float32)
        if product is None:
            product = update
        else:
            product = jnp.dot(
                product, update, precision=HIGHEST, preferred_element_type=jnp.float32
            )
    scaling = jnp.sqrt(rows_all / (trace + 1e-06))
    factor = jnp.dot(
        image * scaling, product, precision=HIGHEST, preferred_element_type=jnp.float32
    )
    factor_ref[...] = factor.astype(jnp.bfloat16)
    start = pl.multiple_of(owner_ref[0] * rows_each, rows_each)
    own_ref[...] = factor_ref[pl.ds(start, rows_each), :]
    core = jnp.zeros((rows, rank), jnp.float32)
    for piece in range(pieces):
        core += jnp.dot(
            columns_ref[piece],
            factor_ref[pl.ds(piece * width, width), :],
            preferred_element_type=jnp.float32,
        )
    core_ref[...] = core / math.sqrt(rows_all)


def vmem(count):
    return [pl.BlockSpec(memory_space=pltpu.VMEM)] * count


def subspace(columns, start_basis):
    pieces, rows, width = columns.shape
    rows_all, rank = start_basis.shape
    owners = lax.axis_size(BOTH)
    rows_each = rows_all // owners
    params = pltpu.CompilerParams(vmem_limit_bytes=VMEM_BYTES)
    partial = pl.pallas_call(
        image_kernel,
        out_shape=jax.ShapeDtypeStruct((rows_all, rank), jnp.float32),
        in_specs=vmem(2),
        out_specs=vmem(1)[0],
        compiler_params=params,
    )(columns, start_basis)
    shares = lax.all_to_all(
        partial.reshape(owners, rows_each, rank), BOTH, split_axis=0, concat_axis=0, tiled=True
    )
    own_image = jnp.sum(shares, axis=0)
    image = lax.all_to_all(
        jnp.broadcast_to(own_image[None], (owners, rows_each, rank)),
        BOTH,
        split_axis=0,
        concat_axis=0,
        tiled=True,
    ).reshape(rows_all, rank)
    owner = lax.axis_index(BOTH).astype(jnp.int32).reshape(1)
    return pl.pallas_call(
        factor_kernel,
        out_shape=(
            jax.ShapeDtypeStruct((rows_each, rank), jnp.bfloat16),
            jax.ShapeDtypeStruct((rows, rank), jnp.float32),
        ),
        in_specs=[pl.BlockSpec(memory_space=pltpu.SMEM)] + vmem(2),
        out_specs=tuple(vmem(2)),
        scratch_shapes=[pltpu.VMEM((rows_all, rank), jnp.bfloat16)],
        compiler_params=params,
    )(owner, image, columns)


def shards(initial_state, velocity, diffusivity, reaction_rate, start_basis):
    field_now = initial_state
    for section_index in range(SECTIONS):
        padded = with_halo(field_now, (("gx", 3), ("gy", 2)), 1)
        field_now = advance(padded, velocity, diffusivity, reaction_rate)
    species, heights, length, width = field_now.shape
    pieces = lax.axis_size("gx")
    each = species // pieces
    columns = lax.all_to_all(
        field_now.astype(jnp.bfloat16), "gx", split_axis=0, concat_axis=0, tiled=True
    ).reshape(pieces, each * heights * length, width)
    own_rows, core = subspace(columns, start_basis)
    return (field_now, own_rows, core.reshape(each, heights, length, start_basis.shape[1]))


def solution(mesh):
    in_specs = (P(None, None, "gy", "gx"), P(None, None, "gy", "gx"), P(), P(), P())
    out_specs = (P(None, None, "gy", "gx"), P(("gx", "gy"), None), P("gx", None, "gy", None))
    return jax.shard_map(shards, mesh=mesh, in_specs=in_specs, out_specs=out_specs, check_vma=False)
```

profile of v0, /device:TPU:0, one launch (start us, length us, event | category | flops | bytes accessed | tf_op | source)
XLA Modules:
  0.0 194.8 jit_solution(12711015228079124257)
XLA Ops:
  0.6 4.4 %fusion.13 = (f32[32,2,64,1]{3,2,1,0:T(8,128)S(1)}, f32[32,2,64,1]{3,2,1,0:T(8,128)}) fusion(f32[32,2,64,128]{3,2,1,0:T(8,128)} %param.5), kind=kLoop, calls=%fused_computation.71 | loop fusion | bytes 65536 | tf_op jit(solution)/shard_map/slice | solution.py:23
  7.3 6.0 %collective-permute-start = (f32[32,2,64,1]{2,0,3,1:T(8,128)S(1)}, f32[32,2,64,1]{2,0,3,1:T(8,128)S(1)}, u32[]{:S(2)}, u32[]{:S(2)}) collective-permute-start(f32[32,2,64,1]{2,0,3,1:T(8,128)S(1)} %copy.63), channel_id=1, source_target_pairs={{4,0},{8,4},{12,8},{16,12},{20,16},{24,20},{28,24},{0,28},{5,1},{9... | collective-permute-start | bytes 49160 | tf_op jit(solution)/shard_map/ppermute | solution.py:26
  14.0 2.8 %copy.37 = f32[32,2,64,128]{3,0,2,1:T(8,128)S(1)} copy(f32[32,2,64,128]{3,2,1,0:T(8,128)} %param.5) | data formatting | bytes 4194304 | tf_op args[0]
  16.9 2.9 %copy.28 = f32[32,2,64,1]{3,0,2,1:T(8,128)} copy(f32[32,2,64,1]{2,0,3,1:T(8,128)S(1)} %collective-permute-done) | data formatting | bytes 32768 | tf_op jit(solution)/shard_map/ppermute | solution.py:26
  20.6 2.9 %copy.30 = f32[32,2,64,1]{3,0,2,1:T(8,128)} copy(f32[32,2,64,1]{2,0,3,1:T(8,128)S(1)} %collective-permute-done.1) | data formatting | bytes 32768 | tf_op jit(solution)/shard_map/ppermute | solution.py:25
  26.6 2.5 %collective-permute-done.3 = f32[32,2,1,130]{3,0,2,1:T(8,128)S(1)} collective-permute-done((f32[32,2,1,130]{3,0,2,1:T(8,128)S(1)}, f32[32,2,1,130]{3,0,2,1:T(8,128)S(1)}, u32[]{:S(2)}, u32[]{:S(2)}) %collective-permute-start.3) | collective-permute-done | bytes 33312 | tf_op jit(solution)/shard_map/ppermute | solution.py:25
  29.2 7.2 %fusion.1 = f32[32,2,64,128]{3,0,2,1:T(8,128)S(1)} fusion(f32[32,2,64,128]{3,0,2,1:T(8,128)} %copy-done.4, f32[32,2,64,1]{3,0,2,1:T(8,128)S(1)} %copy-done.5, f32[32,2,64,1]{3,0,2,1:T(8,128)S(1)} %copy-done.7, f32[32,2,1,130]{3,0,2,1:T(8,128)S(1)} %collective-permute-done.3, f32[32,2,1,130]{3,0,2,1:T(8,128)S(1)} %collective-permute-done.2, ...), kind=kLoop, calls=%fused_computation.13 | loop fusion | flops 17825792 | bytes 4490496 | tf_op jit(solution)/shard_map/sub | solution.py:49
  36.3 2.8 %fusion.12 = (f32[32,2,64,1]{3,0,2,1:T(8,128)}, f32[32,2,64,1]{3,0,2,1:T(8,128)}) fusion(f32[32,2,64,128]{3,0,2,1:T(8,128)S(1)} %fusion.1), kind=kLoop, calls=%fused_computation.70 | loop fusion | bytes 65536 | tf_op jit(solution)/shard_map/slice | solution.py:23
  39.1 2.6 %copy.43 = f32[32,2,64,1]{2,0,3,1:T(8,128)S(1)} copy(f32[32,2,64,1]{3,0,2,1:T(8,128)} %get-tuple-element.28) | data formatting | bytes 32768 | tf_op jit(solution)/shard_map/slice | solution.py:24
  41.8 3.9 %collective-permute-start.4 = (f32[32,2,64,1]{2,0,3,1:T(8,128)S(1)}, f32[32,2,64,1]{2,0,3,1:T(8,128)S(1)}, u32[]{:S(2)}, u32[]{:S(2)}) collective-permute-start(f32[32,2,64,1]{2,0,3,1:T(8,128)S(1)} %copy.43), channel_id=1, source_target_pairs={{4,0},{8,4},{12,8},{16,12},{20,16},{24,20},{28,24},{0,28},{5,1},{9... | collective-permute-start | bytes 49160 | tf_op jit(solution)/shard_map/ppermute | solution.py:26
  45.7 2.6 %copy.45 = f32[32,2,64,1]{2,0,3,1:T(8,128)S(1)} copy(f32[32,2,64,1]{3,0,2,1:T(8,128)} %get-tuple-element.27) | data formatting | bytes 32768 | tf_op jit(solution)/shard_map/slice | solution.py:23
  48.5 2.9 %copy.44 = f32[32,2,64,1]{3,0,2,1:T(8,128)} copy(f32[32,2,64,1]{2,0,3,1:T(8,128)S(1)} %collective-permute-done.4) | data formatting | bytes 32768 | tf_op jit(solution)/shard_map/ppermute | solution.py:26
  51.4 3.7 %collective-permute-done.5 = f32[32,2,64,1]{2,0,3,1:T(8,128)S(1)} collective-permute-done((f32[32,2,64,1]{2,0,3,1:T(8,128)S(1)}, f32[32,2,64,1]{2,0,3,1:T(8,128)S(1)}, u32[]{:S(2)}, u32[]{:S(2)}) %collective-permute-start.5) | collective-permute-done | bytes 16416 | tf_op jit(solution)/shard_map/ppermute | solution.py:25
  55.1 2.9 %copy.46 = f32[32,2,64,1]{3,0,2,1:T(8,128)} copy(f32[32,2,64,1]{2,0,3,1:T(8,128)S(1)} %collective-permute-done.5) | data formatting | bytes 32768 | tf_op jit(solution)/shard_map/ppermute | solution.py:25
  63.0 3.9 %fusion.3 = f32[32,2,64,128]{3,0,2,1:T(8,128)S(1)} fusion(f32[32,2,64,128]{3,0,2,1:T(8,128)S(1)} %fusion.1, f32[32,2,64,1]{3,0,2,1:T(8,128)S(1)} %copy-done.8, f32[32,2,64,1]{3,0,2,1:T(8,128)S(1)} %copy-done.11, f32[32,2,1,130]{3,0,2,1:T(8,128)S(1)} %collective-permute-done.7, f32[32,2,1,130]{3,0,2,1:T(8,128)S(1)} %collective-permute-done.6, ...), kind=kLoop, calls=%fused_computation.15 | loop fusion | flops 17825792 | bytes 4490496 | tf_op jit(solution)/shard_map/sub | solution.py:49
  69.1 2.6 %copy.49 = f32[32,2,64,1]{2,0,3,1:T(8,128)S(1)} copy(f32[32,2,64,1]{3,0,2,1:T(8,128)} %get-tuple-element.26) | data formatting | bytes 32768 | tf_op jit(solution)/shard_map/slice | solution.py:24
  75.6 2.9 %copy.50 = f32[32,2,64,1]{3,0,2,1:T(8,128)} copy(f32[32,2,64,1]{2,0,3,1:T(8,128)S(1)} %collective-permute-done.8) | data formatting | bytes 32768 | tf_op jit(solution)/shard_map/ppermute | solution.py:26
  80.5 2.9 %copy.52 = f32[32,2,64,1]{3,0,2,1:T(8,128)} copy(f32[32,2,64,1]{2,0,3,1:T(8,128)S(1)} %collective-permute-done.9) | data formatting | bytes 32768 | tf_op jit(solution)/shard_map/ppermute | solution.py:25
  88.6 3.9 %fusion.5 = f32[32,2,64,128]{3,0,2,1:T(8,128)S(1)} fusion(f32[32,2,64,128]{3,0,2,1:T(8,128)S(1)} %copy-done.3, f32[32,2,64,1]{3,0,2,1:T(8,128)S(1)} %copy-done.9, f32[32,2,64,1]{3,0,2,1:T(8,128)S(1)} %copy-done.12, f32[32,2,1,130]{3,0,2,1:T(8,128)S(1)} %collective-permute-done.11, f32[32,2,1,130]{3,0,2,1:T(8,128)S(1)} %collective-permute-done.10, ...), kind=kLoop, calls=%fused_computation.17 | loop fusion | flops 17825792 | bytes 4490496 | tf_op jit(solution)/shard_map/sub | solution.py:49
  92.6 2.8 %fusion.10 = (f32[32,2,64,1]{3,0,2,1:T(8,128)}, f32[32,2,64,1]{3,0,2,1:T(8,128)}) fusion(f32[32,2,64,128]{3,0,2,1:T(8,128)S(1)} %fusion.5), kind=kLoop, calls=%fused_computation.68 | loop fusion | bytes 65536 | tf_op jit(solution)/shard_map/slice | solution.py:23
  95.4 2.6 %copy.55 = f32[32,2,64,1]{2,0,3,1:T(8,128)S(1)} copy(f32[32,2,64,1]{3,0,2,1:T(8,128)} %get-tuple-element.24) | data formatting | bytes 32768 | tf_op jit(solution)/shard_map/slice | solution.py:24
  99.8 2.6 %copy.57 = f32[32,2,64,1]{2,0,3,1:T(8,128)S(1)} copy(f32[32,2,64,1]{3,0,2,1:T(8,128)} %get-tuple-element.23) | data formatting | bytes 32768 | tf_op jit(solution)/shard_map/slice | solution.py:23
  102.7 2.9 %copy.56 = f32[32,2,64,1]{3,0,2,1:T(8,128)} copy(f32[32,2,64,1]{2,0,3,1:T(8,128)S(1)} %collective-permute-done.12) | data formatting | bytes 32768 | tf_op jit(solution)/shard_map/ppermute | solution.py:26
  105.6 3.5 %collective-permute-done.13 = f32[32,2,64,1]{2,0,3,1:T(8,128)S(1)} collective-permute-done((f32[32,2,64,1]{2,0,3,1:T(8,128)S(1)}, f32[32,2,64,1]{2,0,3,1:T(8,128)S(1)}, u32[]{:S(2)}, u32[]{:S(2)}) %collective-permute-start.13) | collective-permute-done | bytes 16416 | tf_op jit(solution)/shard_map/ppermute | solution.py:25
  109.0 2.9 %copy.58 = f32[32,2,64,1]{3,0,2,1:T(8,128)} copy(f32[32,2,64,1]{2,0,3,1:T(8,128)S(1)} %collective-permute-done.13) | data formatting | bytes 32768 | tf_op jit(solution)/shard_map/ppermute | solution.py:25
  117.1 4.8 %fusion.8 = (bf16[32,2,64,128]{3,0,2,1:T(8,128)(2,1)S(1)}, f32[32,2,64,128]{3,0,2,1:T(8,128)}) fusion(f32[32,2,64,128]{3,0,2,1:T(8,128)S(1)} %fusion.5, f32[32]{0:T(128)S(1)} %copy-done.14, f32[2,64,128]{2,1,0:T(8,128)S(1)} %get-tuple-element.32, f32[2,64,128]{2,1,0:T(8,128)S(1)} %get-tuple-element.33, f32[2,64,128]{2,1,0:T(8,128)S(1)} %get-tuple-element.31, ...), kind=kLoop, calls=%fused_computation.67 | loop fusion | flops 18350080 | bytes 5539072 | tf_op jit(solution)/shard_map/convert_element_type | solution.py:168
  122.3 28.3 %all_to_all.15 = bf16[32,2,64,128]{3,2,1,0:T(8,128)(2,1)S(1)} all-to-all(bf16[32,2,64,128]{3,2,1,0:T(8,128)(2,1)S(1)} %copy.61), channel_id=1, replica_groups=mesh['gx'=8,'gy'=4] {'gx'}, dimensions={0} | all-to-all | bytes 2097152 | tf_op jit(solution)/shard_map/all_to_all | solution.py:167
  151.9 18.5 %all_to_all.16 = f32[32,32,128]{2,1,0:T(8,128)S(1)} all-to-all(f32[32,32,128]{2,1,0:T(8,128)S(1)} %bitcast.13), channel_id=1, replica_groups=mesh['gx'=8,'gy'=4] {'gx','gy'}, dimensions={0} | all-to-all | bytes 1048576 | tf_op jit(solution)/shard_map/all_to_all | solution.py:134
  171.3 3.3 %all-to-all-start.2 = ((f32[32,32,128]{2,1,0:T(8,128)}), f32[32,32,128]{2,1,0:T(8,128)S(1)}, u32[]{:S(2)}, u32[]{:S(2)}) async-start(f32[32,32,128]{2,1,0:T(8,128)} %broadcast_in_dim.2), calls=%async_computation.2 | async-start | bytes 1048576 | tf_op jit(solution)/shard_map/all_to_all | solution.py:138
  174.6 4.1 %copy.62 = f32[32,2,64,128]{3,2,1,0:T(8,128)} copy(f32[32,2,64,128]{3,0,2,1:T(8,128)} %get-tuple-element.14) | data formatting | bytes 4194304
  178.8 11.2 %all-to-all-done.2 = f32[32,32,128]{2,1,0:T(8,128)S(1)} async-done(((f32[32,32,128]{2,1,0:T(8,128)}), f32[32,32,128]{2,1,0:T(8,128)S(1)}, u32[]{:S(2)}, u32[]{:S(2)}) %all-to-all-start.2) | async-done | bytes 524320 | tf_op jit(solution)/shard_map/all_to_all | solution.py:138
  189.9 4.8 %shard_map.77 = (bf16[32,128]{1,0:T(8,128)(2,1)}, f32[512,128]{1,0:T(8,128)}) custom-call(s32[1]{0:T(128)} %bitcast.3.owner_ref, f32[1024,128]{1,0:T(8,128)S(1)} %bitcast.14, bf16[8,512,128]{2,1,0:T(8,128)(2,1)S(1)} %bitcast.12), custom_call_target="tpu_custom_call" | custom-call | tf_op jit(solution)/shard_map/pallas_call | solution.py:146
  (72 shorter events, 35.0 us)
Async XLA Ops:
  7.3 9.6 %collective-permute-start = (f32[32,2,64,1]{2,0,3,1:T(8,128)S(1)}, f32[32,2,64,1]{2,0,3,1:T(8,128)S(1)}, u32[]{:S(2)}, u32[]{:S(2)}) collective-permute-start(f32[32,2,64,1]{2,0,3,1:T(8,128)S(1)} %copy.63), channel_id=1, source_target_pairs={{4,0},{8,4},{12,8},{16,12},{20,16},{24,20},{28,24},{0,28},{5,1},{9... | collective-permute-start | bytes 49160 | tf_op jit(solution)/shard_map/ppermute | solution.py:26
  14.0 6.6 %collective-permute-start.1 = (f32[32,2,64,1]{2,0,3,1:T(8,128)S(1)}, f32[32,2,64,1]{2,0,3,1:T(8,128)S(1)}, u32[]{:S(2)}, u32[]{:S(2)}) collective-permute-start(f32[32,2,64,1]{2,0,3,1:T(8,128)S(1)} %copy.64), channel_id=1, source_target_pairs={{0,4},{4,8},{8,12},{12,16},{16,20},{20,24},{24,28},{28,0},{1,5},{5... | collective-permute-start | bytes 49160 | tf_op jit(solution)/shard_map/ppermute | solution.py:25
  16.9 6.7 %copy-start.4 = (f32[32,2,64,128]{3,0,2,1:T(8,128)}, f32[32,2,64,128]{3,0,2,1:T(8,128)S(1)}, u32[]{:S(2)}) copy-start(f32[32,2,64,128]{3,0,2,1:T(8,128)S(1)} %copy.37) | copy-start | bytes 6291460
  23.5 5.6 %copy-start.5 = (f32[32,2,64,1]{3,0,2,1:T(8,128)S(1)}, f32[32,2,64,1]{3,0,2,1:T(8,128)}, u32[]{:S(2)}) copy-start(f32[32,2,64,1]{3,0,2,1:T(8,128)} %copy.28) | copy-start | bytes 49156
  23.6 5.6 %copy-start.7 = (f32[32,2,64,1]{3,0,2,1:T(8,128)S(1)}, f32[32,2,64,1]{3,0,2,1:T(8,128)}, u32[]{:S(2)}) copy-start(f32[32,2,64,1]{3,0,2,1:T(8,128)} %copy.30) | copy-start | bytes 49156
  23.6 5.6 %copy-start.14 = (f32[32]{0:T(128)S(1)}, f32[32]{0:T(128)}, u32[]{:S(2)}) copy-start(f32[32]{0:T(128)} %param.8) | copy-start | bytes 388
  23.6 5.6 %copy-start.15 = (f32[32]{0:T(128)S(1)}, f32[32]{0:T(128)}, u32[]{:S(2)}) copy-start(f32[32]{0:T(128)} %param.7) | copy-start | bytes 388
  24.7 2.0 %collective-permute-start.2 = (f32[32,2,1,130]{3,0,2,1:T(8,128)S(1)}, f32[32,2,1,130]{3,0,2,1:T(8,128)S(1)}, u32[]{:S(2)}, u32[]{:S(2)}) collective-permute-start(f32[32,2,1,130]{3,0,2,1:T(8,128)S(1)} %get-tuple-element.21), channel_id=1, source_target_pairs={{1,0},{2,1},{3,2},{0,3},{5,4},{6,5},{7,6},{4,7},{9,8},{10,9},{11,1... | collective-permute-start | bytes 99848 | tf_op jit(solution)/shard_map/ppermute | solution.py:26
  24.7 4.4 %collective-permute-start.3 = (f32[32,2,1,130]{3,0,2,1:T(8,128)S(1)}, f32[32,2,1,130]{3,0,2,1:T(8,128)S(1)}, u32[]{:S(2)}, u32[]{:S(2)}) collective-permute-start(f32[32,2,1,130]{3,0,2,1:T(8,128)S(1)} %get-tuple-element.22), channel_id=1, source_target_pairs={{0,1},{1,2},{2,3},{3,0},{4,5},{5,6},{6,7},{7,4},{8,9},{9,10},{10,1... | collective-permute-start | bytes 99848 | tf_op jit(solution)/shard_map/ppermute | solution.py:25
  41.8 6.7 %collective-permute-start.4 = (f32[32,2,64,1]{2,0,3,1:T(8,128)S(1)}, f32[32,2,64,1]{2,0,3,1:T(8,128)S(1)}, u32[]{:S(2)}, u32[]{:S(2)}) collective-permute-start(f32[32,2,64,1]{2,0,3,1:T(8,128)S(1)} %copy.43), channel_id=1, source_target_pairs={{4,0},{8,4},{12,8},{16,12},{20,16},{24,20},{28,24},{0,28},{5,1},{9... | collective-permute-start | bytes 49160 | tf_op jit(solution)/shard_map/ppermute | solution.py:26
  48.3 6.8 %collective-permute-start.5 = (f32[32,2,64,1]{2,0,3,1:T(8,128)S(1)}, f32[32,2,64,1]{2,0,3,1:T(8,128)S(1)}, u32[]{:S(2)}, u32[]{:S(2)}) collective-permute-start(f32[32,2,64,1]{2,0,3,1:T(8,128)S(1)} %copy.45), channel_id=1, source_target_pairs={{0,4},{4,8},{8,12},{12,16},{16,20},{20,24},{24,28},{28,0},{1,5},{5... | collective-permute-start | bytes 49160 | tf_op jit(solution)/shard_map/ppermute | solution.py:25
  58.0 5.0 %copy-start.8 = (f32[32,2,64,1]{3,0,2,1:T(8,128)S(1)}, f32[32,2,64,1]{3,0,2,1:T(8,128)}, u32[]{:S(2)}) copy-start(f32[32,2,64,1]{3,0,2,1:T(8,128)} %copy.44) | copy-start | bytes 49156
  58.0 5.0 %copy-start.11 = (f32[32,2,64,1]{3,0,2,1:T(8,128)S(1)}, f32[32,2,64,1]{3,0,2,1:T(8,128)}, u32[]{:S(2)}) copy-start(f32[32,2,64,1]{3,0,2,1:T(8,128)} %copy.46) | copy-start | bytes 49156
  59.1 2.2 %collective-permute-start.6 = (f32[32,2,1,130]{3,0,2,1:T(8,128)S(1)}, f32[32,2,1,130]{3,0,2,1:T(8,128)S(1)}, u32[]{:S(2)}, u32[]{:S(2)}) collective-permute-start(f32[32,2,1,130]{3,0,2,1:T(8,128)S(1)} %get-tuple-element.19), channel_id=1, source_target_pairs={{1,0},{2,1},{3,2},{0,3},{5,4},{6,5},{7,6},{4,7},{9,8},{10,9},{11,1... | collective-permute-start | bytes 99848 | tf_op jit(solution)/shard_map/ppermute | solution.py:26
  59.2 3.8 %collective-permute-start.7 = (f32[32,2,1,130]{3,0,2,1:T(8,128)S(1)}, f32[32,2,1,130]{3,0,2,1:T(8,128)S(1)}, u32[]{:S(2)}, u32[]{:S(2)}) collective-permute-start(f32[32,2,1,130]{3,0,2,1:T(8,128)S(1)} %get-tuple-element.20), channel_id=1, source_target_pairs={{0,1},{1,2},{2,3},{3,0},{4,5},{5,6},{6,7},{7,4},{8,9},{9,10},{10,1... | collective-permute-start | bytes 99848 | tf_op jit(solution)/shard_map/ppermute | solution.py:25
  66.9 2.2 %copy-start.1 = (f32[32,2,64,128]{3,0,2,1:T(8,128)}, f32[32,2,64,128]{3,0,2,1:T(8,128)S(1)}, u32[]{:S(2)}) copy-start(f32[32,2,64,128]{3,0,2,1:T(8,128)S(1)} %fusion.3) | copy-start | bytes 6291460
  71.7 3.9 %collective-permute-start.8 = (f32[32,2,64,1]{2,0,3,1:T(8,128)S(1)}, f32[32,2,64,1]{2,0,3,1:T(8,128)S(1)}, u32[]{:S(2)}, u32[]{:S(2)}) collective-permute-start(f32[32,2,64,1]{2,0,3,1:T(8,128)S(1)} %copy.49), channel_id=1, source_target_pairs={{4,0},{8,4},{12,8},{16,12},{20,16},{24,20},{28,24},{0,28},{5,1},{9... | collective-permute-start | bytes 49160 | tf_op jit(solution)/shard_map/ppermute | solution.py:26
  73.9 9.5 %copy-start.2 = (f32[32,2,64,128]{3,0,2,1:T(8,128)S(1)}, f32[32,2,64,128]{3,0,2,1:T(8,128)}, u32[]{:S(2)}) copy-start(f32[32,2,64,128]{3,0,2,1:T(8,128)} %copy-done.1) | copy-start | bytes 6291460
  73.9 6.6 %collective-permute-start.9 = (f32[32,2,64,1]{2,0,3,1:T(8,128)S(1)}, f32[32,2,64,1]{2,0,3,1:T(8,128)S(1)}, u32[]{:S(2)}, u32[]{:S(2)}) collective-permute-start(f32[32,2,64,1]{2,0,3,1:T(8,128)S(1)} %copy.51), channel_id=1, source_target_pairs={{0,4},{4,8},{8,12},{12,16},{16,20},{20,24},{24,28},{28,0},{1,5},{5... | collective-permute-start | bytes 49160 | tf_op jit(solution)/shard_map/ppermute | solution.py:25
  83.4 5.2 %copy-start.3 = (f32[32,2,64,128]{3,0,2,1:T(8,128)S(1)}, f32[32,2,64,128]{3,0,2,1:T(8,128)}, u32[]{:S(2)}) copy-start(f32[32,2,64,128]{3,0,2,1:T(8,128)} %copy-done.1) | copy-start | bytes 6291460
  83.4 5.2 %copy-start.9 = (f32[32,2,64,1]{3,0,2,1:T(8,128)S(1)}, f32[32,2,64,1]{3,0,2,1:T(8,128)}, u32[]{:S(2)}) copy-start(f32[32,2,64,1]{3,0,2,1:T(8,128)} %copy.50) | copy-start | bytes 49156
  83.4 5.2 %copy-start.12 = (f32[32,2,64,1]{3,0,2,1:T(8,128)S(1)}, f32[32,2,64,1]{3,0,2,1:T(8,128)}, u32[]{:S(2)}) copy-start(f32[32,2,64,1]{3,0,2,1:T(8,128)} %copy.52) | copy-start | bytes 49156
  84.5 2.0 %collective-permute-start.10 = (f32[32,2,1,130]{3,0,2,1:T(8,128)S(1)}, f32[32,2,1,130]{3,0,2,1:T(8,128)S(1)}, u32[]{:S(2)}, u32[]{:S(2)}) collective-permute-start(f32[32,2,1,130]{3,0,2,1:T(8,128)S(1)} %get-tuple-element.17), channel_id=1, source_target_pairs={{1,0},{2,1},{3,2},{0,3},{5,4},{6,5},{7,6},{4,7},{9,8},{10,9},{11,1... | collective-permute-start | bytes 99848 | tf_op jit(solution)/shard_map/ppermute | solution.py:26
  84.6 4.1 %collective-permute-start.11 = (f32[32,2,1,130]{3,0,2,1:T(8,128)S(1)}, f32[32,2,1,130]{3,0,2,1:T(8,128)S(1)}, u32[]{:S(2)}, u32[]{:S(2)}) collective-permute-start(f32[32,2,1,130]{3,0,2,1:T(8,128)S(1)} %get-tuple-element.18), channel_id=1, source_target_pairs={{0,1},{1,2},{2,3},{3,0},{4,5},{5,6},{6,7},{7,4},{8,9},{9,10},{10,1... | collective-permute-start | bytes 99848 | tf_op jit(solution)/shard_map/ppermute | solution.py:25
  98.0 4.7 %collective-permute-start.12 = (f32[32,2,64,1]{2,0,3,1:T(8,128)S(1)}, f32[32,2,64,1]{2,0,3,1:T(8,128)S(1)}, u32[]{:S(2)}, u32[]{:S(2)}) collective-permute-start(f32[32,2,64,1]{2,0,3,1:T(8,128)S(1)} %copy.55), channel_id=1, source_target_pairs={{4,0},{8,4},{12,8},{16,12},{20,16},{24,20},{28,24},{0,28},{5,1},{9... | collective-permute-start | bytes 49160 | tf_op jit(solution)/shard_map/ppermute | solution.py:26
  102.4 6.6 %collective-permute-start.13 = (f32[32,2,64,1]{2,0,3,1:T(8,128)S(1)}, f32[32,2,64,1]{2,0,3,1:T(8,128)S(1)}, u32[]{:S(2)}, u32[]{:S(2)}) collective-permute-start(f32[32,2,64,1]{2,0,3,1:T(8,128)S(1)} %copy.57), channel_id=1, source_target_pairs={{0,4},{4,8},{8,12},{12,16},{16,20},{20,24},{24,28},{28,0},{1,5},{5... | collective-permute-start | bytes 49160 | tf_op jit(solution)/shard_map/ppermute | solution.py:25
  112.0 5.1 %copy-start.6 = (f32[32,2,64,1]{3,0,2,1:T(8,128)S(1)}, f32[32,2,64,1]{3,0,2,1:T(8,128)}, u32[]{:S(2)}) copy-start(f32[32,2,64,1]{3,0,2,1:T(8,128)} %copy.56) | copy-start | bytes 49156
  112.0 5.1 %copy-start.10 = (f32[32,2,64,1]{3,0,2,1:T(8,128)S(1)}, f32[32,2,64,1]{3,0,2,1:T(8,128)}, u32[]{:S(2)}) copy-start(f32[32,2,64,1]{3,0,2,1:T(8,128)} %copy.58) | copy-start | bytes 49156
  113.1 2.1 %collective-permute-start.14 = (f32[32,2,1,130]{3,0,2,1:T(8,128)S(1)}, f32[32,2,1,130]{3,0,2,1:T(8,128)S(1)}, u32[]{:S(2)}, u32[]{:S(2)}) collective-permute-start(f32[32,2,1,130]{3,0,2,1:T(8,128)S(1)} %get-tuple-element.15), channel_id=1, source_target_pairs={{1,0},{2,1},{3,2},{0,3},{5,4},{6,5},{7,6},{4,7},{9,8},{10,9},{11,1... | collective-permute-start | bytes 99848 | tf_op jit(solution)/shard_map/ppermute | solution.py:26
  113.1 4.0 %collective-permute-start.15 = (f32[32,2,1,130]{3,0,2,1:T(8,128)S(1)}, f32[32,2,1,130]{3,0,2,1:T(8,128)S(1)}, u32[]{:S(2)}, u32[]{:S(2)}) collective-permute-start(f32[32,2,1,130]{3,0,2,1:T(8,128)S(1)} %get-tuple-element.16), channel_id=1, source_target_pairs={{0,1},{1,2},{2,3},{3,0},{4,5},{5,6},{6,7},{7,4},{8,9},{9,10},{10,1... | collective-permute-start | bytes 99848 | tf_op jit(solution)/shard_map/ppermute | solution.py:25
  121.9 28.7 %copy-start = (bf16[1024,128]{1,0:T(8,128)(2,1)S(1)}, bf16[1024,128]{1,0:T(8,128)(2,1)}, u32[]{:S(2)}) copy-start(bf16[1024,128]{1,0:T(8,128)(2,1)} %basis_ref.1) | copy-start | bytes 786436
  171.3 18.6 %all-to-all-start.2 = ((f32[32,32,128]{2,1,0:T(8,128)}), f32[32,32,128]{2,1,0:T(8,128)S(1)}, u32[]{:S(2)}, u32[]{:S(2)}) async-start(f32[32,32,128]{2,1,0:T(8,128)} %broadcast_in_dim.2), calls=%async_computation.2 | async-start | bytes 1048576 | tf_op jit(solution)/shard_map/all_to_all | solution.py:138
  (1 other events, 1.7 us)
where the time goes:
time: 195 us
  local copies, waits for them, and re-layouts  61 us (31%)
  blocking collectives  46.8 us (24%)
  waiting for transfers between devices  36.1 us (19%)
  other arithmetic  24.1 us (12%)
  starting transfers between devices  19.8 us (10%)
  Pallas kernels  6.15 us (3%)
    all_to_all x1, blocking collectives, shards(): lax.all_to_all(field_now.astype(jnp.bfloat16), 'gx', split_axis=0, concat...  28.3 us
    slice x7, local copies, waits for them, and re-layouts, with_halo(): last = lax.slice_in_dim(x, length - width, length, axis=dim)  18.5 us
    all_to_all x1, blocking collectives, subspace(): lax.all_to_all(partial.reshape(owners, rows_each, rank), BOTH, split_axis...  18.5 us
    ppermute x8, waiting for transfers between devices, with_halo(): before = lax.ppermute(last, axis, up)  18.2 us
    sub x3, other arithmetic, advance(): centre + diffusivity[:, None, None, None] * laplacian - 0.5 * transport  15 us
    ppermute x8, starting transfers between devices, with_halo(): after = lax.ppermute(initial, axis, down)  13 us
    ppermute x4, local copies, waits for them, and re-layouts, with_halo(): before = lax.ppermute(last, axis, up)  11.7 us
    ppermute x4, local copies, waits for them, and re-layouts, with_halo(): after = lax.ppermute(initial, axis, down)  11.7 us
  transfers between devices with their start and end apart: 17, of which 14 were waited for; matrix products, arithmetic and copies ran while one was open for 13% of the time, Pallas kernels for 0%

commit v1 on v0

v1 whole, which is shorter than its diff:
```python
import math

import jax
import jax.numpy as jnp
from jax import lax
from jax.experimental import pallas as pl
from jax.experimental.pallas import tpu as pltpu
from jax.sharding import PartitionSpec as P

SECTIONS = 4
NS_STEPS = 5
HIGHEST = lax.Precision.HIGHEST
VMEM_BYTES = 48 * 1024 * 1024
BOTH = ("gx", "gy")
LANES = 128
WIDTH = SECTIONS
WINDOW = 2 * WIDTH


def near_pairs(count):
    return [(i, i ^ 1) for i in range(count)]


def far_pairs(count):
    return [(i, (i + 1) % count if i % 2 else (i - 1) % count) for i in range(count)]


def swap_near(x, axis):
    return lax.ppermute(x, axis, near_pairs(lax.axis_size(axis)))


def swap_far(x, axis):
    return lax.ppermute(x, axis, far_pairs(lax.axis_size(axis)))


def iota(shape, dim):
    return lax.broadcasted_iota(jnp.int32, shape, dim)


def place_edges(tile, slot, packed):
    width = tile.shape[1]
    lane = iota((tile.shape[0], LANES), 1)
    both = tile
    if width > LANES:
        both = jnp.where(lane < WIDTH, tile[:, :LANES], tile[:, width - LANES :])
    rolled = pltpu.roll(both, WIDTH + WINDOW * slot, 1) if WIDTH + WINDOW * slot < LANES else (
        pltpu.roll(both, WIDTH + WINDOW * slot - LANES, 1)
    )
    return jnp.where(lane // WINDOW == slot, rolled, packed)


def pack_kernel(parity_ref, state_ref, velocity_ref, near_ref, far_ref, edges_ref):
    species, heights, length, width = state_ref.shape
    components = velocity_ref.shape[0]
    even = parity_ref[0] == 0
    sub = iota((8, width), 0)

    def edge_rows(ref, at):
        first = [ref[at, z, pl.ds(0, 8), :] for z in range(2)]
        last = [ref[at, z, pl.ds(length - 8, 8), :] for z in range(2)]
        first = jnp.where(sub < WIDTH, first[0], pltpu.roll(first[1], WIDTH, 0))
        last = jnp.where(sub < WIDTH, pltpu.roll(last[0], WIDTH, 0), last[1])
        return jnp.where(even, last, first), jnp.where(even, first, last)

    def put(pair, one, two):
        near_ref[pair] = jnp.concatenate([one[0], two[0]], axis=0).astype(jnp.bfloat16)
        far_ref[pair] = jnp.concatenate([one[1], two[1]], axis=0).astype(jnp.bfloat16)

    def pair_body(pair, carry):
        put(pair, edge_rows(state_ref, 2 * pair), edge_rows(state_ref, 2 * pair + 1))
        return carry

    lax.fori_loop(0, species // 2, pair_body, 0, unroll=2)
    flows = [edge_rows(velocity_ref, at) for at in range(components)]
    put(species // 2, flows[0], flows[1])
    put(species // 2 + 1, flows[2], flows[2])

    per_group = LANES // WINDOW

    def rows_body(at, carry):
        start = pl.multiple_of(at * 16, 16)
        for z in range(heights):
            target = pl.ds(pl.multiple_of(z * length + start, 16), 16)
            for group in range(species // per_group):
                packed = jnp.zeros((16, LANES), jnp.float32)
                for slot in range(per_group):
                    tile = state_ref[group * per_group + slot, z, pl.ds(start, 16), :]
                    packed = place_edges(tile, slot, packed)
                edges_ref[group, target, :] = packed.astype(jnp.bfloat16)
            packed = jnp.zeros((16, LANES), jnp.float32)
            for slot in range(components):
                packed = place_edges(velocity_ref[slot, z, pl.ds(start, 16), :], slot, packed)
            edges_ref[species // per_group, target, :] = packed.astype(jnp.bfloat16)
        return carry

    lax.fori_loop(0, length // 16, rows_body, 0)


def halo_kernel(parity_ref, near_ref, far_ref, velocity_ref, old_ref, rows_ref, half_ref, edges_ref):
    species, _, width = rows_ref.shape
    components, heights, length, _ = velocity_ref.shape
    even = parity_ref[0] == 0
    sub = iota((8, width), 0)
    per_group = LANES // WINDOW

    def tile_of(at):
        near = near_ref[at // 2].astype(jnp.float32)[8 * (at % 2) : 8 * (at % 2) + 8]
        far = far_ref[at // 2].astype(jnp.float32)[8 * (at % 2) : 8 * (at % 2) + 8]
        after = jnp.where(even, near, far)
        before = jnp.where(even, far, near)
        one = jnp.where(sub < WIDTH, after, pltpu.roll(before, WIDTH, 0))
        two = jnp.where(sub < WIDTH, pltpu.roll(after, WIDTH, 0), before)
        return jnp.concatenate([one, two], axis=0)

    for group in range(species // per_group):
        packed = jnp.zeros((16, LANES), jnp.float32)
        for slot in range(per_group):
            tile = tile_of(group * per_group + slot)
            rows_ref[group * per_group + slot] = tile
            packed = place_edges(tile, slot, packed)
        edges_ref[group] = packed.astype(jnp.bfloat16)
    packed = jnp.zeros((16, LANES), jnp.float32)
    for slot in range(components):
        tile = tile_of(species + slot)
        packed = place_edges(tile, slot, packed)
        for z in range(heights):
            factor = -0.5 if slot == 2 and z == 1 else 0.5
            half_ref[slot, z, pl.ds(0, length), :] = factor * velocity_ref[slot, z]
            half_ref[slot, z, pl.ds(length, 8), :] = factor * tile[8 * z : 8 * z + 8]
    edges_ref[species // per_group] = packed.astype(jnp.bfloat16)


def advance(here, other, east, west, flow, diffusion, rate):
    north = pltpu.roll(here, here.shape[0] - 1, 0)
    south = pltpu.roll(here, 1, 0)
    square = 1.0 + here * here
    inverse = pl.reciprocal(square, approx=True)
    inverse = inverse * (2.0 - square * inverse)
    centre = here * ((1.0 - 6.0 * diffusion - rate) + rate * inverse)
    spread = diffusion * ((east + west) + (north + south))
    moved = flow[0] * (east - west) + flow[1] * (north - south)
    return (centre + other * (diffusion - flow[2])) + (spread - moved)


def window_kernel(parity_ref, own_ref, near_ref, far_ref, spread_ref, rate_ref, border_ref):
    sections, groups, heights, rows, _ = border_ref.shape
    length = rows - 8
    even = parity_ref[0] == 0
    lane = iota((rows, LANES), 1)
    low = lane % WINDOW < WIDTH

    def rows_of(ref, group, z):
        whole = ref[group].astype(jnp.float32)
        body = whole[z * length : (z + 1) * length]
        return jnp.concatenate(
            [body, whole[heights * length + 8 * z : heights * length + 8 * z + 8]], axis=0
        )

    def windows(group):
        out = []
        for z in range(heights):
            own, near, far = [rows_of(r, group, z) for r in (own_ref, near_ref, far_ref)]
            right = jnp.where(even, near, far)
            left = jnp.where(even, far, near)
            out.append((jnp.where(low, left, own), jnp.where(low, own, right)))
        return [[out[z][side] for z in range(heights)] for side in range(2)]

    def spread_lanes(packed, slot):
        part = jnp.where(lane // WINDOW == slot, packed, 0.0)
        step = WINDOW
        while step < LANES:
            part = part + pltpu.roll(part, step, 1)
            step *= 2
        return part

    flows = windows(groups)
    flow = [
        [
            [
                (-0.5 if slot == 2 and z == 1 else 0.5) * spread_lanes(flows[side][z], slot)
                for slot in range(3)
            ]
            for z in range(heights)
        ]
        for side in range(2)
    ]
    for group in range(groups):
        now = windows(group)
        diffusion = spread_ref[group]
        rate = rate_ref[group]
        for section in range(sections):
            for z in range(heights):
                border_ref[section, group, z] = jnp.where(low, now[0][z], now[1][z])
            if section == sections - 1:
                break
            now = [
                [
                    advance(
                        now[side][z],
                        now[side][1 - z],
                        pltpu.roll(now[side][z], LANES - 1, 1),
                        pltpu.roll(now[side][z], 1, 1),
                        flow[side][z],
                        diffusion,
                        rate,
                    )
                    for z in range(heights)
                ]
                for side in range(2)
            ]


def section_kernel(
    first_ref, state_ref, rows_ref, border_ref, half_ref, spread_ref, rate_ref, *rest
):
    evolved_ref, piece_ref = rest[-2:]
    _, heights, length, width = state_ref.shape
    sections = border_ref.shape[0]
    rows = length + 8
    at = first_ref[0] + pl.program_id(0)
    slot = lax.rem(at, LANES // WINDOW)
    shift = LANES - WIDTH - WINDOW * slot
    diffusion = spread_ref[at]
    rate = rate_ref[at]
    lane = iota((rows, width), 1)
    now = [
        jnp.concatenate([state_ref[0, z], rows_ref[0, pl.ds(8 * z, 8), :]], axis=0)
        for z in range(heights)
    ]
    for section in range(sections):
        later = []
        for z in range(heights):
            border = pltpu.roll(border_ref[section, 0, z], shift, 1)
            if width > LANES:
                border = jnp.concatenate([border] * (width // LANES), axis=1)
            east = pltpu.roll(jnp.where(lane == 0, border, now[z]), width - 1, 1)
            west = pltpu.roll(jnp.where(lane == width - 1, border, now[z]), 1, 1)
            flow = [half_ref[slot_at, z] for slot_at in range(3)]
            later.append(advance(now[z], now[1 - z], east, west, flow, diffusion, rate))
        now = later
    for z in range(heights):
        evolved_ref[0, z] = now[z][:length]
        piece_ref[0, pl.ds(z * length, length), :] = now[z][:length].astype(jnp.bfloat16)


def image_kernel(place_ref, basis_ref, *rest):
    columns, image_ref = rest[:-1], rest[-1]
    width = columns[0].shape[1]

    def rows_of(piece):
        return pl.ds(pl.multiple_of((place_ref[0] ^ piece) * width, width), width)

    project = jnp.zeros((columns[0].shape[0], basis_ref.shape[1]), jnp.float32)
    for piece, column in enumerate(columns):
        project += jnp.dot(
            column[...], basis_ref[rows_of(piece), :], preferred_element_type=jnp.float32
        )
    project = project.astype(jnp.bfloat16)
    for piece, column in enumerate(columns):
        image_ref[rows_of(piece), :] = lax.dot_general(
            column[...], project, (((0,), (0,)), ((), ())), preferred_element_type=jnp.float32
        ).astype(image_ref.dtype)


def factor_kernel(place_ref, image_ref, *rest):
    columns, (own_ref, core_ref, factor_ref) = rest[:-3], rest[-3:]
    rows, width = columns[0].shape
    rows_all, rank = image_ref.shape
    rows_each = own_ref.shape[0]
    image = image_ref[...]
    identity = (iota((rank, rank), 0) == iota((rank, rank), 1)).astype(jnp.float32)
    gram = lax.dot_general(
        image,
        image,
        (((0,), (0,)), ((), ())),
        precision=HIGHEST,
        preferred_element_type=jnp.float32,
    )
    trace = jnp.sum(gram * identity)
    gram = gram / (trace + 1e-06)
    product = None
    for step in range(NS_STEPS):
        update = 1.5 * identity - 0.5 * gram
        if step < NS_STEPS - 1:
            gram = jnp.dot(gram, update, precision=HIGHEST, preferred_element_type=jnp.float32)
            gram = jnp.dot(update, gram, precision=HIGHEST, preferred_element_type=jnp.float32)
        if product is None:
            product = update
        else:
            product = jnp.dot(
                product, update, precision=HIGHEST, preferred_element_type=jnp.float32
            )
    scaling = jnp.sqrt(rows_all / (trace + 1e-06))
    factor = jnp.dot(
        image * scaling, product, precision=HIGHEST, preferred_element_type=jnp.float32
    )
    factor_ref[...] = factor.astype(jnp.bfloat16)
    start = pl.multiple_of(place_ref[1] * rows_each, rows_each)
    own_ref[...] = factor_ref[pl.ds(start, rows_each), :]
    core = jnp.zeros((rows, rank), jnp.float32)
    for piece, column in enumerate(columns):
        at = pl.ds(pl.multiple_of((place_ref[0] ^ piece) * width, width), width)
        core += jnp.dot(column[...], factor_ref[at, :], preferred_element_type=jnp.float32)
    core_ref[...] = core / math.sqrt(rows_all)


def call(kernel, out_shape, inputs, **rest):
    return pl.pallas_call(
        kernel,
        out_shape=out_shape,
        compiler_params=pltpu.CompilerParams(vmem_limit_bytes=VMEM_BYTES),
        **rest,
    )(*inputs)


def vmem(count):
    return [pl.BlockSpec(memory_space=pltpu.VMEM)] * count


SCALARS = [pl.BlockSpec(memory_space=pltpu.SMEM)]


def subspace(columns, start_basis):
    rows, width = columns[0].shape
    rows_all, rank = start_basis.shape
    owners = lax.axis_size(BOTH)
    rows_each = rows_all // owners
    place = jnp.stack([lax.axis_index("gx"), lax.axis_index(BOTH)]).astype(jnp.int32)
    partial = call(
        image_kernel,
        jax.ShapeDtypeStruct((rows_all, rank), jnp.float32),
        (place, start_basis, *columns),
        in_specs=SCALARS + vmem(1 + len(columns)),
        out_specs=vmem(1)[0],
    )
    shares = lax.all_to_all(
        partial.reshape(owners, rows_each, rank), BOTH, split_axis=0, concat_axis=0, tiled=True
    )
    own_image = jnp.sum(shares, axis=0)
    image = lax.all_to_all(
        jnp.broadcast_to(own_image[None], (owners, rows_each, rank)),
        BOTH,
        split_axis=0,
        concat_axis=0,
        tiled=True,
    ).reshape(rows_all, rank)
    return call(
        factor_kernel,
        (
            jax.ShapeDtypeStruct((rows_each, rank), jnp.bfloat16),
            jax.ShapeDtypeStruct((rows, rank), jnp.float32),
        ),
        (place, image, *columns),
        in_specs=SCALARS + vmem(1 + len(columns)),
        out_specs=tuple(vmem(2)),
        scratch_shapes=[pltpu.VMEM((rows_all, rank), jnp.bfloat16)],
    )


def borders(initial_state, velocity, diffusivity, reaction_rate):
    species, heights, length, width = initial_state.shape
    groups = species * WINDOW // LANES
    parity = (lax.axis_index("gy") % 2).astype(jnp.int32).reshape(1)
    edge = jax.ShapeDtypeStruct((species // 2 + 2, 16, width), jnp.bfloat16)
    window = jax.ShapeDtypeStruct((groups + 1, heights * (length + 8), LANES), jnp.bfloat16)
    near, far, edges = call(
        pack_kernel,
        (edge, edge, window),
        (parity, initial_state, velocity),
        in_specs=SCALARS + vmem(2),
        out_specs=tuple(vmem(3)),
    )
    near = swap_near(near, "gy")
    far = swap_far(far, "gy")
    last = heights * length // 16
    halo_rows, half, edges = call(
        halo_kernel,
        (
            jax.ShapeDtypeStruct((species, 16, width), jnp.float32),
            jax.ShapeDtypeStruct((3, heights, length + 8, width), jnp.float32),
            window,
        ),
        (parity, near, far, velocity, edges),
        grid=(1,),
        in_specs=SCALARS + vmem(3) + [pl.BlockSpec(memory_space=pl.ANY)],
        out_specs=tuple(
            vmem(2) + [pl.BlockSpec((groups + 1, 16, LANES), lambda i: (0, last, 0))]
        ),
        input_output_aliases={4: 2},
    )
    near = swap_near(edges, "gx")
    far = swap_far(edges, "gx")
    parity = (lax.axis_index("gx") % 2).astype(jnp.int32).reshape(1)
    lanes = [jnp.repeat(v, WINDOW).reshape(groups, 1, LANES) for v in (diffusivity, reaction_rate)]
    border = call(
        window_kernel,
        jax.ShapeDtypeStruct((SECTIONS, groups, heights, length + 8, LANES), jnp.float32),
        (parity, edges, near, far, *lanes),
        in_specs=SCALARS + vmem(5),
        out_specs=vmem(1)[0],
    )
    return halo_rows, half, border


def sections(first, count, evolved, initial_state, halo_rows, border, half, diffusivity, rate):
    species, heights, length, width = initial_state.shape
    per_group = LANES // WINDOW
    state_spec = pl.BlockSpec((1, heights, length, width), lambda i, f: (f[0] + i, 0, 0, 0))
    in_specs = [
        state_spec,
        pl.BlockSpec((1, 16, width), lambda i, f: (f[0] + i, 0, 0)),
        pl.BlockSpec(
            (SECTIONS, 1, heights, length + 8, LANES),
            lambda i, f: (0, (f[0] + i) // per_group, 0, 0, 0),
        ),
        pl.BlockSpec(half.shape, lambda i, f: (0, 0, 0, 0)),
        pl.BlockSpec(memory_space=pltpu.SMEM),
        pl.BlockSpec(memory_space=pltpu.SMEM),
    ]
    inputs = [first, initial_state, halo_rows, border, half, diffusivity, rate]
    aliases = {}
    if evolved is not None:
        in_specs.append(pl.BlockSpec(memory_space=pl.ANY))
        aliases[len(inputs)] = 0
        inputs.append(evolved)
    return call(
        section_kernel,
        (
            jax.ShapeDtypeStruct(initial_state.shape, jnp.float32),
            jax.ShapeDtypeStruct((count, heights * length, width), jnp.bfloat16),
        ),
        inputs,
        grid_spec=pltpu.PrefetchScalarGridSpec(
            num_scalar_prefetch=1,
            grid=(count,),
            in_specs=in_specs,
            out_specs=(
                state_spec,
                pl.BlockSpec((1, heights * length, width), lambda i, f: (i, 0, 0)),
            ),
        ),
        input_output_aliases=aliases,
    )


def shards(initial_state, velocity, diffusivity, reaction_rate, start_basis):
    species, heights, length, width = initial_state.shape
    pieces = lax.axis_size("gx")
    each = species // pieces
    place = lax.axis_index("gx").astype(jnp.int32)
    halo_rows, half, border = borders(initial_state, velocity, diffusivity, reaction_rate)
    evolved = None
    columns = [None] * pieces
    for offset in reversed(range(pieces)):
        first = ((place ^ offset) * each).reshape(1)
        evolved, piece = sections(
            first,
            each,
            evolved,
            initial_state,
            halo_rows,
            border,
            half,
            diffusivity,
            reaction_rate,
        )
        piece = piece.reshape(each * heights * length, width)
        if offset:
            piece = lax.ppermute(piece, "gx", [(i, i ^ offset) for i in range(pieces)])
        columns[offset] = piece
    own_rows, core = subspace(columns, start_basis)
    return (evolved, own_rows, core.reshape(each, heights, length, start_basis.shape[1]))


def solution(mesh):
    in_specs = (P(None, None, "gy", "gx"), P(None, None, "gy", "gx"), P(), P(), P())
    out_specs = (P(None, None, "gy", "gx"), P(("gx", "gy"), None), P("gx", None, "gy", None))
    return jax.shard_map(shards, mesh=mesh, in_specs=in_specs, out_specs=out_specs, check_vma=False)
```

time: 195 us -> 121 us (0.62)
  local copies, waits for them, and re-layouts: 61 us -> 3.72 us
  Pallas kernels: 6.15 us -> 37.7 us
  other arithmetic: 24.1 us -> 0.12 us
  waiting for transfers between devices: 36.1 us -> 16.3 us
  blocking collectives: 46.8 us -> 41.2 us
    pallas_call x2 -> x13, Pallas kernels: 6.15 us -> 37.7 us  [call(): pl.pallas_call(kernel, out_shape=out_shape, compiler_params=pltpu.Compile...]
    slice x10 -> x0, local copies, waits for them, and re-layouts: 26.4 us -> none  [the longest x7 18.5 us: with_halo(): last = lax.slice_in_dim(x, length - width, length, axis=dim)]
    ppermute x8 -> x0, local copies, waits for them, and re-layouts: 23.3 us -> none  [the longest x4 11.7 us: with_halo(): before = lax.ppermute(last, axis, up)]
    sub x3 -> x0, other arithmetic: 15 us -> none  [advance(): centre + diffusivity[:, None, None, None] * laplacian - 0.5 * transport]
    all_to_all x1 -> x0, waiting for transfers between devices: 11.2 us -> none  [subspace(): lax.all_to_all(jnp.broadcast_to(own_image[None], (owners, rows_each, rank...]
    all_to_all x1, blocking collectives: 28.3 us -> 18.4 us  [subspace(): lax.all_to_all(jnp.broadcast_to(own_image[None], (owners, rows_each, rank...]
    ppermute x16 -> x11, waiting for transfers between devices: 24.9 us -> 16.3 us  [the longest x7 8.29 us: shards(): piece = lax.ppermute(piece, 'gx', [(i, i ^ offset) for i in range(pieces)])]
    unnamed x36 -> x16, local copies, waits for them, and re-layouts: 9.95 us -> 3.18 us
  transfers between devices with their start and end apart: 17 -> 11, of which waited for: 14 -> 5; matrix products, arithmetic and copies ran while one was open for 13% -> 0% of each run, Pallas kernels for 0% -> 3%
where the time goes in v1:
time: 121 us; the launch traced here: 120 us
  blocking collectives  41.2 us (34%)
  Pallas kernels  37.7 us (31%)
  starting transfers between devices  20.6 us (17%)
  waiting for transfers between devices  16.3 us (13%)
  local copies, waits for them, and re-layouts  3.72 us (3%)
    pallas_call x13, Pallas kernels, call(): pl.pallas_call(kernel, out_shape=out_shape, compiler_params=pltpu.Compile...  37.7 us
    all_to_all x1, blocking collectives, subspace(): lax.all_to_all(partial.reshape(owners, rows_each, rank), BOTH, split_axis...  22.8 us
    all_to_all x1, blocking collectives, subspace(): lax.all_to_all(jnp.broadcast_to(own_image[None], (owners, rows_each, rank...  18.4 us
    ppermute x7, starting transfers between devices, shards(): piece = lax.ppermute(piece, 'gx', [(i, i ^ offset) for i in range(pieces)])  12.9 us
    ppermute x7, waiting for transfers between devices, shards(): piece = lax.ppermute(piece, 'gx', [(i, i ^ offset) for i in range(pieces)])  8.29 us
    ppermute x2, starting transfers between devices, swap_far(): return lax.ppermute(x, axis, far_pairs(lax.axis_size(axis)))  7.17 us
    ppermute x2, waiting for transfers between devices, swap_far(): return lax.ppermute(x, axis, far_pairs(lax.axis_size(axis)))  5.72 us
    unnamed x16, local copies, waits for them, and re-layouts  3.18 us
  transfers between devices with their start and end apart: 11, of which 5 were waited for; matrix products, arithmetic and copies ran while one was open for 0% of the time, Pallas kernels for 3%

profile of v1, /device:TPU:0, one launch (start us, length us, event | category | flops | bytes accessed | tf_op | source)
XLA Modules:
  0.0 120.5 jit_solution(1687571650484277347)
XLA Ops:
  0.7 1.6 %copy-done = f32[32,2,64,128]{3,2,1,0:T(8,128)S(1)} copy-done((f32[32,2,64,128]{3,2,1,0:T(8,128)S(1)}, f32[32,2,64,128]{3,2,1,0:T(8,128)}, u32[]{:S(2)}) %copy-start) | copy-done | bytes 2097176
  2.3 0.9 copy-done.2
  3.2 0.6 shard_map.76
  3.8 0.5 collective-permute-start
  4.4 2.6 %collective-permute-start.1 = (bf16[18,16,128]{2,1,0:T(8,128)(2,1)S(1)}, bf16[18,16,128]{2,1,0:T(8,128)(2,1)S(1)}, u32[]{:S(2)}, u32[]{:S(2)}) collective-permute-start(bf16[18,16,128]{2,1,0:T(8,128)(2,1)S(1)} %get-tuple-element.28), channel_id=1, source_target_pairs={{0,3},{1,2},{2,1},{3,0},{4,7},{5,6},{6,5},{7,4},{8,11},{9,10},{10,... | collective-permute-start | bytes 221192 | tf_op jit(solution)/shard_map/ppermute | solution.py:33
  7.0 2.5 %collective-permute-done.1.far_ref = bf16[18,16,128]{2,1,0:T(8,128)(2,1)S(1)} collective-permute-done((bf16[18,16,128]{2,1,0:T(8,128)(2,1)S(1)}, bf16[18,16,128]{2,1,0:T(8,128)(2,1)S(1)}, u32[]{:S(2)}, u32[]{:S(2)}) %collective-permute-start.1) | collective-permute-done | bytes 73760 | tf_op jit(solution)/shard_map/ppermute | solution.py:33
  9.5 0.1 shard_map.77
  9.6 4.6 %collective-permute-start.3 = (bf16[3,144,128]{2,1,0:T(8,128)(2,1)S(1)}, bf16[3,144,128]{2,1,0:T(8,128)(2,1)S(1)}, u32[]{:S(2)}, u32[]{:S(2)}) collective-permute-start(bf16[3,144,128]{2,1,0:T(8,128)(2,1)S(1)} %get-tuple-element.31.own_ref), channel_id=1, source_target_pairs={{0,28},{4,8},{8,4},{12,16},{16,12},{20,24},{24,20},{28,0},{1,29},{... | collective-permute-start | bytes 331784 | tf_op jit(solution)/shard_map/ppermute | solution.py:33
  14.7 3.2 %collective-permute-done.3.far_ref = bf16[3,144,128]{2,1,0:T(8,128)(2,1)S(1)} collective-permute-done((bf16[3,144,128]{2,1,0:T(8,128)(2,1)S(1)}, bf16[3,144,128]{2,1,0:T(8,128)(2,1)S(1)}, u32[]{:S(2)}, u32[]{:S(2)}) %collective-permute-start.3) | collective-permute-done | bytes 110624 | tf_op jit(solution)/shard_map/ppermute | solution.py:33
  17.9 2.3 %collective-permute-done.2.near_ref = bf16[3,144,128]{2,1,0:T(8,128)(2,1)S(1)} collective-permute-done((bf16[3,144,128]{2,1,0:T(8,128)(2,1)S(1)}, bf16[3,144,128]{2,1,0:T(8,128)(2,1)S(1)}, u32[]{:S(2)}, u32[]{:S(2)}) %collective-permute-start.2) | collective-permute-done | bytes 110624 | tf_op jit(solution)/shard_map/ppermute | solution.py:29
  20.2 2.3 %shard_map.78.border_ref = f32[4,2,2,72,128]{4,3,2,1,0:T(8,128)S(1)} custom-call(s32[1]{0:T(128)} %bitcast.2.parity_ref, bf16[3,144,128]{2,1,0:T(8,128)(2,1)S(1)} %get-tuple-element.31.own_ref, bf16[3,144,128]{2,1,0:T(8,128)(2,1)S(1)} %collective-permute-done.2.near_ref, bf16[3,144,128]{2,1,0:T(8,128)(2,1)S(1)} %collective-permute-done.3.far_ref, ...), custom_call_target="tpu_custom_call" | custom-call | tf_op jit(solution)/shard_map/pallas_call | solution.py:308
  22.5 3.3 %shard_map.79 = (f32[32,2,64,128]{3,2,1,0:T(8,128)}, bf16[4,128,128]{2,1,0:T(8,128)(2,1)}) custom-call(s32[1]{0:T(128)} %bitcast.11.first_ref, f32[32,2,64,128]{3,2,1,0:T(8,128)S(1)} %copy-done.1, f32[32,16,128]{2,1,0:T(8,128)S(1)} %get-tuple-element.30.rows_ref, f32[4,2,2,72,128]{4,3,2,1,0:T(8,128)S(1)} %shard_map.78.border_ref, ...), custom_call_target="tpu_custom_call" | custom-call | tf_op jit(solution)/shard_map/pallas_call | solution.py:308
  25.8 3.3 %shard_map.80 = (f32[32,2,64,128]{3,2,1,0:T(8,128)}, bf16[4,128,128]{2,1,0:T(8,128)(2,1)}) custom-call(s32[1]{0:T(128)} %bitcast.10.first_ref, f32[32,2,64,128]{3,2,1,0:T(8,128)S(1)} %copy-done.1, f32[32,16,128]{2,1,0:T(8,128)S(1)} %get-tuple-element.30.rows_ref, f32[4,2,2,72,128]{4,3,2,1,0:T(8,128)S(1)} %shard_map.78.border_ref, ...), custom_call_target="tpu_custom_call", output_to_operand_aliasing={{0}: (7, {})} | custom-call | tf_op jit(solution)/shard_map/pallas_call | solution.py:308
  29.1 3.3 %shard_map.81 = (f32[32,2,64,128]{3,2,1,0:T(8,128)}, bf16[4,128,128]{2,1,0:T(8,128)(2,1)}) custom-call(s32[1]{0:T(128)} %bitcast.9.first_ref, f32[32,2,64,128]{3,2,1,0:T(8,128)S(1)} %copy-done.1, f32[32,16,128]{2,1,0:T(8,128)S(1)} %get-tuple-element.30.rows_ref, f32[4,2,2,72,128]{4,3,2,1,0:T(8,128)S(1)} %shard_map.78.border_ref, ...), custom_call_target="tpu_custom_call", output_to_operand_aliasing={{0}: (7, {})} | custom-call | tf_op jit(solution)/shard_map/pallas_call | solution.py:308
  32.3 3.3 %shard_map.82 = (f32[32,2,64,128]{3,2,1,0:T(8,128)}, bf16[4,128,128]{2,1,0:T(8,128)(2,1)}) custom-call(s32[1]{0:T(128)} %bitcast.8.first_ref, f32[32,2,64,128]{3,2,1,0:T(8,128)S(1)} %copy-done.1, f32[32,16,128]{2,1,0:T(8,128)S(1)} %get-tuple-element.30.rows_ref, f32[4,2,2,72,128]{4,3,2,1,0:T(8,128)S(1)} %shard_map.78.border_ref, ...), custom_call_target="tpu_custom_call", output_to_operand_aliasing={{0}: (7, {})} | custom-call | tf_op jit(solution)/shard_map/pallas_call | solution.py:308
  35.6 3.3 %shard_map.83 = (f32[32,2,64,128]{3,2,1,0:T(8,128)}, bf16[4,128,128]{2,1,0:T(8,128)(2,1)}) custom-call(s32[1]{0:T(128)} %bitcast.7.first_ref, f32[32,2,64,128]{3,2,1,0:T(8,128)S(1)} %copy-done.1, f32[32,16,128]{2,1,0:T(8,128)S(1)} %get-tuple-element.30.rows_ref, f32[4,2,2,72,128]{4,3,2,1,0:T(8,128)S(1)} %shard_map.78.border_ref, ...), custom_call_target="tpu_custom_call", output_to_operand_aliasing={{0}: (7, {})} | custom-call | tf_op jit(solution)/shard_map/pallas_call | solution.py:308
  38.8 3.2 %shard_map.84 = (f32[32,2,64,128]{3,2,1,0:T(8,128)}, bf16[4,128,128]{2,1,0:T(8,128)(2,1)S(1)}) custom-call(s32[1]{0:T(128)} %bitcast.6.first_ref, f32[32,2,64,128]{3,2,1,0:T(8,128)S(1)} %copy-done.1, f32[32,16,128]{2,1,0:T(8,128)S(1)} %get-tuple-element.30.rows_ref, f32[4,2,2,72,128]{4,3,2,1,0:T(8,128)S(1)} %shard_map.78.border_ref, ...), custom_call_target="tpu_custom_call", output_to_operand_aliasing={{0}: (7, {})} | custom-call | tf_op jit(solution)/shard_map/pallas_call | solution.py:308
  42.1 3.2 %shard_map.85 = (f32[32,2,64,128]{3,2,1,0:T(8,128)}, bf16[4,128,128]{2,1,0:T(8,128)(2,1)S(1)}) custom-call(s32[1]{0:T(128)} %bitcast.5.first_ref, f32[32,2,64,128]{3,2,1,0:T(8,128)S(1)} %copy-done.1, f32[32,16,128]{2,1,0:T(8,128)S(1)} %get-tuple-element.30.rows_ref, f32[4,2,2,72,128]{4,3,2,1,0:T(8,128)S(1)} %shard_map.78.border_ref, ...), custom_call_target="tpu_custom_call", output_to_operand_aliasing={{0}: (7, {})} | custom-call | tf_op jit(solution)/shard_map/pallas_call | solution.py:308
  45.3 1.2 collective-permute-start.5
  46.5 2.3 %collective-permute-start.6 = (bf16[512,128]{1,0:T(8,128)(2,1)}, bf16[512,128]{1,0:T(8,128)(2,1)}, u32[]{:S(2)}, u32[]{:S(2)}) collective-permute-start(bf16[512,128]{1,0:T(8,128)(2,1)} %bitcast.17), channel_id=1, source_target_pairs={{0,12},{4,8},{8,4},{12,0},{16,28},{20,24},{24,20},{28,16},{1,13},{... | collective-permute-start | bytes 393224 | tf_op jit(solution)/shard_map/ppermute | solution.py:469
  48.8 0.7 collective-permute-start.7
  49.5 1.7 %collective-permute-start.8 = (bf16[512,128]{1,0:T(8,128)(2,1)}, bf16[512,128]{1,0:T(8,128)(2,1)}, u32[]{:S(2)}, u32[]{:S(2)}) collective-permute-start(bf16[512,128]{1,0:T(8,128)(2,1)} %bitcast.19), channel_id=1, source_target_pairs={{0,20},{4,16},{8,28},{12,24},{16,4},{20,0},{24,12},{28,8},{1,21},{... | collective-permute-start | bytes 393224 | tf_op jit(solution)/shard_map/ppermute | solution.py:469
  51.2 2.6 %collective-permute-start.9 = (bf16[512,128]{1,0:T(8,128)(2,1)}, bf16[512,128]{1,0:T(8,128)(2,1)}, u32[]{:S(2)}, u32[]{:S(2)}) collective-permute-start(bf16[512,128]{1,0:T(8,128)(2,1)} %bitcast.20), channel_id=1, source_target_pairs={{0,24},{4,28},{8,16},{12,20},{16,8},{20,12},{24,0},{28,4},{1,25},{... | collective-permute-start | bytes 393224 | tf_op jit(solution)/shard_map/ppermute | solution.py:469
  53.8 4.4 %collective-permute-start.10 = (bf16[512,128]{1,0:T(8,128)(2,1)}, bf16[512,128]{1,0:T(8,128)(2,1)}, u32[]{:S(2)}, u32[]{:S(2)}) collective-permute-start(bf16[512,128]{1,0:T(8,128)(2,1)} %bitcast.21), channel_id=1, source_target_pairs={{0,28},{4,24},{8,20},{12,16},{16,12},{20,8},{24,4},{28,0},{1,29},{... | collective-permute-start | bytes 393224 | tf_op jit(solution)/shard_map/ppermute | solution.py:469
  58.3 3.2 %shard_map.86 = (f32[32,2,64,128]{3,2,1,0:T(8,128)}, bf16[4,128,128]{2,1,0:T(8,128)(2,1)S(1)}) custom-call(s32[1]{0:T(128)} %bitcast.first_ref, f32[32,2,64,128]{3,2,1,0:T(8,128)S(1)} %copy-done.1, f32[32,16,128]{2,1,0:T(8,128)S(1)} %get-tuple-element.30.rows_ref, f32[4,2,2,72,128]{4,3,2,1,0:T(8,128)S(1)} %shard_map.78.border_ref, ...), custom_call_target="tpu_custom_call", output_to_operand_aliasing={{0}: (7, {})} | custom-call | tf_op jit(solution)/shard_map/pallas_call | solution.py:308
  61.5 6.2 %collective-permute-done.7.rest_4_ = bf16[512,128]{1,0:T(8,128)(2,1)} collective-permute-done((bf16[512,128]{1,0:T(8,128)(2,1)}, bf16[512,128]{1,0:T(8,128)(2,1)}, u32[]{:S(2)}, u32[]{:S(2)}) %collective-permute-start.7) | collective-permute-done | bytes 131104 | tf_op jit(solution)/shard_map/ppermute | solution.py:469
  67.7 2.1 %collective-permute-done.8.rest_5_ = bf16[512,128]{1,0:T(8,128)(2,1)} collective-permute-done((bf16[512,128]{1,0:T(8,128)(2,1)}, bf16[512,128]{1,0:T(8,128)(2,1)}, u32[]{:S(2)}, u32[]{:S(2)}) %collective-permute-start.8) | collective-permute-done | bytes 131104 | tf_op jit(solution)/shard_map/ppermute | solution.py:469
  69.8 2.5 %shard_map.87 = f32[1024,128]{1,0:T(8,128)S(1)} custom-call(s32[2]{0:T(128)S(1)} %pad_add_fusion.place_ref, bf16[1024,128]{1,0:T(8,128)(2,1)S(1)} %copy-done.5, bf16[512,128]{1,0:T(8,128)(2,1)S(1)} %bitcast.27, bf16[512,128]{1,0:T(8,128)(2,1)S(1)} %collective-permute-done.4.rest_1_, bf16[512,128]{1,0:T(8,128)(2,1)S(1)} %collective-permute-done.5.rest_2_, ...), custom_call_target="tpu_custom_call" | custom-call | tf_op jit(solution)/shard_map/pallas_call | solution.py:308
  72.3 0.6 copy-done.3
  73.0 22.8 %all_to_all.10 = f32[32,32,128]{2,1,0:T(8,128)S(1)} all-to-all(f32[32,32,128]{2,1,0:T(8,128)S(1)} %bitcast.26), channel_id=1, replica_groups=mesh['gx'=8,'gy'=4] {'gx','gy'}, dimensions={0} | all-to-all | bytes 1048576 | tf_op jit(solution)/shard_map/all_to_all | solution.py:336
  95.9 18.4 %all_to_all.11 = f32[32,32,128]{2,1,0:T(8,128)S(1)} all-to-all(f32[32,32,128]{2,1,0:T(8,128)S(1)} %broadcast_in_dim.26), channel_id=1, replica_groups=mesh['gx'=8,'gy'=4] {'gx','gy'}, dimensions={0} | all-to-all | bytes 1048576 | tf_op jit(solution)/shard_map/all_to_all | solution.py:340
  114.3 6.1 %shard_map.88 = (bf16[32,128]{1,0:T(8,128)(2,1)}, f32[512,128]{1,0:T(8,128)}) custom-call(s32[2]{0:T(128)S(1)} %pad_add_fusion.place_ref, f32[1024,128]{1,0:T(8,128)S(1)} %bitcast.25, bf16[512,128]{1,0:T(8,128)(2,1)S(1)} %bitcast.28, bf16[512,128]{1,0:T(8,128)(2,1)S(1)} %collective-permute-done.4.rest_1_, ...), custom_call_target="tpu_custom_call" | custom-call | tf_op jit(solution)/shard_map/pallas_call | solution.py:308
  (30 shorter events, 0.7 us)
Async XLA Ops:
  0.6 13.6 %copy-start.6 = (f32[32]{0:T(128)S(1)}, f32[32]{0:T(128)}, u32[]{:S(2)}) copy-start(f32[32]{0:T(128)} %spread_ref.15) | copy-start | bytes 388
  0.6 13.7 %copy-start.7 = (f32[32]{0:T(128)S(1)}, f32[32]{0:T(128)}, u32[]{:S(2)}) copy-start(f32[32]{0:T(128)} %rate_ref.15) | copy-start | bytes 388
  0.7 1.6 %copy-start = (f32[32,2,64,128]{3,2,1,0:T(8,128)S(1)}, f32[32,2,64,128]{3,2,1,0:T(8,128)}, u32[]{:S(2)}) copy-start(f32[32,2,64,128]{3,2,1,0:T(8,128)} %state_ref.17) | copy-start | bytes 6291460
  2.3 0.9 copy-start.2
  3.2 19.3 %copy-start.1 = (f32[32,2,64,128]{3,2,1,0:T(8,128)S(1)}, f32[32,2,64,128]{3,2,1,0:T(8,128)}, u32[]{:S(2)}) copy-start(f32[32,2,64,128]{3,2,1,0:T(8,128)} %state_ref.17) | copy-start | bytes 6291460
  3.8 3.1 %collective-permute-start = (bf16[18,16,128]{2,1,0:T(8,128)(2,1)S(1)}, bf16[18,16,128]{2,1,0:T(8,128)(2,1)S(1)}, u32[]{:S(2)}, u32[]{:S(2)}) collective-permute-start(bf16[18,16,128]{2,1,0:T(8,128)(2,1)S(1)} %get-tuple-element.27), channel_id=1, source_target_pairs={{0,1},{1,0},{2,3},{3,2},{4,5},{5,4},{6,7},{7,6},{8,9},{9,8},{10,11... | collective-permute-start | bytes 221192 | tf_op jit(solution)/shard_map/ppermute | solution.py:29
  4.4 5.2 %collective-permute-start.1 = (bf16[18,16,128]{2,1,0:T(8,128)(2,1)S(1)}, bf16[18,16,128]{2,1,0:T(8,128)(2,1)S(1)}, u32[]{:S(2)}, u32[]{:S(2)}) collective-permute-start(bf16[18,16,128]{2,1,0:T(8,128)(2,1)S(1)} %get-tuple-element.28), channel_id=1, source_target_pairs={{0,3},{1,2},{2,1},{3,0},{4,7},{5,6},{6,5},{7,4},{8,11},{9,10},{10,... | collective-permute-start | bytes 221192 | tf_op jit(solution)/shard_map/ppermute | solution.py:33
  9.6 8.2 %collective-permute-start.3 = (bf16[3,144,128]{2,1,0:T(8,128)(2,1)S(1)}, bf16[3,144,128]{2,1,0:T(8,128)(2,1)S(1)}, u32[]{:S(2)}, u32[]{:S(2)}) collective-permute-start(bf16[3,144,128]{2,1,0:T(8,128)(2,1)S(1)} %get-tuple-element.31.own_ref), channel_id=1, source_target_pairs={{0,28},{4,8},{8,4},{12,16},{16,12},{20,24},{24,20},{28,0},{1,29},{... | collective-permute-start | bytes 331784 | tf_op jit(solution)/shard_map/ppermute | solution.py:33
  14.2 6.0 %collective-permute-start.2 = (bf16[3,144,128]{2,1,0:T(8,128)(2,1)S(1)}, bf16[3,144,128]{2,1,0:T(8,128)(2,1)S(1)}, u32[]{:S(2)}, u32[]{:S(2)}) collective-permute-start(bf16[3,144,128]{2,1,0:T(8,128)(2,1)S(1)} %get-tuple-element.31.own_ref), channel_id=1, source_target_pairs={{0,4},{4,0},{8,12},{12,8},{16,20},{20,16},{24,28},{28,24},{1,5},{5... | collective-permute-start | bytes 331784 | tf_op jit(solution)/shard_map/ppermute | solution.py:29
  45.3 5.9 %collective-permute-start.4 = (bf16[512,128]{1,0:T(8,128)(2,1)S(1)}, bf16[512,128]{1,0:T(8,128)(2,1)S(1)}, u32[]{:S(2)}, u32[]{:S(2)}) collective-permute-start(bf16[512,128]{1,0:T(8,128)(2,1)S(1)} %bitcast.32), channel_id=1, source_target_pairs={{0,4},{4,0},{8,12},{12,8},{16,20},{20,16},{24,28},{28,24},{1,5},{5... | collective-permute-start | bytes 393224 | tf_op jit(solution)/shard_map/ppermute | solution.py:469
  45.3 8.5 %collective-permute-start.5 = (bf16[512,128]{1,0:T(8,128)(2,1)S(1)}, bf16[512,128]{1,0:T(8,128)(2,1)S(1)}, u32[]{:S(2)}, u32[]{:S(2)}) collective-permute-start(bf16[512,128]{1,0:T(8,128)(2,1)S(1)} %bitcast.31), channel_id=1, source_target_pairs={{0,8},{4,12},{8,0},{12,4},{16,24},{20,28},{24,16},{28,20},{1,9},{5... | collective-permute-start | bytes 393224 | tf_op jit(solution)/shard_map/ppermute | solution.py:469
  46.5 15.0 %collective-permute-start.6 = (bf16[512,128]{1,0:T(8,128)(2,1)}, bf16[512,128]{1,0:T(8,128)(2,1)}, u32[]{:S(2)}, u32[]{:S(2)}) collective-permute-start(bf16[512,128]{1,0:T(8,128)(2,1)} %bitcast.17), channel_id=1, source_target_pairs={{0,12},{4,8},{8,4},{12,0},{16,28},{20,24},{24,20},{28,16},{1,13},{... | collective-permute-start | bytes 393224 | tf_op jit(solution)/shard_map/ppermute | solution.py:469
  48.8 18.9 %collective-permute-start.7 = (bf16[512,128]{1,0:T(8,128)(2,1)}, bf16[512,128]{1,0:T(8,128)(2,1)}, u32[]{:S(2)}, u32[]{:S(2)}) collective-permute-start(bf16[512,128]{1,0:T(8,128)(2,1)} %bitcast.18), channel_id=1, source_target_pairs={{0,16},{4,20},{8,24},{12,28},{16,0},{20,4},{24,8},{28,12},{1,17},{... | collective-permute-start | bytes 393224 | tf_op jit(solution)/shard_map/ppermute | solution.py:469
  49.5 20.3 %collective-permute-start.8 = (bf16[512,128]{1,0:T(8,128)(2,1)}, bf16[512,128]{1,0:T(8,128)(2,1)}, u32[]{:S(2)}, u32[]{:S(2)}) collective-permute-start(bf16[512,128]{1,0:T(8,128)(2,1)} %bitcast.19), channel_id=1, source_target_pairs={{0,20},{4,16},{8,28},{12,24},{16,4},{20,0},{24,12},{28,8},{1,21},{... | collective-permute-start | bytes 393224 | tf_op jit(solution)/shard_map/ppermute | solution.py:469
  51.2 18.6 %collective-permute-start.9 = (bf16[512,128]{1,0:T(8,128)(2,1)}, bf16[512,128]{1,0:T(8,128)(2,1)}, u32[]{:S(2)}, u32[]{:S(2)}) collective-permute-start(bf16[512,128]{1,0:T(8,128)(2,1)} %bitcast.20), channel_id=1, source_target_pairs={{0,24},{4,28},{8,16},{12,20},{16,8},{20,12},{24,0},{28,4},{1,25},{... | collective-permute-start | bytes 393224 | tf_op jit(solution)/shard_map/ppermute | solution.py:469
  53.8 16.0 %collective-permute-start.10 = (bf16[512,128]{1,0:T(8,128)(2,1)}, bf16[512,128]{1,0:T(8,128)(2,1)}, u32[]{:S(2)}, u32[]{:S(2)}) collective-permute-start(bf16[512,128]{1,0:T(8,128)(2,1)} %bitcast.21), channel_id=1, source_target_pairs={{0,28},{4,24},{8,20},{12,16},{16,12},{20,8},{24,4},{28,0},{1,29},{... | collective-permute-start | bytes 393224 | tf_op jit(solution)/shard_map/ppermute | solution.py:469
  58.3 11.5 %copy-start.5 = (bf16[1024,128]{1,0:T(8,128)(2,1)S(1)}, bf16[1024,128]{1,0:T(8,128)(2,1)}, u32[]{:S(2)}) copy-start(bf16[1024,128]{1,0:T(8,128)(2,1)} %basis_ref.1) | copy-start | bytes 786436
  72.3 0.7 copy-start.3
  73.0 41.4 %copy-start.4 = (bf16[4,128,128]{2,1,0:T(8,128)(2,1)S(1)}, bf16[4,128,128]{2,1,0:T(8,128)(2,1)}, u32[]{:S(2)}) copy-start(bf16[4,128,128]{2,1,0:T(8,128)(2,1)} %copy-done.3) | copy-start | bytes 393220

commit v2 on v1

--- a/solution.py
+++ b/solution.py
@@ -1,3 +1,4 @@
+import functools
 import math
 
 import jax
@@ -10,7 +11,7 @@
 SECTIONS = 4
 NS_STEPS = 5
 HIGHEST = lax.Precision.HIGHEST
-VMEM_BYTES = 48 * 1024 * 1024
+VMEM_BYTES = 24 * 1024 * 1024
 BOTH = ("gx", "gy")
 LANES = 128
 WIDTH = SECTIONS
@@ -130,9 +131,7 @@
     edges_ref[species // per_group] = packed.astype(jnp.bfloat16)
 
 
-def advance(here, other, east, west, flow, diffusion, rate):
-    north = pltpu.roll(here, here.shape[0] - 1, 0)
-    south = pltpu.roll(here, 1, 0)
+def advance(here, other, north, south, east, west, flow, diffusion, rate):
     square = 1.0 + here * here
     inverse = pl.reciprocal(square, approx=True)
     inverse = inverse * (2.0 - square * inverse)
@@ -143,7 +142,9 @@
 
 
 def window_kernel(parity_ref, own_ref, near_ref, far_ref, spread_ref, rate_ref, border_ref):
-    sections, groups, heights, rows, _ = border_ref.shape
+    sections, groups, both, _ = border_ref.shape
+    heights = 2
+    rows = both // heights
     length = rows - 8
     even = parity_ref[0] == 0
     lane = iota((rows, LANES), 1)
@@ -189,8 +190,8 @@
         diffusion = spread_ref[group]
         rate = rate_ref[group]
         for section in range(sections):
-            for z in range(heights):
-                border_ref[section, group, z] = jnp.where(low, now[0][z], now[1][z])
+            border = [jnp.where(low, now[0][z], now[1][z]) for z in range(heights)]
+            border_ref[section, group] = jnp.concatenate(border, axis=0).astype(jnp.bfloat16)
             if section == sections - 1:
                 break
             now = [
@@ -198,6 +199,8 @@
                     advance(
                         now[side][z],
                         now[side][1 - z],
+                        pltpu.roll(now[side][z], rows - 1, 0),
+                        pltpu.roll(now[side][z], 1, 0),
                         pltpu.roll(now[side][z], LANES - 1, 1),
                         pltpu.roll(now[side][z], 1, 1),
                         flow[side][z],
@@ -211,53 +214,129 @@
 
 
 def section_kernel(
-    first_ref, state_ref, rows_ref, border_ref, half_ref, spread_ref, rate_ref, *rest
+    pieces, blocks_ref, state_ref, rows_ref, border_ref, half_ref, spread_ref, rate_ref, *rest
 ):
-    evolved_ref, piece_ref = rest[-2:]
-    _, heights, length, width = state_ref.shape
+    evolved_ref, piece_refs = rest[-5 - pieces], rest[-4 - pieces : -4]
+    land_ref, work_ref, side_ref, arrived = rest[-4:]
+    _, count, heights, length, width = land_ref.shape
+    rows = length + 8
     sections = border_ref.shape[0]
-    rows = length + 8
-    at = first_ref[0] + pl.program_id(0)
-    slot = lax.rem(at, LANES // WINDOW)
-    shift = LANES - WIDTH - WINDOW * slot
-    diffusion = spread_ref[at]
-    rate = rate_ref[at]
-    lane = iota((rows, width), 1)
-    now = [
-        jnp.concatenate([state_ref[0, z], rows_ref[0, pl.ds(8 * z, 8), :]], axis=0)
-        for z in range(heights)
-    ]
+    tiles = length // 8
+    lane = iota((8, width), 1)
+    step = pl.program_id(0)
+    now = lax.rem(step, 2)
+    first = blocks_ref[step] * count
+    diffusion = [spread_ref[first + at] for at in range(count)]
+    rate = [rate_ref[first + at] for at in range(count)]
+
+    def fetch(index, into):
+        return pltpu.make_async_copy(
+            state_ref.at[pl.ds(blocks_ref[index] * count, count)],
+            land_ref.at[into],
+            arrived.at[into],
+        )
+
+    @pl.when(step == 0)
+    def _():
+        fetch(0, 0).start()
+
+    @pl.when(step + 1 < pieces)
+    def _():
+        fetch(step + 1, 1 - now).start()
+
+    lane_from, lane_to = iota((LANES, LANES), 0), iota((LANES, LANES), 1)
+    for at in range(count):
+        base = WINDOW * lax.rem(first + at, LANES // WINDOW) + WIDTH
+        west = (lane_from == base - 1) & (lane_to == LANES - 1)
+        east = (lane_from == base) & (lane_to == 0)
+        chosen = (west | east).astype(jnp.float32).astype(jnp.bfloat16)
+        for section in range(sections):
+            side_ref[section, at] = jnp.dot(
+                border_ref[section, 0], chosen, preferred_element_type=jnp.float32
+            )
+
+    fetch(step, now).wait()
+    for at in range(count):
+        for z in range(heights):
+            tile = rows_ref[at, pl.ds(8 * z, 8), :]
+            work_ref[0, at, z, pl.ds(8, length), :] = land_ref[now, at, z]
+            work_ref[0, at, z, pl.ds(8 + length, 8), :] = tile
+            work_ref[0, at, z, pl.ds(0, 8), :] = tile
+            work_ref[0, at, z, pl.ds(16 + length, 8), :] = land_ref[now, at, z, pl.ds(0, 8), :]
+
     for section in range(sections):
-        later = []
-        for z in range(heights):
-            border = pltpu.roll(border_ref[section, 0, z], shift, 1)
-            if width > LANES:
-                border = jnp.concatenate([border] * (width // LANES), axis=1)
-            east = pltpu.roll(jnp.where(lane == 0, border, now[z]), width - 1, 1)
-            west = pltpu.roll(jnp.where(lane == width - 1, border, now[z]), 1, 1)
-            flow = [half_ref[slot_at, z] for slot_at in range(3)]
-            later.append(advance(now[z], now[1 - z], east, west, flow, diffusion, rate))
-        now = later
-    for z in range(heights):
-        evolved_ref[0, z] = now[z][:length]
-        piece_ref[0, pl.ds(z * length, length), :] = now[z][:length].astype(jnp.bfloat16)
-
-
-def image_kernel(place_ref, basis_ref, *rest):
+        source, target = section % 2, 1 - section % 2
+        final = section == sections - 1
+        for tile in range(tiles if final else tiles + 1):
+            start = 8 * tile
+            flow = [
+                [half_ref[part, z, pl.ds(start, 8), :] for part in range(3)]
+                for z in range(heights)
+            ]
+            for at in range(count):
+                here = [
+                    work_ref[source, at, z, pl.ds(8 + start, 8), :] for z in range(heights)
+                ]
+                for z in range(heights):
+                    border = side_ref[section, at, pl.ds(z * rows + start, 8), :]
+                    if width > LANES:
+                        border = jnp.concatenate([border] * (width // LANES), axis=1)
+                    new = advance(
+                        here[z],
+                        here[1 - z],
+                        work_ref[source, at, z, pl.ds(9 + start, 8), :],
+                        work_ref[source, at, z, pl.ds(7 + start, 8), :],
+                        pltpu.roll(jnp.where(lane == 0, border, here[z]), width - 1, 1),
+                        pltpu.roll(jnp.where(lane == width - 1, border, here[z]), 1, 1),
+                        flow[z],
+                        diffusion[at],
+                        rate[at],
+                    )
+                    if final:
+                        evolved_ref[at, z, pl.ds(start, 8), :] = new
+                    else:
+                        work_ref[target, at, z, pl.ds(8 + start, 8), :] = new
+        if not final:
+            for at in range(count):
+                for z in range(heights):
+                    work_ref[target, at, z, pl.ds(0, 8), :] = work_ref[
+                        target, at, z, pl.ds(8 + length, 8), :
+                    ]
+                    work_ref[target, at, z, pl.ds(16 + length, 8), :] = work_ref[
+                        target, at, z, pl.ds(8, 8), :
+                    ]
+    for piece, piece_ref in enumerate(piece_refs):
+
+        @pl.when(step == piece)
+        def _(piece_ref=piece_ref):
+            for at in range(count):
+                for z in range(heights):
+                    piece_ref[pl.ds((at * heights + z) * length, length), :] = evolved_ref[
+                        at, z
+                    ].astype(jnp.bfloat16)
+
+
+def project_kernel(place_ref, offsets, basis_ref, columns):
+    width = columns[0].shape[1]
+    project = jnp.zeros((columns[0].shape[0], basis_ref.shape[1]), jnp.float32)
+    for offset, column in zip(offsets, columns):
+        rows = pl.ds(pl.multiple_of((place_ref[0] ^ offset) * width, width), width)
+        project += jnp.dot(column[...], basis_ref[rows, :], preferred_element_type=jnp.float32)
+    return project
+
+
+def early_kernel(offsets, place_ref, basis_ref, *rest):
+    rest[-1][...] = project_kernel(place_ref, offsets, basis_ref, rest[:-1])
+
+
+def image_kernel(late, place_ref, basis_ref, early_ref, *rest):
     columns, image_ref = rest[:-1], rest[-1]
     width = columns[0].shape[1]
-
-    def rows_of(piece):
-        return pl.ds(pl.multiple_of((place_ref[0] ^ piece) * width, width), width)
-
-    project = jnp.zeros((columns[0].shape[0], basis_ref.shape[1]), jnp.float32)
-    for piece, column in enumerate(columns):
-        project += jnp.dot(
-            column[...], basis_ref[rows_of(piece), :], preferred_element_type=jnp.float32
-        )
+    project = early_ref[...] + project_kernel(place_ref, range(late), basis_ref, columns[:late])
     project = project.astype(jnp.bfloat16)
     for piece, column in enumerate(columns):
-        image_ref[rows_of(piece), :] = lax.dot_general(
+        rows = pl.ds(pl.multiple_of((place_ref[0] ^ piece) * width, width), width)
+        image_ref[rows, :] = lax.dot_general(
             column[...], project, (((0,), (0,)), ((), ())), preferred_element_type=jnp.float32
         ).astype(image_ref.dtype)
 
@@ -326,17 +405,25 @@
     owners = lax.axis_size(BOTH)
     rows_each = rows_all // owners
     place = jnp.stack([lax.axis_index("gx"), lax.axis_index(BOTH)]).astype(jnp.int32)
+    late = len(columns) // 2
+    early = call(
+        functools.partial(early_kernel, range(late, len(columns))),
+        jax.ShapeDtypeStruct((rows, rank), jnp.float32),
+        (place, start_basis, *columns[late:]),
+        in_specs=SCALARS + vmem(1 + len(columns) - late),
+        out_specs=vmem(1)[0],
+    )
     partial = call(
-        image_kernel,
-        jax.ShapeDtypeStruct((rows_all, rank), jnp.float32),
-        (place, start_basis, *columns),
-        in_specs=SCALARS + vmem(1 + len(columns)),
+        functools.partial(image_kernel, late),
+        jax.ShapeDtypeStruct((rows_all, rank), jnp.bfloat16),
+        (place, start_basis, early, *columns),
+        in_specs=SCALARS + vmem(2 + len(columns)),
         out_specs=vmem(1)[0],
     )
     shares = lax.all_to_all(
         partial.reshape(owners, rows_each, rank), BOTH, split_axis=0, concat_axis=0, tiled=True
     )
-    own_image = jnp.sum(shares, axis=0)
+    own_image = jnp.sum(shares.astype(jnp.float32), axis=0)
     image = lax.all_to_all(
         jnp.broadcast_to(own_image[None], (owners, rows_each, rank)),
         BOTH,
@@ -394,7 +481,9 @@
     lanes = [jnp.repeat(v, WINDOW).reshape(groups, 1, LANES) for v in (diffusivity, reaction_rate)]
     border = call(
         window_kernel,
-        jax.ShapeDtypeStruct((SECTIONS, groups, heights, length + 8, LANES), jnp.float32),
+        jax.ShapeDtypeStruct(
+            (SECTIONS, groups, heights * (length + 8), LANES), jnp.bfloat16
+        ),
         (parity, edges, near, far, *lanes),
         in_specs=SCALARS + vmem(5),
         out_specs=vmem(1)[0],
@@ -402,42 +491,47 @@
     return halo_rows, half, border
 
 
-def sections(first, count, evolved, initial_state, halo_rows, border, half, diffusivity, rate):
+def sections(blocks, evolved, initial_state, halo_rows, border, half, diffusivity, rate):
     species, heights, length, width = initial_state.shape
-    per_group = LANES // WINDOW
-    state_spec = pl.BlockSpec((1, heights, length, width), lambda i, f: (f[0] + i, 0, 0, 0))
+    pieces = blocks.shape[0]
+    count = species // lax.axis_size("gx")
+    per_group = LANES // (WINDOW * count)
+    state_spec = pl.BlockSpec((count, heights, length, width), lambda i, f: (f[i], 0, 0, 0))
     in_specs = [
-        state_spec,
-        pl.BlockSpec((1, 16, width), lambda i, f: (f[0] + i, 0, 0)),
+        pl.BlockSpec(memory_space=pltpu.HBM),
+        pl.BlockSpec((count, 16, width), lambda i, f: (f[i], 0, 0)),
         pl.BlockSpec(
-            (SECTIONS, 1, heights, length + 8, LANES),
-            lambda i, f: (0, (f[0] + i) // per_group, 0, 0, 0),
+            (SECTIONS, 1, heights * (length + 8), LANES),
+            lambda i, f: (0, f[i] // per_group, 0, 0),
         ),
         pl.BlockSpec(half.shape, lambda i, f: (0, 0, 0, 0)),
         pl.BlockSpec(memory_space=pltpu.SMEM),
         pl.BlockSpec(memory_space=pltpu.SMEM),
     ]
-    inputs = [first, initial_state, halo_rows, border, half, diffusivity, rate]
+    inputs = [blocks, initial_state, halo_rows, border, half, diffusivity, rate]
     aliases = {}
     if evolved is not None:
         in_specs.append(pl.BlockSpec(memory_space=pl.ANY))
         aliases[len(inputs)] = 0
         inputs.append(evolved)
+    rows = count * heights * length
+    piece = jax.ShapeDtypeStruct((rows, width), jnp.bfloat16)
     return call(
-        section_kernel,
-        (
-            jax.ShapeDtypeStruct(initial_state.shape, jnp.float32),
-            jax.ShapeDtypeStruct((count, heights * length, width), jnp.bfloat16),
-        ),
+        functools.partial(section_kernel, pieces),
+        (jax.ShapeDtypeStruct(initial_state.shape, jnp.float32),) + (piece,) * pieces,
         inputs,
         grid_spec=pltpu.PrefetchScalarGridSpec(
             num_scalar_prefetch=1,
-            grid=(count,),
+            grid=(pieces,),
             in_specs=in_specs,
-            out_specs=(
-                state_spec,
-                pl.BlockSpec((1, heights * length, width), lambda i, f: (i, 0, 0)),
-            ),
+            out_specs=(state_spec,)
+            + (pl.BlockSpec((rows, width), lambda i, f: (0, 0)),) * pieces,
+            scratch_shapes=[
+                pltpu.VMEM((2, count, heights, length, width), jnp.float32),
+                pltpu.VMEM((2, count, heights, length + 24, width), jnp.float32),
+                pltpu.VMEM((SECTIONS, count, heights * (length + 8), LANES), jnp.float32),
+                pltpu.SemaphoreType.DMA((2,)),
+            ],
         ),
         input_output_aliases=aliases,
     )
@@ -451,11 +545,10 @@
     halo_rows, half, border = borders(initial_state, velocity, diffusivity, reaction_rate)
     evolved = None
     columns = [None] * pieces
-    for offset in reversed(range(pieces)):
-        first = ((place ^ offset) * each).reshape(1)
-        evolved, piece = sections(
-            first,
-            each,
+    for offsets in (range(pieces // 2, pieces), range(pieces // 2)):
+        offsets = offsets[::-1]
+        evolved, *sent = sections(
+            jnp.stack([place ^ offset for offset in offsets]),
             evolved,
             initial_state,
             halo_rows,
@@ -464,10 +557,10 @@
             diffusivity,
             reaction_rate,
         )
-        piece = piece.reshape(each * heights * length, width)
-        if offset:
-            piece = lax.ppermute(piece, "gx", [(i, i ^ offset) for i in range(pieces)])
-        columns[offset] = piece
+        for offset, piece in zip(offsets, sent):
+            if offset:
+                piece = lax.ppermute(piece, "gx", [(i, i ^ offset) for i in range(pieces)])
+            columns[offset] = piece
     own_rows, core = subspace(columns, start_basis)
     return (evolved, own_rows, core.reshape(each, heights, length, start_basis.shape[1]))
 

time: 121 us -> 98.4 us (0.81)
  Pallas kernels: 37.7 us -> 27.7 us
  blocking collectives: 41.2 us -> 32.2 us
  starting transfers between devices: 20.6 us -> 19 us
    pallas_call x13 -> x8, Pallas kernels: 37.7 us -> 27.7 us  [call(): pl.pallas_call(kernel, out_shape=out_shape, compiler_params=pltpu.Compile...]
    all_to_all x1, blocking collectives: 22.8 us -> 14.5 us  [subspace(): lax.all_to_all(partial.reshape(owners, rows_each, rank), BOTH, split_axis...]
    ppermute x7, starting transfers between devices: 12.9 us -> 11.3 us  [shards(): piece = lax.ppermute(piece, 'gx', [(i, i ^ offset) for i in range(pieces)])]
    unnamed x16 -> x14, local copies, waits for them, and re-layouts: 3.18 us -> 2.53 us
  transfers between devices with their start and end apart: 11 -> 11, of which waited for: 5 -> 7; matrix products, arithmetic and copies ran while one was open for 0% -> 1% of each run, Pallas kernels for 3% -> 9%
where the time goes in v2:
time: 98.4 us; the launch traced here: 98.2 us
  blocking collectives  32.2 us (33%)
  Pallas kernels  27.7 us (28%)
  starting transfers between devices  19 us (19%)
  waiting for transfers between devices  15.2 us (15%)
  local copies, waits for them, and re-layouts  3.07 us (3%)
    pallas_call x8, Pallas kernels, call(): pl.pallas_call(kernel, out_shape=out_shape, compiler_params=pltpu.Compile...  27.7 us
    all_to_all x1, blocking collectives, subspace(): lax.all_to_all(jnp.broadcast_to(own_image[None], (owners, rows_each, rank...  17.8 us
    all_to_all x1, blocking collectives, subspace(): lax.all_to_all(partial.reshape(owners, rows_each, rank), BOTH, split_axis...  14.5 us
    ppermute x7, starting transfers between devices, shards(): piece = lax.ppermute(piece, 'gx', [(i, i ^ offset) for i in range(pieces)])  11.3 us
    ppermute x7, waiting for transfers between devices, shards(): piece = lax.ppermute(piece, 'gx', [(i, i ^ offset) for i in range(pieces)])  7.27 us
    ppermute x2, starting transfers between devices, swap_far(): return lax.ppermute(x, axis, far_pairs(lax.axis_size(axis)))  7.17 us
    ppermute x2, waiting for transfers between devices, swap_far(): return lax.ppermute(x, axis, far_pairs(lax.axis_size(axis)))  5.63 us
    unnamed x14, local copies, waits for them, and re-layouts  2.53 us
  transfers between devices with their start and end apart: 11, of which 7 were waited for; matrix products, arithmetic and copies ran while one was open for 1% of the time, Pallas kernels for 9%

profile of v2, /device:TPU:0, one launch (start us, length us, event | category | flops | bytes accessed | tf_op | source)
XLA Modules:
  0.0 98.2 jit_solution(7057619526389488154)
XLA Ops:
  0.7 1.6 %copy-done = f32[32,2,64,128]{3,2,1,0:T(8,128)S(1)} copy-done((f32[32,2,64,128]{3,2,1,0:T(8,128)S(1)}, f32[32,2,64,128]{3,2,1,0:T(8,128)}, u32[]{:S(2)}) %copy-start) | copy-done | bytes 2097176
  2.3 0.9 copy-done.3
  3.2 0.6 shard_map.76
  3.8 0.5 collective-permute-start
  4.4 2.6 %collective-permute-start.1 = (bf16[18,16,128]{2,1,0:T(8,128)(2,1)S(1)}, bf16[18,16,128]{2,1,0:T(8,128)(2,1)S(1)}, u32[]{:S(2)}, u32[]{:S(2)}) collective-permute-start(bf16[18,16,128]{2,1,0:T(8,128)(2,1)S(1)} %get-tuple-element.22), channel_id=1, source_target_pairs={{0,3},{1,2},{2,1},{3,0},{4,7},{5,6},{6,5},{7,4},{8,11},{9,10},{10,... | collective-permute-start | bytes 221192 | tf_op jit(solution)/shard_map/ppermute | solution.py:34
  7.0 0.1 broadcast_in_dim.20
  7.1 0.1 broadcast_in_dim.23
  7.2 0.1 broadcast_in_dim.25
  7.4 0.1 broadcast_in_dim.22
  7.5 2.0 %collective-permute-done.1.far_ref = bf16[18,16,128]{2,1,0:T(8,128)(2,1)S(1)} collective-permute-done((bf16[18,16,128]{2,1,0:T(8,128)(2,1)S(1)}, bf16[18,16,128]{2,1,0:T(8,128)(2,1)S(1)}, u32[]{:S(2)}, u32[]{:S(2)}) %collective-permute-start.1) | collective-permute-done | bytes 73760 | tf_op jit(solution)/shard_map/ppermute | solution.py:34
  9.5 0.1 shard_map.77
  9.7 4.6 %collective-permute-start.3 = (bf16[3,144,128]{2,1,0:T(8,128)(2,1)S(1)}, bf16[3,144,128]{2,1,0:T(8,128)(2,1)S(1)}, u32[]{:S(2)}, u32[]{:S(2)}) collective-permute-start(bf16[3,144,128]{2,1,0:T(8,128)(2,1)S(1)} %get-tuple-element.25.own_ref), channel_id=1, source_target_pairs={{0,28},{4,8},{8,4},{12,16},{16,12},{20,24},{24,20},{28,0},{1,29},{... | collective-permute-start | bytes 331784 | tf_op jit(solution)/shard_map/ppermute | solution.py:34
  14.3 3.6 %collective-permute-done.3.far_ref = bf16[3,144,128]{2,1,0:T(8,128)(2,1)S(1)} collective-permute-done((bf16[3,144,128]{2,1,0:T(8,128)(2,1)S(1)}, bf16[3,144,128]{2,1,0:T(8,128)(2,1)S(1)}, u32[]{:S(2)}, u32[]{:S(2)}) %collective-permute-start.3) | collective-permute-done | bytes 110624 | tf_op jit(solution)/shard_map/ppermute | solution.py:34
  17.9 2.3 %collective-permute-done.2.near_ref = bf16[3,144,128]{2,1,0:T(8,128)(2,1)S(1)} collective-permute-done((bf16[3,144,128]{2,1,0:T(8,128)(2,1)S(1)}, bf16[3,144,128]{2,1,0:T(8,128)(2,1)S(1)}, u32[]{:S(2)}, u32[]{:S(2)}) %collective-permute-start.2) | collective-permute-done | bytes 110624 | tf_op jit(solution)/shard_map/ppermute | solution.py:30
  20.2 2.3 %shard_map.78.border_ref = bf16[4,2,144,128]{3,2,1,0:T(8,128)(2,1)S(1)} custom-call(s32[1]{0:T(128)} %bitcast.5.parity_ref, bf16[3,144,128]{2,1,0:T(8,128)(2,1)S(1)} %get-tuple-element.25.own_ref, bf16[3,144,128]{2,1,0:T(8,128)(2,1)S(1)} %collective-permute-done.2.near_ref, bf16[3,144,128]{2,1,0:T(8,128)(2,1)S(1)} %collective-permute-done.3.far_ref, ...), custom_call_target="tpu_custom_call" | custom-call | tf_op jit(solution)/shard_map/pallas_call | solution.py:387
  22.5 8.4 %shard_map.79 = (f32[32,2,64,128]{3,2,1,0:T(8,128)}, bf16[512,128]{1,0:T(8,128)(2,1)}, bf16[512,128]{1,0:T(8,128)(2,1)}, bf16[512,128]{1,0:T(8,128)(2,1)}, bf16[512,128]{1,0:T(8,128)(2,1)}) custom-call(s32[4]{0:T(128)S(1)} %pad_add_fusion.1.blocks_ref, f32[32,2,64,128]{3,2,1,0:T(8,128)S(1)} %copy-done.1, f32[32,16,128]{2,1,0:T(8,128)S(1)} %get-tuple-element.24.rows_ref, ...), custom_call_target="tpu_custom_call" | custom-call | tf_op jit(solution)/shard_map/pallas_call | solution.py:387
  31.0 0.7 collective-permute-start.4
  31.7 1.3 %collective-permute-start.5 = (bf16[512,128]{1,0:T(8,128)(2,1)}, bf16[512,128]{1,0:T(8,128)(2,1)S(1)}, u32[]{:S(2)}, u32[]{:S(2)}) collective-permute-start(bf16[512,128]{1,0:T(8,128)(2,1)} %get-tuple-element.30), channel_id=1, source_target_pairs={{0,20},{4,16},{8,28},{12,24},{16,4},{20,0},{24,12},{28,8},{1,21},{... | collective-permute-start | bytes 393224 | tf_op jit(solution)/shard_map/ppermute | solution.py:562
  33.1 8.4 %shard_map.80 = (f32[32,2,64,128]{3,2,1,0:T(8,128)}, bf16[512,128]{1,0:T(8,128)(2,1)}, bf16[512,128]{1,0:T(8,128)(2,1)}, bf16[512,128]{1,0:T(8,128)(2,1)}, bf16[512,128]{1,0:T(8,128)(2,1)S(1)}) custom-call(s32[4]{0:T(128)S(1)} %pad_add_fusion.blocks_ref, f32[32,2,64,128]{3,2,1,0:T(8,128)S(1)} %copy-done.1, ...), custom_call_target="tpu_custom_call", output_to_operand_aliasing={{0}: (7, {})} | custom-call | tf_op jit(solution)/shard_map/pallas_call | solution.py:387
  41.5 2.5 %collective-permute-start.8 = (bf16[512,128]{1,0:T(8,128)(2,1)}, bf16[512,128]{1,0:T(8,128)(2,1)S(1)}, u32[]{:S(2)}, u32[]{:S(2)}) collective-permute-start(bf16[512,128]{1,0:T(8,128)(2,1)} %get-tuple-element.34), channel_id=1, source_target_pairs={{0,4},{4,0},{8,12},{12,8},{16,20},{20,16},{24,28},{28,24},{1,5},{5... | collective-permute-start | bytes 393224 | tf_op jit(solution)/shard_map/ppermute | solution.py:562
  44.0 1.7 %collective-permute-start.6 = (bf16[512,128]{1,0:T(8,128)(2,1)}, bf16[512,128]{1,0:T(8,128)(2,1)S(1)}, u32[]{:S(2)}, u32[]{:S(2)}) collective-permute-start(bf16[512,128]{1,0:T(8,128)(2,1)} %get-tuple-element.31), channel_id=1, source_target_pairs={{0,24},{4,28},{8,16},{12,20},{16,8},{20,12},{24,0},{28,4},{1,25},{... | collective-permute-start | bytes 393224 | tf_op jit(solution)/shard_map/ppermute | solution.py:562
  45.6 1.7 %collective-permute-start.7 = (bf16[512,128]{1,0:T(8,128)(2,1)}, bf16[512,128]{1,0:T(8,128)(2,1)S(1)}, u32[]{:S(2)}, u32[]{:S(2)}) collective-permute-start(bf16[512,128]{1,0:T(8,128)(2,1)} %get-tuple-element.32), channel_id=1, source_target_pairs={{0,28},{4,24},{8,20},{12,16},{16,12},{20,8},{24,4},{28,0},{1,29},{... | collective-permute-start | bytes 393224 | tf_op jit(solution)/shard_map/ppermute | solution.py:562
  47.3 3.4 %collective-permute-start.10 = (bf16[512,128]{1,0:T(8,128)(2,1)}, bf16[512,128]{1,0:T(8,128)(2,1)S(1)}, u32[]{:S(2)}, u32[]{:S(2)}) collective-permute-start(bf16[512,128]{1,0:T(8,128)(2,1)} %get-tuple-element.36), channel_id=1, source_target_pairs={{0,12},{4,8},{8,4},{12,0},{16,28},{20,24},{24,20},{28,16},{1,13},{... | collective-permute-start | bytes 393224 | tf_op jit(solution)/shard_map/ppermute | solution.py:562
  50.8 1.6 %collective-permute-done.6.rest_2_.rest_6_ = bf16[512,128]{1,0:T(8,128)(2,1)S(1)} collective-permute-done((bf16[512,128]{1,0:T(8,128)(2,1)}, bf16[512,128]{1,0:T(8,128)(2,1)S(1)}, u32[]{:S(2)}, u32[]{:S(2)}) %collective-permute-start.6) | collective-permute-done | bytes 131104 | tf_op jit(solution)/shard_map/ppermute | solution.py:562
  52.4 2.6 %collective-permute-done.7.rest_3_.rest_7_ = bf16[512,128]{1,0:T(8,128)(2,1)S(1)} collective-permute-done((bf16[512,128]{1,0:T(8,128)(2,1)}, bf16[512,128]{1,0:T(8,128)(2,1)S(1)}, u32[]{:S(2)}, u32[]{:S(2)}) %collective-permute-start.7) | collective-permute-done | bytes 131104 | tf_op jit(solution)/shard_map/ppermute | solution.py:562
  55.0 0.8 shard_map.81.early_ref
  55.8 0.6 collective-permute-done.9.rest_2_
  56.4 2.5 %collective-permute-done.10.rest_3_ = bf16[512,128]{1,0:T(8,128)(2,1)S(1)} collective-permute-done((bf16[512,128]{1,0:T(8,128)(2,1)}, bf16[512,128]{1,0:T(8,128)(2,1)S(1)}, u32[]{:S(2)}, u32[]{:S(2)}) %collective-permute-start.10) | collective-permute-done | bytes 131104 | tf_op jit(solution)/shard_map/ppermute | solution.py:562
  58.9 1.5 %shard_map.82 = bf16[1024,128]{1,0:T(8,128)(2,1)S(1)} custom-call(s32[2]{0:T(128)S(1)} %pad_add_fusion.2.place_ref, bf16[1024,128]{1,0:T(8,128)(2,1)S(1)} %copy-done.2, f32[512,128]{1,0:T(8,128)S(1)} %shard_map.81.early_ref, bf16[512,128]{1,0:T(8,128)(2,1)S(1)} %get-tuple-element.33.rest_0_, bf16[512,128]{1,0:T(8,128)(2,1)S(1)} %collective-permute-done.8.rest_1_, ...), custom_call_target="tpu_custom_call" | custom-call | tf_op jit(solution)/shard_map/pallas_call | solution.py:387
  60.4 14.5 %all_to_all.10 = bf16[32,32,128]{2,1,0:T(8,128)(2,1)S(1)} all-to-all(bf16[32,32,128]{2,1,0:T(8,128)(2,1)S(1)} %bitcast.17), channel_id=1, replica_groups=mesh['gx'=8,'gy'=4] {'gx','gy'}, dimensions={0} | all-to-all | bytes 524288 | tf_op jit(solution)/shard_map/all_to_all | solution.py:423
  75.0 17.8 %all_to_all.11 = f32[32,32,128]{2,1,0:T(8,128)S(1)} all-to-all(f32[32,32,128]{2,1,0:T(8,128)S(1)} %broadcast_in_dim.26), channel_id=1, replica_groups=mesh['gx'=8,'gy'=4] {'gx','gy'}, dimensions={0} | all-to-all | bytes 1048576 | tf_op jit(solution)/shard_map/all_to_all | solution.py:427
  92.7 5.5 %shard_map.83 = (bf16[32,128]{1,0:T(8,128)(2,1)}, f32[512,128]{1,0:T(8,128)}) custom-call(s32[2]{0:T(128)S(1)} %pad_add_fusion.2.place_ref, f32[1024,128]{1,0:T(8,128)S(1)} %bitcast.16, bf16[512,128]{1,0:T(8,128)(2,1)S(1)} %get-tuple-element.33.rest_0_, bf16[512,128]{1,0:T(8,128)(2,1)S(1)} %collective-permute-done.8.rest_1_, ...), custom_call_target="tpu_custom_call" | custom-call | tf_op jit(solution)/shard_map/pallas_call | solution.py:387
  (25 shorter events, 0.5 us)
Async XLA Ops:
  0.6 6.3 %copy-start.5 = (f32[32]{0:T(128)S(1)}, f32[32]{0:T(128)}, u32[]{:S(2)}) copy-start(f32[32]{0:T(128)} %spread_ref.3) | copy-start | bytes 388
  0.6 6.4 %copy-start.6 = (f32[32]{0:T(128)S(1)}, f32[32]{0:T(128)}, u32[]{:S(2)}) copy-start(f32[32]{0:T(128)} %rate_ref.3) | copy-start | bytes 388
  0.7 1.6 %copy-start = (f32[32,2,64,128]{3,2,1,0:T(8,128)S(1)}, f32[32,2,64,128]{3,2,1,0:T(8,128)}, u32[]{:S(2)}) copy-start(f32[32,2,64,128]{3,2,1,0:T(8,128)} %state_ref.5) | copy-start | bytes 6291460
  2.3 0.9 copy-start.3
  3.2 6.3 %copy-start.4 = (f32[3,2,64,128]{3,2,1,0:T(8,128)S(1)}, f32[3,2,64,128]{3,2,1,0:T(8,128)}, u32[]{:S(2)}) copy-start(f32[3,2,64,128]{3,2,1,0:T(8,128)} %velocity_ref.3) | copy-start | bytes 589828
  3.2 19.3 %copy-start.1 = (f32[32,2,64,128]{3,2,1,0:T(8,128)S(1)}, f32[32,2,64,128]{3,2,1,0:T(8,128)}, u32[]{:S(2)}) copy-start(f32[32,2,64,128]{3,2,1,0:T(8,128)} %state_ref.5) | copy-start | bytes 6291460
  3.8 3.6 %collective-permute-start = (bf16[18,16,128]{2,1,0:T(8,128)(2,1)S(1)}, bf16[18,16,128]{2,1,0:T(8,128)(2,1)S(1)}, u32[]{:S(2)}, u32[]{:S(2)}) collective-permute-start(bf16[18,16,128]{2,1,0:T(8,128)(2,1)S(1)} %get-tuple-element.21), channel_id=1, source_target_pairs={{0,1},{1,0},{2,3},{3,2},{4,5},{5,4},{6,7},{7,6},{8,9},{9,8},{10,11... | collective-permute-start | bytes 221192 | tf_op jit(solution)/shard_map/ppermute | solution.py:30
  4.4 5.2 %collective-permute-start.1 = (bf16[18,16,128]{2,1,0:T(8,128)(2,1)S(1)}, bf16[18,16,128]{2,1,0:T(8,128)(2,1)S(1)}, u32[]{:S(2)}, u32[]{:S(2)}) collective-permute-start(bf16[18,16,128]{2,1,0:T(8,128)(2,1)S(1)} %get-tuple-element.22), channel_id=1, source_target_pairs={{0,3},{1,2},{2,1},{3,0},{4,7},{5,6},{6,5},{7,4},{8,11},{9,10},{10,... | collective-permute-start | bytes 221192 | tf_op jit(solution)/shard_map/ppermute | solution.py:34
  9.7 8.2 %collective-permute-start.3 = (bf16[3,144,128]{2,1,0:T(8,128)(2,1)S(1)}, bf16[3,144,128]{2,1,0:T(8,128)(2,1)S(1)}, u32[]{:S(2)}, u32[]{:S(2)}) collective-permute-start(bf16[3,144,128]{2,1,0:T(8,128)(2,1)S(1)} %get-tuple-element.25.own_ref), channel_id=1, source_target_pairs={{0,28},{4,8},{8,4},{12,16},{16,12},{20,24},{24,20},{28,0},{1,29},{... | collective-permute-start | bytes 331784 | tf_op jit(solution)/shard_map/ppermute | solution.py:34
  14.2 6.0 %collective-permute-start.2 = (bf16[3,144,128]{2,1,0:T(8,128)(2,1)S(1)}, bf16[3,144,128]{2,1,0:T(8,128)(2,1)S(1)}, u32[]{:S(2)}, u32[]{:S(2)}) collective-permute-start(bf16[3,144,128]{2,1,0:T(8,128)(2,1)S(1)} %get-tuple-element.25.own_ref), channel_id=1, source_target_pairs={{0,4},{4,0},{8,12},{12,8},{16,20},{20,16},{24,28},{28,24},{1,5},{5... | collective-permute-start | bytes 331784 | tf_op jit(solution)/shard_map/ppermute | solution.py:30
  31.0 16.3 %collective-permute-start.4 = (bf16[512,128]{1,0:T(8,128)(2,1)}, bf16[512,128]{1,0:T(8,128)(2,1)S(1)}, u32[]{:S(2)}, u32[]{:S(2)}) collective-permute-start(bf16[512,128]{1,0:T(8,128)(2,1)} %get-tuple-element.29), channel_id=1, source_target_pairs={{0,16},{4,20},{8,24},{12,28},{16,0},{20,4},{24,8},{28,12},{1,17},{... | collective-permute-start | bytes 393224 | tf_op jit(solution)/shard_map/ppermute | solution.py:562
  31.7 15.6 %collective-permute-start.5 = (bf16[512,128]{1,0:T(8,128)(2,1)}, bf16[512,128]{1,0:T(8,128)(2,1)S(1)}, u32[]{:S(2)}, u32[]{:S(2)}) collective-permute-start(bf16[512,128]{1,0:T(8,128)(2,1)} %get-tuple-element.30), channel_id=1, source_target_pairs={{0,20},{4,16},{8,28},{12,24},{16,4},{20,0},{24,12},{28,8},{1,21},{... | collective-permute-start | bytes 393224 | tf_op jit(solution)/shard_map/ppermute | solution.py:562
  33.1 21.9 %copy-start.2 = (bf16[1024,128]{1,0:T(8,128)(2,1)S(1)}, bf16[1024,128]{1,0:T(8,128)(2,1)}, u32[]{:S(2)}) copy-start(bf16[1024,128]{1,0:T(8,128)(2,1)} %basis_ref.3) | copy-start | bytes 786436
  41.5 14.4 %collective-permute-start.8 = (bf16[512,128]{1,0:T(8,128)(2,1)}, bf16[512,128]{1,0:T(8,128)(2,1)S(1)}, u32[]{:S(2)}, u32[]{:S(2)}) collective-permute-start(bf16[512,128]{1,0:T(8,128)(2,1)} %get-tuple-element.34), channel_id=1, source_target_pairs={{0,4},{4,0},{8,12},{12,8},{16,20},{20,16},{24,28},{28,24},{1,5},{5... | collective-permute-start | bytes 393224 | tf_op jit(solution)/shard_map/ppermute | solution.py:562
  44.0 8.5 %collective-permute-start.6 = (bf16[512,128]{1,0:T(8,128)(2,1)}, bf16[512,128]{1,0:T(8,128)(2,1)S(1)}, u32[]{:S(2)}, u32[]{:S(2)}) collective-permute-start(bf16[512,128]{1,0:T(8,128)(2,1)} %get-tuple-element.31), channel_id=1, source_target_pairs={{0,24},{4,28},{8,16},{12,20},{16,8},{20,12},{24,0},{28,4},{1,25},{... | collective-permute-start | bytes 393224 | tf_op jit(solution)/shard_map/ppermute | solution.py:562
  45.6 9.3 %collective-permute-start.7 = (bf16[512,128]{1,0:T(8,128)(2,1)}, bf16[512,128]{1,0:T(8,128)(2,1)S(1)}, u32[]{:S(2)}, u32[]{:S(2)}) collective-permute-start(bf16[512,128]{1,0:T(8,128)(2,1)} %get-tuple-element.32), channel_id=1, source_target_pairs={{0,28},{4,24},{8,20},{12,16},{16,12},{20,8},{24,4},{28,0},{1,29},{... | collective-permute-start | bytes 393224 | tf_op jit(solution)/shard_map/ppermute | solution.py:562
  47.3 9.1 %collective-permute-start.9 = (bf16[512,128]{1,0:T(8,128)(2,1)}, bf16[512,128]{1,0:T(8,128)(2,1)S(1)}, u32[]{:S(2)}, u32[]{:S(2)}) collective-permute-start(bf16[512,128]{1,0:T(8,128)(2,1)} %get-tuple-element.35), channel_id=1, source_target_pairs={{0,8},{4,12},{8,0},{12,4},{16,24},{20,28},{24,16},{28,20},{1,9},{5... | collective-permute-start | bytes 393224 | tf_op jit(solution)/shard_map/ppermute | solution.py:562
  47.3 11.6 %collective-permute-start.10 = (bf16[512,128]{1,0:T(8,128)(2,1)}, bf16[512,128]{1,0:T(8,128)(2,1)S(1)}, u32[]{:S(2)}, u32[]{:S(2)}) collective-permute-start(bf16[512,128]{1,0:T(8,128)(2,1)} %get-tuple-element.36), channel_id=1, source_target_pairs={{0,12},{4,8},{8,4},{12,0},{16,28},{20,24},{24,20},{28,16},{1,13},{... | collective-permute-start | bytes 393224 | tf_op jit(solution)/shard_map/ppermute | solution.py:562

commit v3 on v2

--- a/solution.py
+++ b/solution.py
@@ -12,6 +12,7 @@
 NS_STEPS = 5
 HIGHEST = lax.Precision.HIGHEST
 VMEM_BYTES = 24 * 1024 * 1024
+FULL_VMEM_BYTES = 60 * 1024 * 1024
 BOTH = ("gx", "gy")
 LANES = 128
 WIDTH = SECTIONS
@@ -50,15 +51,28 @@
     return jnp.where(lane // WINDOW == slot, rolled, packed)
 
 
-def pack_kernel(parity_ref, state_ref, velocity_ref, near_ref, far_ref, edges_ref):
-    species, heights, length, width = state_ref.shape
+def rows_kernel(parity_ref, state_ref, velocity_ref, near_ref, far_ref, first_ref, last_ref, arrived):
+    species, _, length, width = state_ref.shape
     components = velocity_ref.shape[0]
     even = parity_ref[0] == 0
     sub = iota((8, width), 0)
-
-    def edge_rows(ref, at):
-        first = [ref[at, z, pl.ds(0, 8), :] for z in range(2)]
-        last = [ref[at, z, pl.ds(length - 8, 8), :] for z in range(2)]
+    copies = []
+    for ref, start, count in ((state_ref, 0, species), (velocity_ref, species, components)):
+        for side, land_ref in enumerate((first_ref, last_ref)):
+            copies.append(
+                pltpu.make_async_copy(
+                    ref.at[:, :, pl.ds(side * (length - 8), 8), :],
+                    land_ref.at[pl.ds(start, count)],
+                    arrived.at[len(copies)],
+                )
+            )
+            copies[-1].start()
+    for copy in copies:
+        copy.wait()
+
+    def edge_rows(at):
+        first = [first_ref[at, z] for z in range(2)]
+        last = [last_ref[at, z] for z in range(2)]
         first = jnp.where(sub < WIDTH, first[0], pltpu.roll(first[1], WIDTH, 0))
         last = jnp.where(sub < WIDTH, pltpu.roll(last[0], WIDTH, 0), last[1])
         return jnp.where(even, last, first), jnp.where(even, first, last)
@@ -67,15 +81,16 @@
         near_ref[pair] = jnp.concatenate([one[0], two[0]], axis=0).astype(jnp.bfloat16)
         far_ref[pair] = jnp.concatenate([one[1], two[1]], axis=0).astype(jnp.bfloat16)
 
-    def pair_body(pair, carry):
-        put(pair, edge_rows(state_ref, 2 * pair), edge_rows(state_ref, 2 * pair + 1))
-        return carry
-
-    lax.fori_loop(0, species // 2, pair_body, 0, unroll=2)
-    flows = [edge_rows(velocity_ref, at) for at in range(components)]
+    for pair in range(species // 2):
+        put(pair, edge_rows(2 * pair), edge_rows(2 * pair + 1))
+    flows = [edge_rows(species + at) for at in range(components)]
     put(species // 2, flows[0], flows[1])
     put(species // 2 + 1, flows[2], flows[2])
 
+
+def edges_kernel(state_ref, velocity_ref, edges_ref):
+    species, heights, length, _ = state_ref.shape
+    components = velocity_ref.shape[0]
     per_group = LANES // WINDOW
 
     def rows_body(at, carry):
@@ -142,8 +157,9 @@
 
 
 def window_kernel(parity_ref, own_ref, near_ref, far_ref, spread_ref, rate_ref, border_ref):
-    sections, groups, both, _ = border_ref.shape
-    heights = 2
+    groups, total, _ = border_ref.shape
+    heights, sections = 2, SECTIONS
+    both = total // sections
     rows = both // heights
     length = rows - 8
     even = parity_ref[0] == 0
@@ -191,7 +207,9 @@
         rate = rate_ref[group]
         for section in range(sections):
             border = [jnp.where(low, now[0][z], now[1][z]) for z in range(heights)]
-            border_ref[section, group] = jnp.concatenate(border, axis=0).astype(jnp.bfloat16)
+            border_ref[group, pl.ds(section * both, both), :] = jnp.concatenate(
+                border, axis=0
+            ).astype(jnp.bfloat16)
             if section == sections - 1:
                 break
             now = [
@@ -220,7 +238,7 @@
     land_ref, work_ref, side_ref, arrived = rest[-4:]
     _, count, heights, length, width = land_ref.shape
     rows = length + 8
-    sections = border_ref.shape[0]
+    sections = SECTIONS
     tiles = length // 8
     lane = iota((8, width), 1)
     step = pl.program_id(0)
@@ -250,10 +268,7 @@
         west = (lane_from == base - 1) & (lane_to == LANES - 1)
         east = (lane_from == base) & (lane_to == 0)
         chosen = (west | east).astype(jnp.float32).astype(jnp.bfloat16)
-        for section in range(sections):
-            side_ref[section, at] = jnp.dot(
-                border_ref[section, 0], chosen, preferred_element_type=jnp.float32
-            )
+        side_ref[at] = jnp.dot(border_ref[0], chosen, preferred_element_type=jnp.float32)
 
     fetch(step, now).wait()
     for at in range(count):
@@ -278,7 +293,7 @@
                     work_ref[source, at, z, pl.ds(8 + start, 8), :] for z in range(heights)
                 ]
                 for z in range(heights):
-                    border = side_ref[section, at, pl.ds(z * rows + start, 8), :]
+                    border = side_ref[at, pl.ds((section * heights + z) * rows + start, 8), :]
                     if width > LANES:
                         border = jnp.concatenate([border] * (width // LANES), axis=1)
                     new = advance(
@@ -383,11 +398,11 @@
     core_ref[...] = core / math.sqrt(rows_all)
 
 
-def call(kernel, out_shape, inputs, **rest):
+def call(kernel, out_shape, inputs, vmem_bytes=VMEM_BYTES, **rest):
     return pl.pallas_call(
         kernel,
         out_shape=out_shape,
-        compiler_params=pltpu.CompilerParams(vmem_limit_bytes=VMEM_BYTES),
+        compiler_params=pltpu.CompilerParams(vmem_limit_bytes=vmem_bytes),
         **rest,
     )(*inputs)
 
@@ -450,12 +465,23 @@
     parity = (lax.axis_index("gy") % 2).astype(jnp.int32).reshape(1)
     edge = jax.ShapeDtypeStruct((species // 2 + 2, 16, width), jnp.bfloat16)
     window = jax.ShapeDtypeStruct((groups + 1, heights * (length + 8), LANES), jnp.bfloat16)
-    near, far, edges = call(
-        pack_kernel,
-        (edge, edge, window),
+    fields = species + velocity.shape[0]
+    land = pltpu.VMEM((fields, heights, 8, width), jnp.float32)
+    near, far = call(
+        rows_kernel,
+        (edge, edge),
         (parity, initial_state, velocity),
-        in_specs=SCALARS + vmem(2),
-        out_specs=tuple(vmem(3)),
+        in_specs=SCALARS + [pl.BlockSpec(memory_space=pltpu.HBM)] * 2,
+        out_specs=tuple(vmem(2)),
+        scratch_shapes=[land, land, pltpu.SemaphoreType.DMA((4,))],
+        vmem_bytes=FULL_VMEM_BYTES,
+    )
+    edges = call(
+        edges_kernel,
+        window,
+        (initial_state, velocity),
+        in_specs=vmem(2),
+        out_specs=vmem(1)[0],
     )
     near = swap_near(near, "gy")
     far = swap_far(far, "gy")
@@ -482,7 +508,7 @@
     border = call(
         window_kernel,
         jax.ShapeDtypeStruct(
-            (SECTIONS, groups, heights * (length + 8), LANES), jnp.bfloat16
+            (groups, SECTIONS * heights * (length + 8), LANES), jnp.bfloat16
         ),
         (parity, edges, near, far, *lanes),
         in_specs=SCALARS + vmem(5),
@@ -501,8 +527,8 @@
         pl.BlockSpec(memory_space=pltpu.HBM),
         pl.BlockSpec((count, 16, width), lambda i, f: (f[i], 0, 0)),
         pl.BlockSpec(
-            (SECTIONS, 1, heights * (length + 8), LANES),
-            lambda i, f: (0, f[i] // per_group, 0, 0),
+            (1, SECTIONS * heights * (length + 8), LANES),
+            lambda i, f: (f[i] // per_group, 0, 0),
         ),
         pl.BlockSpec(half.shape, lambda i, f: (0, 0, 0, 0)),
         pl.BlockSpec(memory_space=pltpu.SMEM),
@@ -529,7 +555,7 @@
             scratch_shapes=[
                 pltpu.VMEM((2, count, heights, length, width), jnp.float32),
                 pltpu.VMEM((2, count, heights, length + 24, width), jnp.float32),
-                pltpu.VMEM((SECTIONS, count, heights * (length + 8), LANES), jnp.float32),
+                pltpu.VMEM((count, SECTIONS * heights * (length + 8), LANES), jnp.float32),
                 pltpu.SemaphoreType.DMA((2,)),
             ],
         ),
@@ -545,8 +571,12 @@
     halo_rows, half, border = borders(initial_state, velocity, diffusivity, reaction_rate)
     evolved = None
     columns = [None] * pieces
-    for offsets in (range(pieces // 2, pieces), range(pieces // 2)):
-        offsets = offsets[::-1]
+    half_way, quarter = pieces // 2, pieces // 4
+    for offsets in (
+        [*range(half_way, half_way + quarter)],
+        [*range(half_way + quarter, pieces), *range(1, half_way)],
+        [0],
+    ):
         evolved, *sent = sections(
             jnp.stack([place ^ offset for offset in offsets]),
             evolved,

time: 98.4 us -> 95 us (0.965)
  waiting for transfers between devices: 15.2 us -> 12.2 us
  Pallas kernels: 27.7 us -> 30.4 us
  local copies, waits for them, and re-layouts: 3.07 us -> 0.64 us
    pallas_call x8 -> x10, Pallas kernels: 27.7 us -> 30.4 us  [call(): pl.pallas_call(kernel, out_shape=out_shape, compiler_params=pltpu.Compile...]
    ppermute x7, waiting for transfers between devices: 7.27 us -> 4.61 us  [shards(): piece = lax.ppermute(piece, 'gx', [(i, i ^ offset) for i in range(pieces)])]
    unnamed x14 -> x10, local copies, waits for them, and re-layouts: 2.53 us -> 0.02 us
  transfers between devices with their start and end apart: 11 -> 11, of which waited for: 7 -> 5; matrix products, arithmetic and copies ran while one was open for 1% -> 1% of each run, Pallas kernels for 9% -> 14%
where the time goes in v3:
time: 95 us; the launch traced here: 94.7 us
  blocking collectives  31.6 us (33%)
  Pallas kernels  30.4 us (32%)
  starting transfers between devices  18.9 us (20%)
  waiting for transfers between devices  12.2 us (13%)
    pallas_call x10, Pallas kernels, call(): pl.pallas_call(kernel, out_shape=out_shape, compiler_params=pltpu.Compile...  30.4 us
    all_to_all x1, blocking collectives, subspace(): lax.all_to_all(jnp.broadcast_to(own_image[None], (owners, rows_each, rank...  17.8 us
    all_to_all x1, blocking collectives, subspace(): lax.all_to_all(partial.reshape(owners, rows_each, rank), BOTH, split_axis...  13.8 us
    ppermute x7, starting transfers between devices, shards(): piece = lax.ppermute(piece, 'gx', [(i, i ^ offset) for i in range(pieces)])  11.3 us
    ppermute x2, starting transfers between devices, swap_far(): return lax.ppermute(x, axis, far_pairs(lax.axis_size(axis)))  7.14 us
    ppermute x2, waiting for transfers between devices, swap_far(): return lax.ppermute(x, axis, far_pairs(lax.axis_size(axis)))  5.28 us
    ppermute x7, waiting for transfers between devices, shards(): piece = lax.ppermute(piece, 'gx', [(i, i ^ offset) for i in range(pieces)])  4.61 us
    ppermute x2, waiting for transfers between devices, swap_near(): return lax.ppermute(x, axis, near_pairs(lax.axis_size(axis)))  2.28 us
  transfers between devices with their start and end apart: 11, of which 5 were waited for; matrix products, arithmetic and copies ran while one was open for 1% of the time, Pallas kernels for 14%

profile of v3, /device:TPU:0, one launch (start us, length us, event | category | flops | bytes accessed | tf_op | source)
XLA Modules:
  0.0 94.7 jit_solution(1515753586387837115)
XLA Ops:
  0.7 1.9 %shard_map.76 = (bf16[18,16,128]{2,1,0:T(8,128)(2,1)}, bf16[18,16,128]{2,1,0:T(8,128)(2,1)}) custom-call(s32[1]{0:T(128)} %bitcast.1.parity_ref, f32[32,2,64,128]{3,2,1,0:T(8,128)} %state_ref.9, f32[3,2,64,128]{3,2,1,0:T(8,128)} %velocity_ref.5), custom_call_target="tpu_custom_call" | custom-call | tf_op jit(solution)/shard_map/pallas_call | solution.py:402
  2.6 0.5 collective-permute-start
  3.1 2.6 %collective-permute-start.1 = (bf16[18,16,128]{2,1,0:T(8,128)(2,1)}, bf16[18,16,128]{2,1,0:T(8,128)(2,1)S(1)}, u32[]{:S(2)}, u32[]{:S(2)}) collective-permute-start(bf16[18,16,128]{2,1,0:T(8,128)(2,1)} %get-tuple-element.22), channel_id=1, source_target_pairs={{0,3},{1,2},{2,1},{3,0},{4,7},{5,6},{6,5},{7,4},{8,11},{9,10},{10,... | collective-permute-start | bytes 221192 | tf_op jit(solution)/shard_map/ppermute | solution.py:35
  5.7 0.6 shard_map.77.old_ref
  6.3 0.1 broadcast_in_dim.20
  6.4 0.1 broadcast_in_dim.23
  6.6 0.1 broadcast_in_dim.25
  6.7 0.1 broadcast_in_dim.22
  6.8 1.6 %collective-permute-done.1.far_ref = bf16[18,16,128]{2,1,0:T(8,128)(2,1)S(1)} collective-permute-done((bf16[18,16,128]{2,1,0:T(8,128)(2,1)}, bf16[18,16,128]{2,1,0:T(8,128)(2,1)S(1)}, u32[]{:S(2)}, u32[]{:S(2)}) %collective-permute-start.1) | collective-permute-done | bytes 73760 | tf_op jit(solution)/shard_map/ppermute | solution.py:35
  8.5 0.1 shard_map.78
  8.6 4.5 %collective-permute-start.3 = (bf16[3,144,128]{2,1,0:T(8,128)(2,1)S(1)}, bf16[3,144,128]{2,1,0:T(8,128)(2,1)S(1)}, u32[]{:S(2)}, u32[]{:S(2)}) collective-permute-start(bf16[3,144,128]{2,1,0:T(8,128)(2,1)S(1)} %get-tuple-element.24.own_ref), channel_id=1, source_target_pairs={{0,28},{4,8},{8,4},{12,16},{16,12},{20,24},{24,20},{28,0},{1,29},{... | collective-permute-start | bytes 331784 | tf_op jit(solution)/shard_map/ppermute | solution.py:35
  13.1 0.1 pad_add_fusion.blocks_ref
  13.2 3.6 %collective-permute-done.3.far_ref = bf16[3,144,128]{2,1,0:T(8,128)(2,1)S(1)} collective-permute-done((bf16[3,144,128]{2,1,0:T(8,128)(2,1)S(1)}, bf16[3,144,128]{2,1,0:T(8,128)(2,1)S(1)}, u32[]{:S(2)}, u32[]{:S(2)}) %collective-permute-start.3) | collective-permute-done | bytes 110624 | tf_op jit(solution)/shard_map/ppermute | solution.py:35
  16.9 2.3 %collective-permute-done.2.near_ref = bf16[3,144,128]{2,1,0:T(8,128)(2,1)S(1)} collective-permute-done((bf16[3,144,128]{2,1,0:T(8,128)(2,1)S(1)}, bf16[3,144,128]{2,1,0:T(8,128)(2,1)S(1)}, u32[]{:S(2)}, u32[]{:S(2)}) %collective-permute-start.2) | collective-permute-done | bytes 110624 | tf_op jit(solution)/shard_map/ppermute | solution.py:31
  19.1 2.3 %shard_map.79.border_ref = bf16[2,576,128]{2,1,0:T(8,128)(2,1)S(1)} custom-call(s32[1]{0:T(128)} %bitcast.2.parity_ref, bf16[3,144,128]{2,1,0:T(8,128)(2,1)S(1)} %get-tuple-element.24.own_ref, bf16[3,144,128]{2,1,0:T(8,128)(2,1)S(1)} %collective-permute-done.2.near_ref, bf16[3,144,128]{2,1,0:T(8,128)(2,1)S(1)} %collective-permute-done.3.far_ref, ...), custom_call_target="tpu_custom_call" | custom-call | tf_op jit(solution)/shard_map/pallas_call | solution.py:402
  21.5 4.8 %shard_map.80 = (f32[32,2,64,128]{3,2,1,0:T(8,128)}, bf16[512,128]{1,0:T(8,128)(2,1)}, bf16[512,128]{1,0:T(8,128)(2,1)}) custom-call(s32[2]{0:T(128)S(1)} %pad_add_fusion.blocks_ref, f32[32,2,64,128]{3,2,1,0:T(8,128)S(1)} %copy-done, f32[32,16,128]{2,1,0:T(8,128)S(1)} %get-tuple-element.23.rows_ref, bf16[2,576,128]{2,1,0:T(8,128)(2,1)S(1)} %shard_map.79.border_ref, ...), custom_call_target="tpu_custom_call" | custom-call | tf_op jit(solution)/shard_map/pallas_call | solution.py:402
  26.3 0.8 collective-permute-start.4
  27.0 1.3 %collective-permute-start.5 = (bf16[512,128]{1,0:T(8,128)(2,1)}, bf16[512,128]{1,0:T(8,128)(2,1)S(1)}, u32[]{:S(2)}, u32[]{:S(2)}) collective-permute-start(bf16[512,128]{1,0:T(8,128)(2,1)} %get-tuple-element.30), channel_id=1, source_target_pairs={{0,20},{4,16},{8,28},{12,24},{16,4},{20,0},{24,12},{28,8},{1,21},{... | collective-permute-start | bytes 393224 | tf_op jit(solution)/shard_map/ppermute | solution.py:592
  28.3 0.1 stack.43.blocks_ref
  28.4 9.3 %shard_map.81 = (f32[32,2,64,128]{3,2,1,0:T(8,128)}, bf16[512,128]{1,0:T(8,128)(2,1)}, bf16[512,128]{1,0:T(8,128)(2,1)}, bf16[512,128]{1,0:T(8,128)(2,1)}, bf16[...) custom-call(s32[5]{0:T(128)S(1)} %stack.43.blocks_ref, ...), custom_call_target="tpu_custom_call", output_to_operand_aliasing={{0}: (7, {})} | custom-call | tf_op jit(solution)/shard_map/pallas_call | solution.py:402
  37.8 3.1 %collective-permute-start.6 = (bf16[512,128]{1,0:T(8,128)(2,1)}, bf16[512,128]{1,0:T(8,128)(2,1)S(1)}, u32[]{:S(2)}, u32[]{:S(2)}) collective-permute-start(bf16[512,128]{1,0:T(8,128)(2,1)} %get-tuple-element.31), channel_id=1, source_target_pairs={{0,24},{4,28},{8,16},{12,20},{16,8},{20,12},{24,0},{28,4},{1,25},{... | collective-permute-start | bytes 393224 | tf_op jit(solution)/shard_map/ppermute | solution.py:592
  40.9 2.6 %collective-permute-start.7 = (bf16[512,128]{1,0:T(8,128)(2,1)}, bf16[512,128]{1,0:T(8,128)(2,1)S(1)}, u32[]{:S(2)}, u32[]{:S(2)}) collective-permute-start(bf16[512,128]{1,0:T(8,128)(2,1)} %get-tuple-element.32), channel_id=1, source_target_pairs={{0,28},{4,24},{8,20},{12,16},{16,12},{20,8},{24,4},{28,0},{1,29},{... | collective-permute-start | bytes 393224 | tf_op jit(solution)/shard_map/ppermute | solution.py:592
  43.5 3.5 %collective-permute-start.10 = (bf16[512,128]{1,0:T(8,128)(2,1)}, bf16[512,128]{1,0:T(8,128)(2,1)}, u32[]{:S(2)}, u32[]{:S(2)}) collective-permute-start(bf16[512,128]{1,0:T(8,128)(2,1)} %get-tuple-element.36), channel_id=1, source_target_pairs={{0,12},{4,8},{8,4},{12,0},{16,28},{20,24},{24,20},{28,16},{1,13},{... | collective-permute-start | bytes 393224 | tf_op jit(solution)/shard_map/ppermute | solution.py:592
  47.0 0.1 pad_add_fusion.1.place_ref
  47.1 2.6 %shard_map.82 = (f32[32,2,64,128]{3,2,1,0:T(8,128)}, bf16[512,128]{1,0:T(8,128)(2,1)S(1)}) custom-call(s32[1]{0:T(128)} %bitcast.blocks_ref, f32[32,2,64,128]{3,2,1,0:T(8,128)S(1)} %copy-done, f32[32,16,128]{2,1,0:T(8,128)S(1)} %get-tuple-element.23.rows_ref, bf16[2,576,128]{2,1,0:T(8,128)(2,1)S(1)} %shard_map.79.border_ref, ...), custom_call_target="tpu_custom_call", output_to_operand_aliasing={{0}: (7, {})} | custom-call | tf_op jit(solution)/shard_map/pallas_call | solution.py:402
  49.7 1.2 %collective-permute-done.7.rest_3_.rest_7_ = bf16[512,128]{1,0:T(8,128)(2,1)S(1)} collective-permute-done((bf16[512,128]{1,0:T(8,128)(2,1)}, bf16[512,128]{1,0:T(8,128)(2,1)S(1)}, u32[]{:S(2)}, u32[]{:S(2)}) %collective-permute-start.7) | collective-permute-done | bytes 131104 | tf_op jit(solution)/shard_map/ppermute | solution.py:592
  50.9 0.8 shard_map.83.early_ref
  51.8 3.4 %collective-permute-done.10.rest_3_ = bf16[512,128]{1,0:T(8,128)(2,1)} collective-permute-done((bf16[512,128]{1,0:T(8,128)(2,1)}, bf16[512,128]{1,0:T(8,128)(2,1)}, u32[]{:S(2)}, u32[]{:S(2)}) %collective-permute-start.10) | collective-permute-done | bytes 131104 | tf_op jit(solution)/shard_map/ppermute | solution.py:592
  55.2 1.9 %shard_map.84 = bf16[1024,128]{1,0:T(8,128)(2,1)S(1)} custom-call(s32[2]{0:T(128)S(1)} %pad_add_fusion.1.place_ref, bf16[1024,128]{1,0:T(8,128)(2,1)S(1)} %copy-done.2, f32[512,128]{1,0:T(8,128)S(1)} %shard_map.83.early_ref, bf16[512,128]{1,0:T(8,128)(2,1)S(1)} %get-tuple-element.33.rest_0_, bf16[512,128]{1,0:T(8,128)(2,1)S(1)} %collective-permute-done.8.rest_1_, ...), custom_call_target="tpu_custom_call" | custom-call | tf_op jit(solution)/shard_map/pallas_call | solution.py:402
  57.1 13.8 %all_to_all.10 = bf16[32,32,128]{2,1,0:T(8,128)(2,1)S(1)} all-to-all(bf16[32,32,128]{2,1,0:T(8,128)(2,1)S(1)} %bitcast.17), channel_id=1, replica_groups=mesh['gx'=8,'gy'=4] {'gx','gy'}, dimensions={0} | all-to-all | bytes 524288 | tf_op jit(solution)/shard_map/all_to_all | solution.py:438
  71.0 17.8 %all_to_all.11 = f32[32,32,128]{2,1,0:T(8,128)S(1)} all-to-all(f32[32,32,128]{2,1,0:T(8,128)S(1)} %broadcast_in_dim.26), channel_id=1, replica_groups=mesh['gx'=8,'gy'=4] {'gx','gy'}, dimensions={0} | all-to-all | bytes 1048576 | tf_op jit(solution)/shard_map/all_to_all | solution.py:442
  88.8 5.9 %shard_map.85 = (bf16[32,128]{1,0:T(8,128)(2,1)}, f32[512,128]{1,0:T(8,128)}) custom-call(s32[2]{0:T(128)S(1)} %pad_add_fusion.1.place_ref, f32[1024,128]{1,0:T(8,128)S(1)} %bitcast.16, bf16[512,128]{1,0:T(8,128)(2,1)S(1)} %get-tuple-element.33.rest_0_, bf16[512,128]{1,0:T(8,128)(2,1)S(1)} %collective-permute-done.8.rest_1_, ...), custom_call_target="tpu_custom_call" | custom-call | tf_op jit(solution)/shard_map/pallas_call | solution.py:402
  (23 shorter events, 0.3 us)
Async XLA Ops:
  0.6 5.1 %copy-start = (f32[32,2,64,128]{3,2,1,0:T(8,128)S(1)}, f32[32,2,64,128]{3,2,1,0:T(8,128)}, u32[]{:S(2)}) copy-start(f32[32,2,64,128]{3,2,1,0:T(8,128)} %state_ref.9) | copy-start | bytes 6291460
  0.6 5.1 %copy-start.1 = (f32[3,2,64,128]{3,2,1,0:T(8,128)S(1)}, f32[3,2,64,128]{3,2,1,0:T(8,128)}, u32[]{:S(2)}) copy-start(f32[3,2,64,128]{3,2,1,0:T(8,128)} %velocity_ref.5) | copy-start | bytes 589828
  0.7 5.7 %copy-start.3 = (f32[32]{0:T(128)S(1)}, f32[32]{0:T(128)}, u32[]{:S(2)}) copy-start(f32[32]{0:T(128)} %spread_ref.5) | copy-start | bytes 388
  0.7 5.7 %copy-start.4 = (f32[32]{0:T(128)S(1)}, f32[32]{0:T(128)}, u32[]{:S(2)}) copy-start(f32[32]{0:T(128)} %rate_ref.5) | copy-start | bytes 388
  2.6 4.2 %collective-permute-start = (bf16[18,16,128]{2,1,0:T(8,128)(2,1)}, bf16[18,16,128]{2,1,0:T(8,128)(2,1)S(1)}, u32[]{:S(2)}, u32[]{:S(2)}) collective-permute-start(bf16[18,16,128]{2,1,0:T(8,128)(2,1)} %get-tuple-element.21), channel_id=1, source_target_pairs={{0,1},{1,0},{2,3},{3,2},{4,5},{5,4},{6,7},{7,6},{8,9},{9,8},{10,11... | collective-permute-start | bytes 221192 | tf_op jit(solution)/shard_map/ppermute | solution.py:31
  3.1 5.4 %collective-permute-start.1 = (bf16[18,16,128]{2,1,0:T(8,128)(2,1)}, bf16[18,16,128]{2,1,0:T(8,128)(2,1)S(1)}, u32[]{:S(2)}, u32[]{:S(2)}) collective-permute-start(bf16[18,16,128]{2,1,0:T(8,128)(2,1)} %get-tuple-element.22), channel_id=1, source_target_pairs={{0,3},{1,2},{2,1},{3,0},{4,7},{5,6},{6,5},{7,4},{8,11},{9,10},{10,... | collective-permute-start | bytes 221192 | tf_op jit(solution)/shard_map/ppermute | solution.py:35
  8.6 8.2 %collective-permute-start.3 = (bf16[3,144,128]{2,1,0:T(8,128)(2,1)S(1)}, bf16[3,144,128]{2,1,0:T(8,128)(2,1)S(1)}, u32[]{:S(2)}, u32[]{:S(2)}) collective-permute-start(bf16[3,144,128]{2,1,0:T(8,128)(2,1)S(1)} %get-tuple-element.24.own_ref), channel_id=1, source_target_pairs={{0,28},{4,8},{8,4},{12,16},{16,12},{20,24},{24,20},{28,0},{1,29},{... | collective-permute-start | bytes 331784 | tf_op jit(solution)/shard_map/ppermute | solution.py:35
  13.1 6.0 %collective-permute-start.2 = (bf16[3,144,128]{2,1,0:T(8,128)(2,1)S(1)}, bf16[3,144,128]{2,1,0:T(8,128)(2,1)S(1)}, u32[]{:S(2)}, u32[]{:S(2)}) collective-permute-start(bf16[3,144,128]{2,1,0:T(8,128)(2,1)S(1)} %get-tuple-element.24.own_ref), channel_id=1, source_target_pairs={{0,4},{4,0},{8,12},{12,8},{16,20},{20,16},{24,28},{28,24},{1,5},{5... | collective-permute-start | bytes 331784 | tf_op jit(solution)/shard_map/ppermute | solution.py:31
  26.3 17.2 %collective-permute-start.4 = (bf16[512,128]{1,0:T(8,128)(2,1)}, bf16[512,128]{1,0:T(8,128)(2,1)S(1)}, u32[]{:S(2)}, u32[]{:S(2)}) collective-permute-start(bf16[512,128]{1,0:T(8,128)(2,1)} %get-tuple-element.29), channel_id=1, source_target_pairs={{0,16},{4,20},{8,24},{12,28},{16,0},{20,4},{24,8},{28,12},{1,17},{... | collective-permute-start | bytes 393224 | tf_op jit(solution)/shard_map/ppermute | solution.py:592
  27.0 16.5 %collective-permute-start.5 = (bf16[512,128]{1,0:T(8,128)(2,1)}, bf16[512,128]{1,0:T(8,128)(2,1)S(1)}, u32[]{:S(2)}, u32[]{:S(2)}) collective-permute-start(bf16[512,128]{1,0:T(8,128)(2,1)} %get-tuple-element.30), channel_id=1, source_target_pairs={{0,20},{4,16},{8,28},{12,24},{16,4},{20,0},{24,12},{28,8},{1,21},{... | collective-permute-start | bytes 393224 | tf_op jit(solution)/shard_map/ppermute | solution.py:592
  37.8 11.9 %collective-permute-start.6 = (bf16[512,128]{1,0:T(8,128)(2,1)}, bf16[512,128]{1,0:T(8,128)(2,1)S(1)}, u32[]{:S(2)}, u32[]{:S(2)}) collective-permute-start(bf16[512,128]{1,0:T(8,128)(2,1)} %get-tuple-element.31), channel_id=1, source_target_pairs={{0,24},{4,28},{8,16},{12,20},{16,8},{20,12},{24,0},{28,4},{1,25},{... | collective-permute-start | bytes 393224 | tf_op jit(solution)/shard_map/ppermute | solution.py:592
  40.9 10.0 %collective-permute-start.7 = (bf16[512,128]{1,0:T(8,128)(2,1)}, bf16[512,128]{1,0:T(8,128)(2,1)S(1)}, u32[]{:S(2)}, u32[]{:S(2)}) collective-permute-start(bf16[512,128]{1,0:T(8,128)(2,1)} %get-tuple-element.32), channel_id=1, source_target_pairs={{0,28},{4,24},{8,20},{12,16},{16,12},{20,8},{24,4},{28,0},{1,29},{... | collective-permute-start | bytes 393224 | tf_op jit(solution)/shard_map/ppermute | solution.py:592
  43.5 8.3 %collective-permute-start.8 = (bf16[512,128]{1,0:T(8,128)(2,1)}, bf16[512,128]{1,0:T(8,128)(2,1)S(1)}, u32[]{:S(2)}, u32[]{:S(2)}) collective-permute-start(bf16[512,128]{1,0:T(8,128)(2,1)} %get-tuple-element.34), channel_id=1, source_target_pairs={{0,4},{4,0},{8,12},{12,8},{16,20},{20,16},{24,28},{28,24},{1,5},{5... | collective-permute-start | bytes 393224 | tf_op jit(solution)/shard_map/ppermute | solution.py:592
  43.5 8.3 %collective-permute-start.9 = (bf16[512,128]{1,0:T(8,128)(2,1)}, bf16[512,128]{1,0:T(8,128)(2,1)}, u32[]{:S(2)}, u32[]{:S(2)}) collective-permute-start(bf16[512,128]{1,0:T(8,128)(2,1)} %get-tuple-element.35), channel_id=1, source_target_pairs={{0,8},{4,12},{8,0},{12,4},{16,24},{20,28},{24,16},{28,20},{1,9},{5... | collective-permute-start | bytes 393224 | tf_op jit(solution)/shard_map/ppermute | solution.py:592
  43.5 11.7 %collective-permute-start.10 = (bf16[512,128]{1,0:T(8,128)(2,1)}, bf16[512,128]{1,0:T(8,128)(2,1)}, u32[]{:S(2)}, u32[]{:S(2)}) collective-permute-start(bf16[512,128]{1,0:T(8,128)(2,1)} %get-tuple-element.36), channel_id=1, source_target_pairs={{0,12},{4,8},{8,4},{12,0},{16,28},{20,24},{24,20},{28,16},{1,13},{... | collective-permute-start | bytes 393224 | tf_op jit(solution)/shard_map/ppermute | solution.py:592
  47.1 3.9 %copy-start.2 = (bf16[1024,128]{1,0:T(8,128)(2,1)S(1)}, bf16[1024,128]{1,0:T(8,128)(2,1)}, u32[]{:S(2)}) copy-start(bf16[1024,128]{1,0:T(8,128)(2,1)} %basis_ref.3) | copy-start | bytes 786436

commit v4 on v3

--- a/solution.py
+++ b/solution.py
@@ -182,19 +182,22 @@
             out.append((jnp.where(low, left, own), jnp.where(low, own, right)))
         return [[out[z][side] for z in range(heights)] for side in range(2)]
 
-    def spread_lanes(packed, slot):
-        part = jnp.where(lane // WINDOW == slot, packed, 0.0)
-        step = WINDOW
-        while step < LANES:
-            part = part + pltpu.roll(part, step, 1)
-            step *= 2
-        return part
-
     flows = windows(groups)
+    packed = jnp.concatenate([flow for side in flows for flow in side], axis=0)
+    packed = packed.astype(jnp.bfloat16)
+    lane_from, lane_to = iota((LANES, LANES), 0), iota((LANES, LANES), 1)
+
+    def spread_lanes(slot):
+        chosen = (lane_from // WINDOW == slot) & (lane_from % WINDOW == lane_to % WINDOW)
+        chosen = chosen.astype(jnp.float32).astype(jnp.bfloat16)
+        return jnp.dot(packed, chosen, preferred_element_type=jnp.float32)
+
+    spread = [spread_lanes(slot) for slot in range(3)]
     flow = [
         [
             [
-                (-0.5 if slot == 2 and z == 1 else 0.5) * spread_lanes(flows[side][z], slot)
+                (-0.5 if slot == 2 and z == 1 else 0.5)
+                * spread[slot][(side * heights + z) * rows : (side * heights + z + 1) * rows]
                 for slot in range(3)
             ]
             for z in range(heights)

time: 95 us -> 93.6 us (0.985)
  Pallas kernels: 30.4 us -> 29.1 us
    pallas_call x10, Pallas kernels: 30.4 us -> 29.1 us  [call(): pl.pallas_call(kernel, out_shape=out_shape, compiler_params=pltpu.Compile...]
where the time goes in v4:
time: 93.6 us; the launch traced here: 93.4 us
  blocking collectives  31.6 us (34%)
  Pallas kernels  29.1 us (31%)
  starting transfers between devices  18.9 us (20%)
  waiting for transfers between devices  12.2 us (13%)
    pallas_call x10, Pallas kernels, call(): pl.pallas_call(kernel, out_shape=out_shape, compiler_params=pltpu.Compile...  29.1 us
    all_to_all x1, blocking collectives, subspace(): lax.all_to_all(jnp.broadcast_to(own_image[None], (owners, rows_each, rank...  17.8 us
    all_to_all x1, blocking collectives, subspace(): lax.all_to_all(partial.reshape(owners, rows_each, rank), BOTH, split_axis...  13.8 us
    ppermute x7, starting transfers between devices, shards(): piece = lax.ppermute(piece, 'gx', [(i, i ^ offset) for i in range(pieces)])  11.3 us
    ppermute x2, starting transfers between devices, swap_far(): return lax.ppermute(x, axis, far_pairs(lax.axis_size(axis)))  7.14 us
    ppermute x2, waiting for transfers between devices, swap_far(): return lax.ppermute(x, axis, far_pairs(lax.axis_size(axis)))  5.28 us
    ppermute x7, waiting for transfers between devices, shards(): piece = lax.ppermute(piece, 'gx', [(i, i ^ offset) for i in range(pieces)])  4.61 us
    ppermute x2, waiting for transfers between devices, swap_near(): return lax.ppermute(x, axis, near_pairs(lax.axis_size(axis)))  2.28 us
  transfers between devices with their start and end apart: 11, of which 5 were waited for; matrix products, arithmetic and copies ran while one was open for 1% of the time, Pallas kernels for 14%

profile of v4, /device:TPU:0, one launch (start us, length us, event | category | flops | bytes accessed | tf_op | source)
XLA Modules:
  0.0 93.4 jit_solution(11853739996952110241)
XLA Ops:
  0.7 1.9 %shard_map.76 = (bf16[18,16,128]{2,1,0:T(8,128)(2,1)}, bf16[18,16,128]{2,1,0:T(8,128)(2,1)}) custom-call(s32[1]{0:T(128)} %bitcast.1.parity_ref, f32[32,2,64,128]{3,2,1,0:T(8,128)} %state_ref.9, f32[3,2,64,128]{3,2,1,0:T(8,128)} %velocity_ref.5), custom_call_target="tpu_custom_call" | custom-call | tf_op jit(solution)/shard_map/pallas_call | solution.py:405
  2.6 0.5 collective-permute-start
  3.1 2.6 %collective-permute-start.1 = (bf16[18,16,128]{2,1,0:T(8,128)(2,1)}, bf16[18,16,128]{2,1,0:T(8,128)(2,1)S(1)}, u32[]{:S(2)}, u32[]{:S(2)}) collective-permute-start(bf16[18,16,128]{2,1,0:T(8,128)(2,1)} %get-tuple-element.22), channel_id=1, source_target_pairs={{0,3},{1,2},{2,1},{3,0},{4,7},{5,6},{6,5},{7,4},{8,11},{9,10},{10,... | collective-permute-start | bytes 221192 | tf_op jit(solution)/shard_map/ppermute | solution.py:35
  5.7 0.6 shard_map.77.old_ref
  6.3 0.1 broadcast_in_dim.20
  6.4 0.1 broadcast_in_dim.23
  6.6 0.1 broadcast_in_dim.25
  6.7 0.1 broadcast_in_dim.22
  6.8 1.6 %collective-permute-done.1.far_ref = bf16[18,16,128]{2,1,0:T(8,128)(2,1)S(1)} collective-permute-done((bf16[18,16,128]{2,1,0:T(8,128)(2,1)}, bf16[18,16,128]{2,1,0:T(8,128)(2,1)S(1)}, u32[]{:S(2)}, u32[]{:S(2)}) %collective-permute-start.1) | collective-permute-done | bytes 73760 | tf_op jit(solution)/shard_map/ppermute | solution.py:35
  8.5 0.1 shard_map.78
  8.6 4.5 %collective-permute-start.3 = (bf16[3,144,128]{2,1,0:T(8,128)(2,1)S(1)}, bf16[3,144,128]{2,1,0:T(8,128)(2,1)S(1)}, u32[]{:S(2)}, u32[]{:S(2)}) collective-permute-start(bf16[3,144,128]{2,1,0:T(8,128)(2,1)S(1)} %get-tuple-element.24.own_ref), channel_id=1, source_target_pairs={{0,28},{4,8},{8,4},{12,16},{16,12},{20,24},{24,20},{28,0},{1,29},{... | collective-permute-start | bytes 331784 | tf_op jit(solution)/shard_map/ppermute | solution.py:35
  13.1 0.1 pad_add_fusion.blocks_ref
  13.2 3.6 %collective-permute-done.3.far_ref = bf16[3,144,128]{2,1,0:T(8,128)(2,1)S(1)} collective-permute-done((bf16[3,144,128]{2,1,0:T(8,128)(2,1)S(1)}, bf16[3,144,128]{2,1,0:T(8,128)(2,1)S(1)}, u32[]{:S(2)}, u32[]{:S(2)}) %collective-permute-start.3) | collective-permute-done | bytes 110624 | tf_op jit(solution)/shard_map/ppermute | solution.py:35
  16.9 2.3 %collective-permute-done.2.near_ref = bf16[3,144,128]{2,1,0:T(8,128)(2,1)S(1)} collective-permute-done((bf16[3,144,128]{2,1,0:T(8,128)(2,1)S(1)}, bf16[3,144,128]{2,1,0:T(8,128)(2,1)S(1)}, u32[]{:S(2)}, u32[]{:S(2)}) %collective-permute-start.2) | collective-permute-done | bytes 110624 | tf_op jit(solution)/shard_map/ppermute | solution.py:31
  19.1 1.0 %shard_map.79.border_ref = bf16[2,576,128]{2,1,0:T(8,128)(2,1)S(1)} custom-call(s32[1]{0:T(128)} %bitcast.2.parity_ref, bf16[3,144,128]{2,1,0:T(8,128)(2,1)S(1)} %get-tuple-element.24.own_ref, bf16[3,144,128]{2,1,0:T(8,128)(2,1)S(1)} %collective-permute-done.2.near_ref, bf16[3,144,128]{2,1,0:T(8,128)(2,1)S(1)} %collective-permute-done.3.far_ref, ...), custom_call_target="tpu_custom_call" | custom-call | tf_op jit(solution)/shard_map/pallas_call | solution.py:405
  20.2 4.8 %shard_map.80 = (f32[32,2,64,128]{3,2,1,0:T(8,128)}, bf16[512,128]{1,0:T(8,128)(2,1)}, bf16[512,128]{1,0:T(8,128)(2,1)}) custom-call(s32[2]{0:T(128)S(1)} %pad_add_fusion.blocks_ref, f32[32,2,64,128]{3,2,1,0:T(8,128)S(1)} %copy-done, f32[32,16,128]{2,1,0:T(8,128)S(1)} %get-tuple-element.23.rows_ref, bf16[2,576,128]{2,1,0:T(8,128)(2,1)S(1)} %shard_map.79.border_ref, ...), custom_call_target="tpu_custom_call" | custom-call | tf_op jit(solution)/shard_map/pallas_call | solution.py:405
  24.9 0.8 collective-permute-start.4
  25.7 1.3 %collective-permute-start.5 = (bf16[512,128]{1,0:T(8,128)(2,1)}, bf16[512,128]{1,0:T(8,128)(2,1)S(1)}, u32[]{:S(2)}, u32[]{:S(2)}) collective-permute-start(bf16[512,128]{1,0:T(8,128)(2,1)} %get-tuple-element.30), channel_id=1, source_target_pairs={{0,20},{4,16},{8,28},{12,24},{16,4},{20,0},{24,12},{28,8},{1,21},{... | collective-permute-start | bytes 393224 | tf_op jit(solution)/shard_map/ppermute | solution.py:595
  27.0 0.1 stack.43.blocks_ref
  27.1 9.3 %shard_map.81 = (f32[32,2,64,128]{3,2,1,0:T(8,128)}, bf16[512,128]{1,0:T(8,128)(2,1)}, bf16[512,128]{1,0:T(8,128)(2,1)}, bf16[512,128]{1,0:T(8,128)(2,1)}, bf16[...) custom-call(s32[5]{0:T(128)S(1)} %stack.43.blocks_ref, ...), custom_call_target="tpu_custom_call", output_to_operand_aliasing={{0}: (7, {})} | custom-call | tf_op jit(solution)/shard_map/pallas_call | solution.py:405
  36.4 3.1 %collective-permute-start.6 = (bf16[512,128]{1,0:T(8,128)(2,1)}, bf16[512,128]{1,0:T(8,128)(2,1)S(1)}, u32[]{:S(2)}, u32[]{:S(2)}) collective-permute-start(bf16[512,128]{1,0:T(8,128)(2,1)} %get-tuple-element.31), channel_id=1, source_target_pairs={{0,24},{4,28},{8,16},{12,20},{16,8},{20,12},{24,0},{28,4},{1,25},{... | collective-permute-start | bytes 393224 | tf_op jit(solution)/shard_map/ppermute | solution.py:595
  39.5 2.6 %collective-permute-start.7 = (bf16[512,128]{1,0:T(8,128)(2,1)}, bf16[512,128]{1,0:T(8,128)(2,1)S(1)}, u32[]{:S(2)}, u32[]{:S(2)}) collective-permute-start(bf16[512,128]{1,0:T(8,128)(2,1)} %get-tuple-element.32), channel_id=1, source_target_pairs={{0,28},{4,24},{8,20},{12,16},{16,12},{20,8},{24,4},{28,0},{1,29},{... | collective-permute-start | bytes 393224 | tf_op jit(solution)/shard_map/ppermute | solution.py:595
  42.2 3.5 %collective-permute-start.10 = (bf16[512,128]{1,0:T(8,128)(2,1)}, bf16[512,128]{1,0:T(8,128)(2,1)}, u32[]{:S(2)}, u32[]{:S(2)}) collective-permute-start(bf16[512,128]{1,0:T(8,128)(2,1)} %get-tuple-element.36), channel_id=1, source_target_pairs={{0,12},{4,8},{8,4},{12,0},{16,28},{20,24},{24,20},{28,16},{1,13},{... | collective-permute-start | bytes 393224 | tf_op jit(solution)/shard_map/ppermute | solution.py:595
  45.7 0.1 pad_add_fusion.1.place_ref
  45.7 2.6 %shard_map.82 = (f32[32,2,64,128]{3,2,1,0:T(8,128)}, bf16[512,128]{1,0:T(8,128)(2,1)S(1)}) custom-call(s32[1]{0:T(128)} %bitcast.blocks_ref, f32[32,2,64,128]{3,2,1,0:T(8,128)S(1)} %copy-done, f32[32,16,128]{2,1,0:T(8,128)S(1)} %get-tuple-element.23.rows_ref, bf16[2,576,128]{2,1,0:T(8,128)(2,1)S(1)} %shard_map.79.border_ref, ...), custom_call_target="tpu_custom_call", output_to_operand_aliasing={{0}: (7, {})} | custom-call | tf_op jit(solution)/shard_map/pallas_call | solution.py:405
  48.4 1.2 %collective-permute-done.7.rest_3_.rest_7_ = bf16[512,128]{1,0:T(8,128)(2,1)S(1)} collective-permute-done((bf16[512,128]{1,0:T(8,128)(2,1)}, bf16[512,128]{1,0:T(8,128)(2,1)S(1)}, u32[]{:S(2)}, u32[]{:S(2)}) %collective-permute-start.7) | collective-permute-done | bytes 131104 | tf_op jit(solution)/shard_map/ppermute | solution.py:595
  49.6 0.8 shard_map.83.early_ref
  50.4 3.4 %collective-permute-done.10.rest_3_ = bf16[512,128]{1,0:T(8,128)(2,1)} collective-permute-done((bf16[512,128]{1,0:T(8,128)(2,1)}, bf16[512,128]{1,0:T(8,128)(2,1)}, u32[]{:S(2)}, u32[]{:S(2)}) %collective-permute-start.10) | collective-permute-done | bytes 131104 | tf_op jit(solution)/shard_map/ppermute | solution.py:595
  53.9 1.9 %shard_map.84 = bf16[1024,128]{1,0:T(8,128)(2,1)S(1)} custom-call(s32[2]{0:T(128)S(1)} %pad_add_fusion.1.place_ref, bf16[1024,128]{1,0:T(8,128)(2,1)S(1)} %copy-done.2, f32[512,128]{1,0:T(8,128)S(1)} %shard_map.83.early_ref, bf16[512,128]{1,0:T(8,128)(2,1)S(1)} %get-tuple-element.33.rest_0_, bf16[512,128]{1,0:T(8,128)(2,1)S(1)} %collective-permute-done.8.rest_1_, ...), custom_call_target="tpu_custom_call" | custom-call | tf_op jit(solution)/shard_map/pallas_call | solution.py:405
  55.8 13.8 %all_to_all.10 = bf16[32,32,128]{2,1,0:T(8,128)(2,1)S(1)} all-to-all(bf16[32,32,128]{2,1,0:T(8,128)(2,1)S(1)} %bitcast.17), channel_id=1, replica_groups=mesh['gx'=8,'gy'=4] {'gx','gy'}, dimensions={0} | all-to-all | bytes 524288 | tf_op jit(solution)/shard_map/all_to_all | solution.py:441
  69.7 17.8 %all_to_all.11 = f32[32,32,128]{2,1,0:T(8,128)S(1)} all-to-all(f32[32,32,128]{2,1,0:T(8,128)S(1)} %broadcast_in_dim.26), channel_id=1, replica_groups=mesh['gx'=8,'gy'=4] {'gx','gy'}, dimensions={0} | all-to-all | bytes 1048576 | tf_op jit(solution)/shard_map/all_to_all | solution.py:445
  87.5 5.9 %shard_map.85 = (bf16[32,128]{1,0:T(8,128)(2,1)}, f32[512,128]{1,0:T(8,128)}) custom-call(s32[2]{0:T(128)S(1)} %pad_add_fusion.1.place_ref, f32[1024,128]{1,0:T(8,128)S(1)} %bitcast.16, bf16[512,128]{1,0:T(8,128)(2,1)S(1)} %get-tuple-element.33.rest_0_, bf16[512,128]{1,0:T(8,128)(2,1)S(1)} %collective-permute-done.8.rest_1_, ...), custom_call_target="tpu_custom_call" | custom-call | tf_op jit(solution)/shard_map/pallas_call | solution.py:405
  (23 shorter events, 0.3 us)
Async XLA Ops:
  0.6 5.1 %copy-start = (f32[32,2,64,128]{3,2,1,0:T(8,128)S(1)}, f32[32,2,64,128]{3,2,1,0:T(8,128)}, u32[]{:S(2)}) copy-start(f32[32,2,64,128]{3,2,1,0:T(8,128)} %state_ref.9) | copy-start | bytes 6291460
  0.6 5.1 %copy-start.1 = (f32[3,2,64,128]{3,2,1,0:T(8,128)S(1)}, f32[3,2,64,128]{3,2,1,0:T(8,128)}, u32[]{:S(2)}) copy-start(f32[3,2,64,128]{3,2,1,0:T(8,128)} %velocity_ref.5) | copy-start | bytes 589828
  0.7 5.7 %copy-start.3 = (f32[32]{0:T(128)S(1)}, f32[32]{0:T(128)}, u32[]{:S(2)}) copy-start(f32[32]{0:T(128)} %spread_ref.5) | copy-start | bytes 388
  0.7 5.7 %copy-start.4 = (f32[32]{0:T(128)S(1)}, f32[32]{0:T(128)}, u32[]{:S(2)}) copy-start(f32[32]{0:T(128)} %rate_ref.5) | copy-start | bytes 388
  2.6 4.2 %collective-permute-start = (bf16[18,16,128]{2,1,0:T(8,128)(2,1)}, bf16[18,16,128]{2,1,0:T(8,128)(2,1)S(1)}, u32[]{:S(2)}, u32[]{:S(2)}) collective-permute-start(bf16[18,16,128]{2,1,0:T(8,128)(2,1)} %get-tuple-element.21), channel_id=1, source_target_pairs={{0,1},{1,0},{2,3},{3,2},{4,5},{5,4},{6,7},{7,6},{8,9},{9,8},{10,11... | collective-permute-start | bytes 221192 | tf_op jit(solution)/shard_map/ppermute | solution.py:31
  3.1 5.4 %collective-permute-start.1 = (bf16[18,16,128]{2,1,0:T(8,128)(2,1)}, bf16[18,16,128]{2,1,0:T(8,128)(2,1)S(1)}, u32[]{:S(2)}, u32[]{:S(2)}) collective-permute-start(bf16[18,16,128]{2,1,0:T(8,128)(2,1)} %get-tuple-element.22), channel_id=1, source_target_pairs={{0,3},{1,2},{2,1},{3,0},{4,7},{5,6},{6,5},{7,4},{8,11},{9,10},{10,... | collective-permute-start | bytes 221192 | tf_op jit(solution)/shard_map/ppermute | solution.py:35
  8.6 8.2 %collective-permute-start.3 = (bf16[3,144,128]{2,1,0:T(8,128)(2,1)S(1)}, bf16[3,144,128]{2,1,0:T(8,128)(2,1)S(1)}, u32[]{:S(2)}, u32[]{:S(2)}) collective-permute-start(bf16[3,144,128]{2,1,0:T(8,128)(2,1)S(1)} %get-tuple-element.24.own_ref), channel_id=1, source_target_pairs={{0,28},{4,8},{8,4},{12,16},{16,12},{20,24},{24,20},{28,0},{1,29},{... | collective-permute-start | bytes 331784 | tf_op jit(solution)/shard_map/ppermute | solution.py:35
  13.1 6.0 %collective-permute-start.2 = (bf16[3,144,128]{2,1,0:T(8,128)(2,1)S(1)}, bf16[3,144,128]{2,1,0:T(8,128)(2,1)S(1)}, u32[]{:S(2)}, u32[]{:S(2)}) collective-permute-start(bf16[3,144,128]{2,1,0:T(8,128)(2,1)S(1)} %get-tuple-element.24.own_ref), channel_id=1, source_target_pairs={{0,4},{4,0},{8,12},{12,8},{16,20},{20,16},{24,28},{28,24},{1,5},{5... | collective-permute-start | bytes 331784 | tf_op jit(solution)/shard_map/ppermute | solution.py:31
  24.9 17.2 %collective-permute-start.4 = (bf16[512,128]{1,0:T(8,128)(2,1)}, bf16[512,128]{1,0:T(8,128)(2,1)S(1)}, u32[]{:S(2)}, u32[]{:S(2)}) collective-permute-start(bf16[512,128]{1,0:T(8,128)(2,1)} %get-tuple-element.29), channel_id=1, source_target_pairs={{0,16},{4,20},{8,24},{12,28},{16,0},{20,4},{24,8},{28,12},{1,17},{... | collective-permute-start | bytes 393224 | tf_op jit(solution)/shard_map/ppermute | solution.py:595
  25.7 16.5 %collective-permute-start.5 = (bf16[512,128]{1,0:T(8,128)(2,1)}, bf16[512,128]{1,0:T(8,128)(2,1)S(1)}, u32[]{:S(2)}, u32[]{:S(2)}) collective-permute-start(bf16[512,128]{1,0:T(8,128)(2,1)} %get-tuple-element.30), channel_id=1, source_target_pairs={{0,20},{4,16},{8,28},{12,24},{16,4},{20,0},{24,12},{28,8},{1,21},{... | collective-permute-start | bytes 393224 | tf_op jit(solution)/shard_map/ppermute | solution.py:595
  36.4 12.0 %collective-permute-start.6 = (bf16[512,128]{1,0:T(8,128)(2,1)}, bf16[512,128]{1,0:T(8,128)(2,1)S(1)}, u32[]{:S(2)}, u32[]{:S(2)}) collective-permute-start(bf16[512,128]{1,0:T(8,128)(2,1)} %get-tuple-element.31), channel_id=1, source_target_pairs={{0,24},{4,28},{8,16},{12,20},{16,8},{20,12},{24,0},{28,4},{1,25},{... | collective-permute-start | bytes 393224 | tf_op jit(solution)/shard_map/ppermute | solution.py:595
  39.5 10.0 %collective-permute-start.7 = (bf16[512,128]{1,0:T(8,128)(2,1)}, bf16[512,128]{1,0:T(8,128)(2,1)S(1)}, u32[]{:S(2)}, u32[]{:S(2)}) collective-permute-start(bf16[512,128]{1,0:T(8,128)(2,1)} %get-tuple-element.32), channel_id=1, source_target_pairs={{0,28},{4,24},{8,20},{12,16},{16,12},{20,8},{24,4},{28,0},{1,29},{... | collective-permute-start | bytes 393224 | tf_op jit(solution)/shard_map/ppermute | solution.py:595
  42.2 8.3 %collective-permute-start.8 = (bf16[512,128]{1,0:T(8,128)(2,1)}, bf16[512,128]{1,0:T(8,128)(2,1)S(1)}, u32[]{:S(2)}, u32[]{:S(2)}) collective-permute-start(bf16[512,128]{1,0:T(8,128)(2,1)} %get-tuple-element.34), channel_id=1, source_target_pairs={{0,4},{4,0},{8,12},{12,8},{16,20},{20,16},{24,28},{28,24},{1,5},{5... | collective-permute-start | bytes 393224 | tf_op jit(solution)/shard_map/ppermute | solution.py:595
  42.2 8.3 %collective-permute-start.9 = (bf16[512,128]{1,0:T(8,128)(2,1)}, bf16[512,128]{1,0:T(8,128)(2,1)}, u32[]{:S(2)}, u32[]{:S(2)}) collective-permute-start(bf16[512,128]{1,0:T(8,128)(2,1)} %get-tuple-element.35), channel_id=1, source_target_pairs={{0,8},{4,12},{8,0},{12,4},{16,24},{20,28},{24,16},{28,20},{1,9},{5... | collective-permute-start | bytes 393224 | tf_op jit(solution)/shard_map/ppermute | solution.py:595
  42.2 11.7 %collective-permute-start.10 = (bf16[512,128]{1,0:T(8,128)(2,1)}, bf16[512,128]{1,0:T(8,128)(2,1)}, u32[]{:S(2)}, u32[]{:S(2)}) collective-permute-start(bf16[512,128]{1,0:T(8,128)(2,1)} %get-tuple-element.36), channel_id=1, source_target_pairs={{0,12},{4,8},{8,4},{12,0},{16,28},{20,24},{24,20},{28,16},{1,13},{... | collective-permute-start | bytes 393224 | tf_op jit(solution)/shard_map/ppermute | solution.py:595
  45.7 3.9 %copy-start.2 = (bf16[1024,128]{1,0:T(8,128)(2,1)S(1)}, bf16[1024,128]{1,0:T(8,128)(2,1)}, u32[]{:S(2)}) copy-start(bf16[1024,128]{1,0:T(8,128)(2,1)} %basis_ref.3) | copy-start | bytes 786436

commit v5 on v4

--- a/solution.py
+++ b/solution.py
@@ -266,12 +266,17 @@
         fetch(step + 1, 1 - now).start()
 
     lane_from, lane_to = iota((LANES, LANES), 0), iota((LANES, LANES), 1)
-    for at in range(count):
+    def chosen(at):
         base = WINDOW * lax.rem(first + at, LANES // WINDOW) + WIDTH
         west = (lane_from == base - 1) & (lane_to == LANES - 1)
         east = (lane_from == base) & (lane_to == 0)
-        chosen = (west | east).astype(jnp.float32).astype(jnp.bfloat16)
-        side_ref[at] = jnp.dot(border_ref[0], chosen, preferred_element_type=jnp.float32)
+        return (west | east).astype(jnp.float32).astype(jnp.bfloat16)
+
+    for at in range(0, count, 2):
+        pair = jnp.concatenate([chosen(at), chosen(at + 1)], axis=1)
+        aligned = jnp.dot(border_ref[0], pair, preferred_element_type=jnp.float32)
+        side_ref[at] = aligned[:, :LANES]
+        side_ref[at + 1] = aligned[:, LANES:]
 
     fetch(step, now).wait()
     for at in range(count):

time: 93.6 us -> 93.9 us (level)
  transfers between devices with their start and end apart: 11 -> 11, of which waited for: 5 -> 5; matrix products, arithmetic and copies ran while one was open for 1% -> 1% of each run, Pallas kernels for 14% -> 15%
where the time goes in v5:
time: 93.9 us; the launch traced here: 93.7 us
  blocking collectives  31.6 us (34%)
  Pallas kernels  29.4 us (31%)
  starting transfers between devices  18.9 us (20%)
  waiting for transfers between devices  12.1 us (13%)
    pallas_call x10, Pallas kernels, call(): pl.pallas_call(kernel, out_shape=out_shape, compiler_params=pltpu.Compile...  29.4 us
    all_to_all x1, blocking collectives, subspace(): lax.all_to_all(jnp.broadcast_to(own_image[None], (owners, rows_each, rank...  17.8 us
    all_to_all x1, blocking collectives, subspace(): lax.all_to_all(partial.reshape(owners, rows_each, rank), BOTH, split_axis...  13.8 us
    ppermute x7, starting transfers between devices, shards(): piece = lax.ppermute(piece, 'gx', [(i, i ^ offset) for i in range(pieces)])  11.3 us
    ppermute x2, starting transfers between devices, swap_far(): return lax.ppermute(x, axis, far_pairs(lax.axis_size(axis)))  7.14 us
    ppermute x2, waiting for transfers between devices, swap_far(): return lax.ppermute(x, axis, far_pairs(lax.axis_size(axis)))  5.28 us
    ppermute x7, waiting for transfers between devices, shards(): piece = lax.ppermute(piece, 'gx', [(i, i ^ offset) for i in range(pieces)])  4.57 us
    ppermute x2, waiting for transfers between devices, swap_near(): return lax.ppermute(x, axis, near_pairs(lax.axis_size(axis)))  2.28 us
  transfers between devices with their start and end apart: 11, of which 5 were waited for; matrix products, arithmetic and copies ran while one was open for 1% of the time, Pallas kernels for 15%

profile of v5, /device:TPU:0, one launch (start us, length us, event | category | flops | bytes accessed | tf_op | source)
XLA Modules:
  0.0 93.7 jit_solution(3096452539198318389)
XLA Ops:
  0.7 1.9 %shard_map.76 = (bf16[18,16,128]{2,1,0:T(8,128)(2,1)}, bf16[18,16,128]{2,1,0:T(8,128)(2,1)}) custom-call(s32[1]{0:T(128)} %bitcast.1.parity_ref, f32[32,2,64,128]{3,2,1,0:T(8,128)} %state_ref.9, f32[3,2,64,128]{3,2,1,0:T(8,128)} %velocity_ref.5), custom_call_target="tpu_custom_call" | custom-call | tf_op jit(solution)/shard_map/pallas_call | solution.py:410
  2.6 0.5 collective-permute-start
  3.1 2.6 %collective-permute-start.1 = (bf16[18,16,128]{2,1,0:T(8,128)(2,1)}, bf16[18,16,128]{2,1,0:T(8,128)(2,1)S(1)}, u32[]{:S(2)}, u32[]{:S(2)}) collective-permute-start(bf16[18,16,128]{2,1,0:T(8,128)(2,1)} %get-tuple-element.22), channel_id=1, source_target_pairs={{0,3},{1,2},{2,1},{3,0},{4,7},{5,6},{6,5},{7,4},{8,11},{9,10},{10,... | collective-permute-start | bytes 221192 | tf_op jit(solution)/shard_map/ppermute | solution.py:35
  5.7 0.6 shard_map.77.old_ref
  6.3 0.1 broadcast_in_dim.20
  6.4 0.1 broadcast_in_dim.23
  6.6 0.1 broadcast_in_dim.25
  6.7 0.1 broadcast_in_dim.22
  6.8 1.6 %collective-permute-done.1.far_ref = bf16[18,16,128]{2,1,0:T(8,128)(2,1)S(1)} collective-permute-done((bf16[18,16,128]{2,1,0:T(8,128)(2,1)}, bf16[18,16,128]{2,1,0:T(8,128)(2,1)S(1)}, u32[]{:S(2)}, u32[]{:S(2)}) %collective-permute-start.1) | collective-permute-done | bytes 73760 | tf_op jit(solution)/shard_map/ppermute | solution.py:35
  8.5 0.1 shard_map.78
  8.6 4.5 %collective-permute-start.3 = (bf16[3,144,128]{2,1,0:T(8,128)(2,1)S(1)}, bf16[3,144,128]{2,1,0:T(8,128)(2,1)S(1)}, u32[]{:S(2)}, u32[]{:S(2)}) collective-permute-start(bf16[3,144,128]{2,1,0:T(8,128)(2,1)S(1)} %get-tuple-element.24.own_ref), channel_id=1, source_target_pairs={{0,28},{4,8},{8,4},{12,16},{16,12},{20,24},{24,20},{28,0},{1,29},{... | collective-permute-start | bytes 331784 | tf_op jit(solution)/shard_map/ppermute | solution.py:35
  13.1 0.1 pad_add_fusion.blocks_ref
  13.2 3.6 %collective-permute-done.3.far_ref = bf16[3,144,128]{2,1,0:T(8,128)(2,1)S(1)} collective-permute-done((bf16[3,144,128]{2,1,0:T(8,128)(2,1)S(1)}, bf16[3,144,128]{2,1,0:T(8,128)(2,1)S(1)}, u32[]{:S(2)}, u32[]{:S(2)}) %collective-permute-start.3) | collective-permute-done | bytes 110624 | tf_op jit(solution)/shard_map/ppermute | solution.py:35
  16.9 2.3 %collective-permute-done.2.near_ref = bf16[3,144,128]{2,1,0:T(8,128)(2,1)S(1)} collective-permute-done((bf16[3,144,128]{2,1,0:T(8,128)(2,1)S(1)}, bf16[3,144,128]{2,1,0:T(8,128)(2,1)S(1)}, u32[]{:S(2)}, u32[]{:S(2)}) %collective-permute-start.2) | collective-permute-done | bytes 110624 | tf_op jit(solution)/shard_map/ppermute | solution.py:31
  19.1 1.0 %shard_map.79.border_ref = bf16[2,576,128]{2,1,0:T(8,128)(2,1)S(1)} custom-call(s32[1]{0:T(128)} %bitcast.2.parity_ref, bf16[3,144,128]{2,1,0:T(8,128)(2,1)S(1)} %get-tuple-element.24.own_ref, bf16[3,144,128]{2,1,0:T(8,128)(2,1)S(1)} %collective-permute-done.2.near_ref, bf16[3,144,128]{2,1,0:T(8,128)(2,1)S(1)} %collective-permute-done.3.far_ref, ...), custom_call_target="tpu_custom_call" | custom-call | tf_op jit(solution)/shard_map/pallas_call | solution.py:410
  20.2 4.9 %shard_map.80 = (f32[32,2,64,128]{3,2,1,0:T(8,128)}, bf16[512,128]{1,0:T(8,128)(2,1)}, bf16[512,128]{1,0:T(8,128)(2,1)}) custom-call(s32[2]{0:T(128)S(1)} %pad_add_fusion.blocks_ref, f32[32,2,64,128]{3,2,1,0:T(8,128)S(1)} %copy-done, f32[32,16,128]{2,1,0:T(8,128)S(1)} %get-tuple-element.23.rows_ref, bf16[2,576,128]{2,1,0:T(8,128)(2,1)S(1)} %shard_map.79.border_ref, ...), custom_call_target="tpu_custom_call" | custom-call | tf_op jit(solution)/shard_map/pallas_call | solution.py:410
  25.0 0.8 collective-permute-start.4
  25.8 1.3 %collective-permute-start.5 = (bf16[512,128]{1,0:T(8,128)(2,1)}, bf16[512,128]{1,0:T(8,128)(2,1)S(1)}, u32[]{:S(2)}, u32[]{:S(2)}) collective-permute-start(bf16[512,128]{1,0:T(8,128)(2,1)} %get-tuple-element.30), channel_id=1, source_target_pairs={{0,20},{4,16},{8,28},{12,24},{16,4},{20,0},{24,12},{28,8},{1,21},{... | collective-permute-start | bytes 393224 | tf_op jit(solution)/shard_map/ppermute | solution.py:600
  27.1 0.1 stack.43.blocks_ref
  27.2 9.6 %shard_map.81 = (f32[32,2,64,128]{3,2,1,0:T(8,128)}, bf16[512,128]{1,0:T(8,128)(2,1)}, bf16[512,128]{1,0:T(8,128)(2,1)}, bf16[512,128]{1,0:T(8,128)(2,1)}, bf16[...) custom-call(s32[5]{0:T(128)S(1)} %stack.43.blocks_ref, ...), custom_call_target="tpu_custom_call", output_to_operand_aliasing={{0}: (7, {})} | custom-call | tf_op jit(solution)/shard_map/pallas_call | solution.py:410
  36.8 3.1 %collective-permute-start.6 = (bf16[512,128]{1,0:T(8,128)(2,1)}, bf16[512,128]{1,0:T(8,128)(2,1)S(1)}, u32[]{:S(2)}, u32[]{:S(2)}) collective-permute-start(bf16[512,128]{1,0:T(8,128)(2,1)} %get-tuple-element.31), channel_id=1, source_target_pairs={{0,24},{4,28},{8,16},{12,20},{16,8},{20,12},{24,0},{28,4},{1,25},{... | collective-permute-start | bytes 393224 | tf_op jit(solution)/shard_map/ppermute | solution.py:600
  39.9 2.6 %collective-permute-start.7 = (bf16[512,128]{1,0:T(8,128)(2,1)}, bf16[512,128]{1,0:T(8,128)(2,1)S(1)}, u32[]{:S(2)}, u32[]{:S(2)}) collective-permute-start(bf16[512,128]{1,0:T(8,128)(2,1)} %get-tuple-element.32), channel_id=1, source_target_pairs={{0,28},{4,24},{8,20},{12,16},{16,12},{20,8},{24,4},{28,0},{1,29},{... | collective-permute-start | bytes 393224 | tf_op jit(solution)/shard_map/ppermute | solution.py:600
  42.5 3.5 %collective-permute-start.10 = (bf16[512,128]{1,0:T(8,128)(2,1)}, bf16[512,128]{1,0:T(8,128)(2,1)}, u32[]{:S(2)}, u32[]{:S(2)}) collective-permute-start(bf16[512,128]{1,0:T(8,128)(2,1)} %get-tuple-element.36), channel_id=1, source_target_pairs={{0,12},{4,8},{8,4},{12,0},{16,28},{20,24},{24,20},{28,16},{1,13},{... | collective-permute-start | bytes 393224 | tf_op jit(solution)/shard_map/ppermute | solution.py:600
  46.0 0.1 pad_add_fusion.1.place_ref
  46.1 2.7 %shard_map.82 = (f32[32,2,64,128]{3,2,1,0:T(8,128)}, bf16[512,128]{1,0:T(8,128)(2,1)S(1)}) custom-call(s32[1]{0:T(128)} %bitcast.blocks_ref, f32[32,2,64,128]{3,2,1,0:T(8,128)S(1)} %copy-done, f32[32,16,128]{2,1,0:T(8,128)S(1)} %get-tuple-element.23.rows_ref, bf16[2,576,128]{2,1,0:T(8,128)(2,1)S(1)} %shard_map.79.border_ref, ...), custom_call_target="tpu_custom_call", output_to_operand_aliasing={{0}: (7, {})} | custom-call | tf_op jit(solution)/shard_map/pallas_call | solution.py:410
  48.8 1.1 %collective-permute-done.7.rest_3_.rest_7_ = bf16[512,128]{1,0:T(8,128)(2,1)S(1)} collective-permute-done((bf16[512,128]{1,0:T(8,128)(2,1)}, bf16[512,128]{1,0:T(8,128)(2,1)S(1)}, u32[]{:S(2)}, u32[]{:S(2)}) %collective-permute-start.7) | collective-permute-done | bytes 131104 | tf_op jit(solution)/shard_map/ppermute | solution.py:600
  49.9 0.8 shard_map.83.early_ref
  50.8 3.4 %collective-permute-done.10.rest_3_ = bf16[512,128]{1,0:T(8,128)(2,1)} collective-permute-done((bf16[512,128]{1,0:T(8,128)(2,1)}, bf16[512,128]{1,0:T(8,128)(2,1)}, u32[]{:S(2)}, u32[]{:S(2)}) %collective-permute-start.10) | collective-permute-done | bytes 131104 | tf_op jit(solution)/shard_map/ppermute | solution.py:600
  54.2 1.9 %shard_map.84 = bf16[1024,128]{1,0:T(8,128)(2,1)S(1)} custom-call(s32[2]{0:T(128)S(1)} %pad_add_fusion.1.place_ref, bf16[1024,128]{1,0:T(8,128)(2,1)S(1)} %copy-done.2, f32[512,128]{1,0:T(8,128)S(1)} %shard_map.83.early_ref, bf16[512,128]{1,0:T(8,128)(2,1)S(1)} %get-tuple-element.33.rest_0_, bf16[512,128]{1,0:T(8,128)(2,1)S(1)} %collective-permute-done.8.rest_1_, ...), custom_call_target="tpu_custom_call" | custom-call | tf_op jit(solution)/shard_map/pallas_call | solution.py:410
  56.1 13.8 %all_to_all.10 = bf16[32,32,128]{2,1,0:T(8,128)(2,1)S(1)} all-to-all(bf16[32,32,128]{2,1,0:T(8,128)(2,1)S(1)} %bitcast.17), channel_id=1, replica_groups=mesh['gx'=8,'gy'=4] {'gx','gy'}, dimensions={0} | all-to-all | bytes 524288 | tf_op jit(solution)/shard_map/all_to_all | solution.py:446
  70.0 17.8 %all_to_all.11 = f32[32,32,128]{2,1,0:T(8,128)S(1)} all-to-all(f32[32,32,128]{2,1,0:T(8,128)S(1)} %broadcast_in_dim.26), channel_id=1, replica_groups=mesh['gx'=8,'gy'=4] {'gx','gy'}, dimensions={0} | all-to-all | bytes 1048576 | tf_op jit(solution)/shard_map/all_to_all | solution.py:450
  87.8 5.9 %shard_map.85 = (bf16[32,128]{1,0:T(8,128)(2,1)}, f32[512,128]{1,0:T(8,128)}) custom-call(s32[2]{0:T(128)S(1)} %pad_add_fusion.1.place_ref, f32[1024,128]{1,0:T(8,128)S(1)} %bitcast.16, bf16[512,128]{1,0:T(8,128)(2,1)S(1)} %get-tuple-element.33.rest_0_, bf16[512,128]{1,0:T(8,128)(2,1)S(1)} %collective-permute-done.8.rest_1_, ...), custom_call_target="tpu_custom_call" | custom-call | tf_op jit(solution)/shard_map/pallas_call | solution.py:410
  (23 shorter events, 0.3 us)
Async XLA Ops:
  0.6 5.1 %copy-start = (f32[32,2,64,128]{3,2,1,0:T(8,128)S(1)}, f32[32,2,64,128]{3,2,1,0:T(8,128)}, u32[]{:S(2)}) copy-start(f32[32,2,64,128]{3,2,1,0:T(8,128)} %state_ref.9) | copy-start | bytes 6291460
  0.6 5.1 %copy-start.1 = (f32[3,2,64,128]{3,2,1,0:T(8,128)S(1)}, f32[3,2,64,128]{3,2,1,0:T(8,128)}, u32[]{:S(2)}) copy-start(f32[3,2,64,128]{3,2,1,0:T(8,128)} %velocity_ref.5) | copy-start | bytes 589828
  0.7 5.7 %copy-start.3 = (f32[32]{0:T(128)S(1)}, f32[32]{0:T(128)}, u32[]{:S(2)}) copy-start(f32[32]{0:T(128)} %spread_ref.5) | copy-start | bytes 388
  0.7 5.7 %copy-start.4 = (f32[32]{0:T(128)S(1)}, f32[32]{0:T(128)}, u32[]{:S(2)}) copy-start(f32[32]{0:T(128)} %rate_ref.5) | copy-start | bytes 388
  2.6 4.2 %collective-permute-start = (bf16[18,16,128]{2,1,0:T(8,128)(2,1)}, bf16[18,16,128]{2,1,0:T(8,128)(2,1)S(1)}, u32[]{:S(2)}, u32[]{:S(2)}) collective-permute-start(bf16[18,16,128]{2,1,0:T(8,128)(2,1)} %get-tuple-element.21), channel_id=1, source_target_pairs={{0,1},{1,0},{2,3},{3,2},{4,5},{5,4},{6,7},{7,6},{8,9},{9,8},{10,11... | collective-permute-start | bytes 221192 | tf_op jit(solution)/shard_map/ppermute | solution.py:31
  3.1 5.4 %collective-permute-start.1 = (bf16[18,16,128]{2,1,0:T(8,128)(2,1)}, bf16[18,16,128]{2,1,0:T(8,128)(2,1)S(1)}, u32[]{:S(2)}, u32[]{:S(2)}) collective-permute-start(bf16[18,16,128]{2,1,0:T(8,128)(2,1)} %get-tuple-element.22), channel_id=1, source_target_pairs={{0,3},{1,2},{2,1},{3,0},{4,7},{5,6},{6,5},{7,4},{8,11},{9,10},{10,... | collective-permute-start | bytes 221192 | tf_op jit(solution)/shard_map/ppermute | solution.py:35
  8.6 8.2 %collective-permute-start.3 = (bf16[3,144,128]{2,1,0:T(8,128)(2,1)S(1)}, bf16[3,144,128]{2,1,0:T(8,128)(2,1)S(1)}, u32[]{:S(2)}, u32[]{:S(2)}) collective-permute-start(bf16[3,144,128]{2,1,0:T(8,128)(2,1)S(1)} %get-tuple-element.24.own_ref), channel_id=1, source_target_pairs={{0,28},{4,8},{8,4},{12,16},{16,12},{20,24},{24,20},{28,0},{1,29},{... | collective-permute-start | bytes 331784 | tf_op jit(solution)/shard_map/ppermute | solution.py:35
  13.1 6.0 %collective-permute-start.2 = (bf16[3,144,128]{2,1,0:T(8,128)(2,1)S(1)}, bf16[3,144,128]{2,1,0:T(8,128)(2,1)S(1)}, u32[]{:S(2)}, u32[]{:S(2)}) collective-permute-start(bf16[3,144,128]{2,1,0:T(8,128)(2,1)S(1)} %get-tuple-element.24.own_ref), channel_id=1, source_target_pairs={{0,4},{4,0},{8,12},{12,8},{16,20},{20,16},{24,28},{28,24},{1,5},{5... | collective-permute-start | bytes 331784 | tf_op jit(solution)/shard_map/ppermute | solution.py:31
  25.0 17.5 %collective-permute-start.4 = (bf16[512,128]{1,0:T(8,128)(2,1)}, bf16[512,128]{1,0:T(8,128)(2,1)S(1)}, u32[]{:S(2)}, u32[]{:S(2)}) collective-permute-start(bf16[512,128]{1,0:T(8,128)(2,1)} %get-tuple-element.29), channel_id=1, source_target_pairs={{0,16},{4,20},{8,24},{12,28},{16,0},{20,4},{24,8},{28,12},{1,17},{... | collective-permute-start | bytes 393224 | tf_op jit(solution)/shard_map/ppermute | solution.py:600
  25.8 16.7 %collective-permute-start.5 = (bf16[512,128]{1,0:T(8,128)(2,1)}, bf16[512,128]{1,0:T(8,128)(2,1)S(1)}, u32[]{:S(2)}, u32[]{:S(2)}) collective-permute-start(bf16[512,128]{1,0:T(8,128)(2,1)} %get-tuple-element.30), channel_id=1, source_target_pairs={{0,20},{4,16},{8,28},{12,24},{16,4},{20,0},{24,12},{28,8},{1,21},{... | collective-permute-start | bytes 393224 | tf_op jit(solution)/shard_map/ppermute | solution.py:600
  36.8 12.0 %collective-permute-start.6 = (bf16[512,128]{1,0:T(8,128)(2,1)}, bf16[512,128]{1,0:T(8,128)(2,1)S(1)}, u32[]{:S(2)}, u32[]{:S(2)}) collective-permute-start(bf16[512,128]{1,0:T(8,128)(2,1)} %get-tuple-element.31), channel_id=1, source_target_pairs={{0,24},{4,28},{8,16},{12,20},{16,8},{20,12},{24,0},{28,4},{1,25},{... | collective-permute-start | bytes 393224 | tf_op jit(solution)/shard_map/ppermute | solution.py:600
  39.9 10.1 %collective-permute-start.7 = (bf16[512,128]{1,0:T(8,128)(2,1)}, bf16[512,128]{1,0:T(8,128)(2,1)S(1)}, u32[]{:S(2)}, u32[]{:S(2)}) collective-permute-start(bf16[512,128]{1,0:T(8,128)(2,1)} %get-tuple-element.32), channel_id=1, source_target_pairs={{0,28},{4,24},{8,20},{12,16},{16,12},{20,8},{24,4},{28,0},{1,29},{... | collective-permute-start | bytes 393224 | tf_op jit(solution)/shard_map/ppermute | solution.py:600
  42.5 8.3 %collective-permute-start.8 = (bf16[512,128]{1,0:T(8,128)(2,1)}, bf16[512,128]{1,0:T(8,128)(2,1)S(1)}, u32[]{:S(2)}, u32[]{:S(2)}) collective-permute-start(bf16[512,128]{1,0:T(8,128)(2,1)} %get-tuple-element.34), channel_id=1, source_target_pairs={{0,4},{4,0},{8,12},{12,8},{16,20},{20,16},{24,28},{28,24},{1,5},{5... | collective-permute-start | bytes 393224 | tf_op jit(solution)/shard_map/ppermute | solution.py:600
  42.5 8.3 %collective-permute-start.9 = (bf16[512,128]{1,0:T(8,128)(2,1)}, bf16[512,128]{1,0:T(8,128)(2,1)}, u32[]{:S(2)}, u32[]{:S(2)}) collective-permute-start(bf16[512,128]{1,0:T(8,128)(2,1)} %get-tuple-element.35), channel_id=1, source_target_pairs={{0,8},{4,12},{8,0},{12,4},{16,24},{20,28},{24,16},{28,20},{1,9},{5... | collective-permute-start | bytes 393224 | tf_op jit(solution)/shard_map/ppermute | solution.py:600
  42.5 11.7 %collective-permute-start.10 = (bf16[512,128]{1,0:T(8,128)(2,1)}, bf16[512,128]{1,0:T(8,128)(2,1)}, u32[]{:S(2)}, u32[]{:S(2)}) collective-permute-start(bf16[512,128]{1,0:T(8,128)(2,1)} %get-tuple-element.36), channel_id=1, source_target_pairs={{0,12},{4,8},{8,4},{12,0},{16,28},{20,24},{24,20},{28,16},{1,13},{... | collective-permute-start | bytes 393224 | tf_op jit(solution)/shard_map/ppermute | solution.py:600
  46.1 3.9 %copy-start.2 = (bf16[1024,128]{1,0:T(8,128)(2,1)S(1)}, bf16[1024,128]{1,0:T(8,128)(2,1)}, u32[]{:S(2)}) copy-start(bf16[1024,128]{1,0:T(8,128)(2,1)} %basis_ref.3) | copy-start | bytes 786436
